TPU v7x, 32 devices: a whole 2x2x4 slice. The times are simulated.
32 devices in a mesh: ws: 4 (over z), seq: 8 (over y, x, core).
Axes of the slice: x: 2, y: 2, z: 4, core: 2. Of those that a mesh axis runs over, the one named last changes fastest.
Arguments:
- tokens: bfloat16 [4, 3072, 1536], P('ws', 'seq'), may hold values from -16 to 16
- w_same: bfloat16 [1536, 1536], replicated, may hold values from -0.15625 to 0.15625
- w_partner: bfloat16 [1536, 1536], replicated, may hold values from -0.15625 to 0.15625
- w_query: bfloat16 [1536, 1024], replicated, may hold values from -0.15625 to 0.15625
- w_key: bfloat16 [1536, 128], replicated, may hold values from -0.15625 to 0.15625
- w_value: bfloat16 [1536, 192], replicated, may hold values from -0.15625 to 0.15625
- w_out: bfloat16 [1536, 1536], replicated, may hold values from -0.15625 to 0.15625
Outputs:
- attended: bfloat16 [4, 3072, 1536], P('ws', 'seq')
All inputs are finite; a program needn't handle non-finite values.
Results may differ from a plain program's by a relative error of at most 0.012.
Values may be sent and summed in bfloat16 or wider, within the bound.
No kernel may reach another device: no remote copies, remote signals or barrier semaphores. Data moves between devices by JAX's collectives and lax.ppermute only.
A program may use at most 192 MiB of HBM per device.

v0:
```python
import jax
import jax.numpy as jnp
from jax import lax
from jax.sharding import PartitionSpec as P


def swapped(value, axis, bit):
    mask = 2**bit
    pairs = [(source, source ^ mask) for source in range(lax.axis_size(axis))]
    return lax.ppermute(value, axis, pairs)


def body(tokens, w_same, w_partner, w_query, w_key, w_value, w_out):
    count = lax.axis_size("seq")
    local = tokens[0]
    partner = swapped(tokens, "ws", 0)
    pieces = partner.reshape(count, partner.shape[1] // count, partner.shape[2])
    pieces = lax.all_to_all(pieces, "seq", split_axis=0, concat_axis=0, tiled=True)
    pieces = lax.all_to_all(jnp.flip(pieces, 0), "seq", split_axis=0, concat_axis=0, tiled=True)
    partner = pieces.reshape(tokens.shape)
    mirrored = jnp.flip(partner[0], 0)
    hidden = (
        jnp.dot(local, w_same, preferred_element_type=jnp.float32)
        + jnp.dot(mirrored, w_partner, preferred_element_type=jnp.float32)
    ).astype(jnp.bfloat16)
    query = jnp.dot(hidden, w_query, preferred_element_type=jnp.float32).astype(jnp.bfloat16)
    keys = jnp.dot(hidden, w_key, preferred_element_type=jnp.float32).astype(jnp.bfloat16)
    values = jnp.dot(hidden, w_value, preferred_element_type=jnp.float32).astype(jnp.bfloat16)
    rows = local.shape[0]
    key_width = w_key.shape[1]
    value_width = w_value.shape[1]
    head_count = w_query.shape[1] // key_width
    query_rows = query.reshape(rows * head_count, key_width)
    factor = key_width ** (-0.5)
    top = jnp.full((rows * head_count,), -jnp.inf, jnp.float32)
    total = jnp.zeros((rows * head_count,), jnp.float32)
    accum = jnp.zeros((rows * head_count, value_width), jnp.float32)
    scores = (
        lax.dot_general(
            query_rows,
            lax.all_gather(keys, "seq", axis=0, tiled=True),
            (((1,), (1,)), ((), ())),
            preferred_element_type=jnp.float32,
        )
        * factor
    )
    peak = jnp.max(scores, axis=1)
    decay = jnp.exp(top - peak)
    weights = jnp.exp(scores - peak[:, None])
    total = total * decay + jnp.sum(weights, axis=1)
    accum = accum * decay[:, None] + jnp.dot(
        weights.astype(jnp.bfloat16),
        lax.all_gather(values, "seq", axis=0, tiled=True),
        preferred_element_type=jnp.float32,
    )
    peak, total, accum = (peak, total, accum)
    mixed = (accum / total[:, None]).astype(jnp.bfloat16).reshape(rows, head_count * value_width)
    result = jnp.dot(mixed, w_out, preferred_element_type=jnp.float32).astype(jnp.bfloat16)
    return result[None]


def solution(mesh):
    placed = (P("ws", "seq", None), P(), P(), P(), P(), P(), P())
    return jax.shard_map(
        body, mesh=mesh, in_specs=placed, out_specs=P("ws", "seq", None), check_vma=False
    )
```

profile of v0, /device:TPU:0, one launch (start us, length us, event | category | flops | bytes accessed | tf_op | source)
XLA Modules:
  0.0 182.0 jit_solution(6034208135109014671)
XLA Ops:
  6.5 3.0 %collective-permute-start = (bf16[1,384,1536]{2,1,0:T(8,128)(2,1)}, bf16[1,384,1536]{2,1,0:T(8,128)(2,1)S(1)}, u32[]{:S(2)}, u32[]{:S(2)}) collective-permute-start(bf16[1,384,1536]{2,1,0:T(8,128)(2,1)} %param.7), channel_id=1, source_target_pairs={{0,8},{8,0},{16,24},{24,16},{1,9},{9,1},{17,25},{25,17},{2,10},{10... | collective-permute-start | bytes 3538952 | tf_op jit(solution)/shard_map/ppermute | solution.py:10
  9.6 26.2 %collective-permute-done = bf16[1,384,1536]{2,1,0:T(8,128)(2,1)S(1)} collective-permute-done((bf16[1,384,1536]{2,1,0:T(8,128)(2,1)}, bf16[1,384,1536]{2,1,0:T(8,128)(2,1)S(1)}, u32[]{:S(2)}, u32[]{:S(2)}) %collective-permute-start) | collective-permute-done | bytes 1179680 | tf_op jit(solution)/shard_map/ppermute | solution.py:10
  35.7 20.5 %all_to_all.10 = bf16[8,48,1536]{2,1,0:T(8,128)(2,1)} all-to-all(bf16[8,48,1536]{2,1,0:T(8,128)(2,1)S(1)} %bitcast.21), channel_id=1, replica_groups=mesh['ws'=4,'seq'=8] {'seq'}, dimensions={0} | all-to-all | bytes 2359296 | tf_op jit(solution)/shard_map/all_to_all | solution.py:18
  56.3 2.4 %rev.8 = bf16[8,48,1536]{2,1,0:T(8,128)(2,1)} reverse(bf16[8,48,1536]{2,1,0:T(8,128)(2,1)} %all_to_all.10), dimensions={0} | reverse | bytes 2359296 | tf_op jit(solution)/shard_map/jit(_flip)/rev | solution.py:19
  58.6 4.3 %all-to-all-start.1 = ((bf16[8,48,1536]{2,1,0:T(8,128)(2,1)}), bf16[8,48,1536]{2,1,0:T(8,128)(2,1)}, u32[]{:S(2)}, u32[]{:S(2)}) async-start(bf16[8,48,1536]{2,1,0:T(8,128)(2,1)} %rev.8), calls=%async_computation.1 | async-start | bytes 2359296 | tf_op jit(solution)/shard_map/all_to_all | solution.py:19
  62.9 0.0 all-gather.2.cloned.1.call-start
  63.0 6.1 %fusion.15 = f32[384,1536]{1,0:T(8,128)} fusion(bf16[1536,1536]{1,0:T(8,128)(2,1)} %param.8, bf16[1,384,1536]{2,1,0:T(8,128)(2,1)} %param.7), kind=kOutput, calls=%fused_computation.13 | convolution fusion | flops 1811939328 | bytes 8257536 | tf_op jit(solution)/shard_map/dot_general | solution.py:23
  69.1 10.7 %all-to-all-done.1 = bf16[8,48,1536]{2,1,0:T(8,128)(2,1)} async-done(((bf16[8,48,1536]{2,1,0:T(8,128)(2,1)}), bf16[8,48,1536]{2,1,0:T(8,128)(2,1)}, u32[]{:S(2)}, u32[]{:S(2)}) %all-to-all-start.1) | async-done | bytes 1179680 | tf_op jit(solution)/shard_map/all_to_all | solution.py:19
  79.7 17.4 %rev.9 = bf16[384,1536]{1,0:T(8,128)(2,1)} reverse(bf16[384,1536]{1,0:T(8,128)(2,1)} %bitcast.2), dimensions={0} | reverse | bytes 2359296 | tf_op jit(solution)/shard_map/jit(_flip)/rev | solution.py:21
  97.2 5.4 %fusion.13 = bf16[384,1536]{1,0:T(8,128)(2,1)S(1)} fusion(f32[384,1536]{1,0:T(8,128)} %fusion.15, bf16[384,1536]{1,0:T(8,128)(2,1)} %rev.9, bf16[1536,1536]{1,0:T(8,128)(2,1)} %param.9), kind=kOutput, calls=%fused_computation.10 | convolution fusion | flops 1813118976 | bytes 9437184 | tf_op jit(solution)/shard_map/dot_general | solution.py:24
  102.6 1.0 copy-done.2
  103.6 2.3 %convolution_convert_fusion.1 = bf16[384,1024]{1,0:T(8,128)(2,1)} fusion(bf16[384,1536]{1,0:T(8,128)(2,1)S(1)} %fusion.13, bf16[1536,1024]{1,0:T(8,128)(2,1)S(1)} %copy-done), kind=kOutput, calls=%fused_computation.12 | convolution fusion | flops 1208352768 | bytes 5111808 | tf_op jit(solution)/shard_map/dot_general | solution.py:26
  106.0 1.5 reshape.21
  107.5 1.8 convolution_convert_fusion.3
  109.3 9.6 %all_gather.6 = bf16[3072,128]{1,0:T(8,128)(2,1)S(1)} all-gather(bf16[384,128]{1,0:T(8,128)(2,1)S(1)} %convolution_convert_fusion.3), channel_id=1, replica_groups=mesh['ws'=4,'seq'=8] {'seq'}, dimensions={0}, use_global_device_ids=true | all-gather | bytes 884736 | tf_op jit(solution)/shard_map/all_gather | solution.py:41
  119.0 1.2 convolution_convert_fusion.2
  120.1 0.0 all-gather.2.cloned.1.call-update
  120.1 15.0 %multiply_reduce_fusion = (f32[3072]{0:T(1024)S(1)}, f32[3072,3072]{0,1:T(8,128)}) fusion(bf16[3072,128]{1,0:T(8,128)(2,1)S(1)} %reshape.21, bf16[3072,128]{1,0:T(8,128)(2,1)S(1)} %all_gather.6), kind=kOutput, calls=%fused_computation.1 | convolution fusion | flops 2434790400 | bytes 39333888 | tf_op jit(solution)/shard_map/dot_general | solution.py:39
  135.1 15.3 %fusion = f32[3072]{0:T(1024)S(1)} fusion(f32[3072,3072]{0,1:T(8,128)} %get-tuple-element.8, f32[3072]{0:T(1024)S(1)} %get-tuple-element.7), kind=kLoop, calls=%fused_computation.2 | loop fusion | flops 28308480 | bytes 37773312 | tf_op jit(solution)/shard_map/reduce_sum | solution.py:50
  150.5 0.0 all-gather.2.cloned.1.call-done
  150.5 15.9 %fusion.10 = bf16[3072,192]{0,1:T(8,128)(2,1)S(1)} fusion(bf16[3072,192]{1,0:T(8,128)(2,1)} %all-gather.2.cloned.1.call-done, f32[3072,3072]{0,1:T(8,128)} %get-tuple-element.8, f32[3072]{0:T(1024)S(1)} %get-tuple-element.7, f32[3072]{0:T(1024)S(1)} %get-tuple-element.6, f32[3072]{0:T(1024)S(1)} %get-tuple-element.5), kind=kOutput, calls=%fused_computation.7 | convolution fusion | flops 3653959680 | bytes 40144896 | tf_op jit(solution)/shard_map/dot_general | solution.py:51
  166.4 0.7 copy.8
  167.1 2.2 %reshape.22 = bf16[384,1536]{1,0:T(8,128)(2,1)} reshape(bf16[3072,192]{1,0:T(8,128)(2,1)S(1)} %copy.8) | data formatting | bytes 2359296 | tf_op jit(solution)/shard_map/reshape | solution.py:57
  169.3 5.8 %fusion.14 = bf16[1,384,1536]{2,1,0:T(8,128)(2,1)} fusion(bf16[384,1536]{1,0:T(8,128)(2,1)} %reshape.22, bf16[1536,1536]{1,0:T(8,128)(2,1)} %param.13), kind=kOutput, calls=%fused_computation.11 | convolution fusion | flops 1812529152 | bytes 7077888 | tf_op jit(solution)/shard_map/dot_general | solution.py:58
  (12 shorter events, 0.0 us)
Async XLA Ops:
  6.5 97.1 %copy-start = (bf16[1536,1024]{1,0:T(8,128)(2,1)S(1)}, bf16[1536,1024]{1,0:T(8,128)(2,1)}, u32[]{:S(2)}) copy-start(bf16[1536,1024]{1,0:T(8,128)(2,1)} %param.10) | copy-start | bytes 9437188
  6.5 29.2 %collective-permute-start = (bf16[1,384,1536]{2,1,0:T(8,128)(2,1)}, bf16[1,384,1536]{2,1,0:T(8,128)(2,1)S(1)}, u32[]{:S(2)}, u32[]{:S(2)}) collective-permute-start(bf16[1,384,1536]{2,1,0:T(8,128)(2,1)} %param.7), channel_id=1, source_target_pairs={{0,8},{8,0},{16,24},{24,16},{1,9},{9,1},{17,25},{25,17},{2,10},{10... | collective-permute-start | bytes 3538952 | tf_op jit(solution)/shard_map/ppermute | solution.py:10
  58.6 21.1 %all-to-all-start.1 = ((bf16[8,48,1536]{2,1,0:T(8,128)(2,1)}), bf16[8,48,1536]{2,1,0:T(8,128)(2,1)}, u32[]{:S(2)}, u32[]{:S(2)}) async-start(bf16[8,48,1536]{2,1,0:T(8,128)(2,1)} %rev.8), calls=%async_computation.1 | async-start | bytes 2359296 | tf_op jit(solution)/shard_map/all_to_all | solution.py:19
  62.9 87.6 %all-gather.2.cloned.1.call-start = ((), (), s32[]{:S(2)}) async-start(), calls=%async_computation.2 | async-start | bytes 1769472 | tf_op jit(solution)/shard_map/all_gather | solution.py:53
  102.6 1.0 copy-start.2
  103.6 3.9 %copy-start.4 = (bf16[1536,128]{1,0:T(8,128)(2,1)S(1)}, bf16[1536,128]{1,0:T(8,128)(2,1)}, u32[]{:S(2)}) copy-start(bf16[1536,128]{1,0:T(8,128)(2,1)} %param.11) | copy-start | bytes 1179652
  106.0 13.0 %copy-start.3 = (bf16[384,1536]{1,0:T(8,128)(2,1)S(1)}, bf16[384,1536]{1,0:T(8,128)(2,1)}, u32[]{:S(2)}) copy-start(bf16[384,1536]{1,0:T(8,128)(2,1)} %copy-done.2) | copy-start | bytes 3538948
  107.5 11.4 %copy-start.5 = (bf16[1536,192]{0,1:T(8,128)(2,1)S(1)}, bf16[1536,192]{0,1:T(8,128)(2,1)}, u32[]{:S(2)}) copy-start(bf16[1536,192]{0,1:T(8,128)(2,1)} %param.12) | copy-start | bytes 1769476
  169.3 5.8 %copy-start.1 = (bf16[1536,1024]{1,0:T(8,128)(2,1)S(1)}, bf16[1536,1024]{1,0:T(8,128)(2,1)}, u32[]{:S(2)}) copy-start(bf16[1536,1024]{1,0:T(8,128)(2,1)} %param.10) | copy-start | bytes 9437188
Sparse Core Ops, SparseCore 0:
  120.3 26.0 all-gather.1
where the time goes:
time: 184 us; the launch traced here: 182 us
  matrix products  53.6 us (29%)
  waiting for transfers between devices  36.9 us (20%)
  blocking collectives  30.2 us (16%)
  local copies, waits for them, and re-layouts  25.3 us (14%)
  other arithmetic  15.4 us (8%)
  between operations  13.5 us (7%)
  starting transfers between devices  7.33 us (4%)
    ppermute x1, waiting for transfers between devices, swapped(): return lax.ppermute(value, axis, pairs)  26.2 us
    all_to_all x1, blocking collectives, body(): lax.all_to_all(pieces, 'seq', split_axis=0, concat_axis=0, tiled=True)  20.5 us
    rev x1, local copies, waits for them, and re-layouts, body(): mirrored = jnp.flip(partner[0], 0)  17.4 us
    dot_general x1, matrix products, body(): jnp.dot(weights.astype(jnp.bfloat16), lax.all_gather(values, 'seq', axis=...  15.9 us
    reduce_sum x1, other arithmetic, body(): total = total * decay + jnp.sum(weights, axis=1)  15.3 us
    dot_general x1, matrix products, body(): lax.dot_general(query_rows, lax.all_gather(keys, 'seq', axis=0, tiled=Tru...  15 us
    all_to_all x1, waiting for transfers between devices, body(): lax.all_to_all(jnp.flip(pieces, 0), 'seq', split_axis=0, concat_axis=0, t...  10.7 us
    all_gather x1, blocking collectives, body(): lax.all_gather(keys, 'seq', axis=0, tiled=True)  9.62 us
  transfers between devices with their start and end apart: 3, of which 2 were waited for; matrix products, arithmetic and copies ran while one was open for 20% of the time, Pallas kernels for 0%

commit v1 on v0

v1 whole, which is shorter than its diff:
```python
import functools
import math

import jax
import jax.numpy as jnp
from jax import lax
from jax.experimental import pallas as pl
from jax.experimental.pallas import tpu as pltpu
from jax.sharding import PartitionSpec as P

F32 = jnp.float32
BF16 = jnp.bfloat16
CONTRACT_LAST = (((1,), (1,)), ((), ()))
CHUNKS = (1,)
VMEM_LIMIT = 40 << 20


def whole(memory_space=pltpu.VMEM):
    return pl.BlockSpec(memory_space=memory_space)


def same_kernel(tokens, w_same, out):
    out[...] = jnp.dot(tokens[...], w_same[...], preferred_element_type=F32)


def same_product(tokens, w_same):
    rows, width = tokens.shape
    features = w_same.shape[1]
    tile = 512 if features % 512 == 0 else features
    return pl.pallas_call(
        same_kernel,
        grid=(features // tile,),
        in_specs=[
            pl.BlockSpec((rows, width), lambda i: (0, 0)),
            pl.BlockSpec((width, tile), lambda i: (0, i)),
        ],
        out_specs=pl.BlockSpec((rows, tile), lambda i: (0, i)),
        out_shape=jax.ShapeDtypeStruct((rows, features), F32),
        compiler_params=pltpu.CompilerParams(vmem_limit_bytes=16 << 20),
        cost_estimate=pl.CostEstimate(
            flops=2 * rows * width * features,
            bytes_accessed=2 * width * features + 6 * rows * features,
            transcendentals=0,
        ),
        name="same_product",
    )(tokens, w_same)


def reversed_rows(block):
    rows = block.shape[0]
    row = lax.broadcasted_iota(jnp.int32, (rows, rows), 0)
    column = lax.broadcasted_iota(jnp.int32, (rows, rows), 1)
    swap = (row + column == rows - 1).astype(F32).astype(BF16)
    return jnp.dot(swap, block, preferred_element_type=F32).astype(BF16)


def pack(pair, value, rows, lanes):
    width = value.shape[1]
    at = rows
    for lane in range(0, width - width % lanes, lanes):
        pair[at : at + rows, :] = value[:, lane : lane + lanes]
        at += rows
    rest = width % lanes
    if rest:
        share = rows * rest // lanes
        pair[at : at + share, :] = jnp.concatenate(
            [value[i * share : (i + 1) * share, width - rest :] for i in range(lanes // rest)], 1
        )


def unpack(pair, at, rows, lanes, width):
    key = pair[at : at + rows, :]
    at += rows
    parts = []
    for _ in range(width // lanes):
        parts.append(pair[at : at + rows, :])
        at += rows
    rest = width % lanes
    if rest:
        share = rows * rest // lanes
        tail = pair[at : at + share, :]
        parts.append(
            jnp.concatenate([tail[:, i * rest : (i + 1) * rest] for i in range(lanes // rest)], 0)
        )
    return key, jnp.concatenate(parts, 1)


def project_kernel(first, arrived, same, w_partner, w_query, w_key, w_value, query, pair):
    rows = arrived.shape[0]
    keys = w_key.shape[1]
    mirrored = reversed_rows(arrived[...])
    hidden = (
        same[first : first + rows, :] + jnp.dot(mirrored, w_partner[...], preferred_element_type=F32)
    ).astype(BF16)
    pair[:rows, :] = jnp.dot(hidden, w_key[...], preferred_element_type=F32).astype(BF16)
    value = lax.dot_general(
        hidden, w_value[...], CONTRACT_LAST, preferred_element_type=F32
    ).astype(BF16)
    pack(pair, value, rows, keys)
    query[...] = jnp.dot(hidden, w_query[...], preferred_element_type=F32).astype(BF16)


def project(first, arrived, same, w_partner, w_query, w_key, w_value):
    rows, width = arrived.shape
    queries, keys, values = w_query.shape[1], w_key.shape[1], w_value.shape[0]
    total = queries + keys + values
    return pl.pallas_call(
        functools.partial(project_kernel, first),
        in_specs=[whole()] * 6,
        out_specs=[whole()] * 2,
        out_shape=[
            jax.ShapeDtypeStruct((rows, queries), BF16),
            jax.ShapeDtypeStruct((rows * (keys + values) // keys, keys), BF16),
        ],
        compiler_params=pltpu.CompilerParams(vmem_limit_bytes=VMEM_LIMIT),
        cost_estimate=pl.CostEstimate(
            flops=2 * rows * width * (width + total),
            bytes_accessed=2 * width * (width + total),
            transcendentals=0,
        ),
        name="project",
    )(arrived, same, w_partner, w_query, w_key, w_value)


def attend_kernel(shape, *refs):
    n_query, blocks, has_state, last, heads, keys, values = shape
    refs = list(refs)
    queries = [refs.pop(0) for _ in range(n_query)]
    pairs = [refs.pop(0) for _ in blocks]
    if has_state:
        old_sum, old_peak = refs.pop(0), refs.pop(0)
    if last:
        w_out, out = refs.pop(0), refs.pop(0)
    else:
        new_sum, new_peak = refs.pop(0), refs.pop(0)
    held, extended, scores = refs.pop(0), refs.pop(0), refs.pop(0)
    if last:
        mixed = refs.pop(0)
    padded = extended.shape[1]
    scale = keys**-0.5 * math.log2(math.e)
    start = 0
    for pair, block in zip(pairs, blocks):
        packed = block * (keys + values) // keys
        for at in range(0, pair.shape[0], packed):
            key, value = unpack(pair, at, block, keys, values)
            held[start : start + block, :] = key
            extended[start : start + block, :values] = value
            start += block
    extended[:, values:] = jnp.ones((start, padded - values), BF16)
    step = 512 if start % 512 == 0 else 256

    def score(head, slot):
        column = pl.ds(pl.multiple_of(head * keys, keys), keys)
        parts = [query[:, column] for query in queries]
        query = jnp.concatenate(parts, 0) if len(parts) > 1 else parts[0]
        peak = None
        for at in range(0, start, step):
            block = lax.dot_general(
                query, held[at : at + step, :], CONTRACT_LAST, preferred_element_type=F32
            )
            scores[slot, :, at : at + step] = block
            for lane in range(0, step, 128):
                part = block[:, lane : lane + 128]
                peak = part if peak is None else jnp.maximum(peak, part)
        peak = jnp.max(peak, axis=1, keepdims=True)
        if has_state:
            peak = jnp.maximum(peak, old_peak[head][:, :1])
        return peak

    def mix(head, slot, peak):
        total = None
        for at in range(0, start, step):
            weights = jnp.exp2((scores[slot, :, at : at + step] - peak) * scale).astype(BF16)
            part = jnp.dot(weights, extended[at : at + step, :], preferred_element_type=F32)
            total = part if total is None else total + part
        if has_state:
            decay = jnp.exp2((old_peak[head][:, :1] - peak) * scale)
            total = total + old_sum[head] * decay
        if last:
            return (total[:, :values] / total[:, values : values + 1]).astype(BF16)
        new_sum[head] = total
        new_peak[head] = jnp.broadcast_to(peak, new_peak.shape[1:])
        return None

    def two_heads(index, peak):
        head = 2 * index
        other = score(head + 1, 1)
        left = mix(head, 0, peak)
        following = score(jnp.minimum(head + 2, heads - 1), 0)
        right = mix(head + 1, 1, other)
        if last:
            column = pl.ds(pl.multiple_of(index * 2 * values, 2 * values), 2 * values)
            mixed[:, column] = jnp.concatenate([left, right], 1)
        return following

    lax.fori_loop(0, heads // 2, two_heads, score(0, 0))
    if last:
        out[...] = jnp.dot(mixed[...], w_out[...], preferred_element_type=F32).astype(BF16)


def attend(queries, pairs, blocks, state, w_out, keys, values):
    rows = sum(query.shape[0] for query in queries)
    heads = queries[0].shape[1] // keys
    seen = sum(pair.shape[0] for pair in pairs) * keys // (keys + values)
    padded = (values // 128 + 1) * 128
    last = w_out is not None
    shape = (len(queries), blocks, state is not None, last, heads, keys, values)
    arguments = list(queries) + list(pairs) + (list(state) if state is not None else [])
    scratch = [pltpu.VMEM((seen, keys), BF16), pltpu.VMEM((seen, padded), BF16), pltpu.VMEM((2, rows, seen), F32)]
    if last:
        arguments.append(w_out)
        out_shape = jax.ShapeDtypeStruct((rows, w_out.shape[1]), BF16)
        out_specs = whole()
        scratch.append(pltpu.VMEM((rows, heads * values), BF16))
    else:
        out_shape = [
            jax.ShapeDtypeStruct((heads, rows, padded), F32),
            jax.ShapeDtypeStruct((heads, rows, 128), F32),
        ]
        out_specs = [whole()] * 2
    flops = 2 * rows * heads * seen * (keys + values)
    if last:
        flops += 2 * rows * heads * values * w_out.shape[1]
    return pl.pallas_call(
        functools.partial(attend_kernel, shape),
        in_specs=[whole()] * len(arguments),
        out_specs=out_specs,
        out_shape=out_shape,
        scratch_shapes=scratch,
        compiler_params=pltpu.CompilerParams(vmem_limit_bytes=VMEM_LIMIT),
        cost_estimate=pl.CostEstimate(
            flops=flops, bytes_accessed=2 * seen * (keys + values), transcendentals=rows * heads * seen
        ),
        name="attend",
    )(*arguments)


def gathered(pair):
    count = lax.axis_size("seq")
    parts = [pair] + [
        lax.ppermute(pair, "seq", [(s, s ^ k) for s in range(count)]) for k in range(2, count, 2)
    ]
    mine = jnp.concatenate(parts, 0)
    other = lax.ppermute(mine, "seq", [(s, s ^ 1) for s in range(count)])
    return [mine, other]


def body(tokens, w_same, w_partner, w_query, w_key, w_value, w_out):
    lanes, count = lax.axis_size("ws"), lax.axis_size("seq")
    local = tokens[0]
    rows = local.shape[0]
    keys, values = w_key.shape[1], w_value.shape[1]
    opposite = [
        (w * count + s, (w ^ 1) * count + count - 1 - s) for w in range(lanes) for s in range(count)
    ]
    sizes = [rows * part // sum(CHUNKS) for part in CHUNKS]
    starts = [sum(sizes[:i]) for i in range(len(sizes))]
    arrived = [
        lax.ppermute(local[rows - a - n : rows - a], ("ws", "seq"), opposite) if n < rows
        else lax.ppermute(local, ("ws", "seq"), opposite)
        for a, n in zip(starts, sizes)
    ]
    same = same_product(local, w_same)
    queries, pairs = [], []
    for a, block in zip(starts, arrived):
        query, pair = project(a, block, same, w_partner, w_query, w_key, w_value.T)
        queries.append(query)
        pairs.append(gathered(pair))
    state = None
    for index, (pair, size) in enumerate(zip(pairs, sizes)):
        final = w_out if index == len(pairs) - 1 else None
        state = attend(queries, pair, [size] * len(pair), state, final, keys, values)
    result = state
    return result[None]


def solution(mesh):
    placed = (P("ws", "seq", None), P(), P(), P(), P(), P(), P())
    return jax.shard_map(
        body, mesh=mesh, in_specs=placed, out_specs=P("ws", "seq", None), check_vma=False
    )
```

time: 184 us -> 73.5 us (0.40)
  matrix products: 53.6 us -> 0 us
  blocking collectives: 30.2 us -> 0 us
  Pallas kernels: 0 us -> 23 us
  local copies, waits for them, and re-layouts: 25.3 us -> 7.68 us
  other arithmetic: 15.4 us -> 0.01 us
  between operations: 13.5 us -> 0.06 us
  waiting for transfers between devices: 36.9 us -> 34.2 us
    dot_general x8 -> x0, matrix products: 53.6 us -> none  [the longest x1 15.9 us: body(): jnp.dot(weights.astype(jnp.bfloat16), lax.all_gather(values, 'seq', axis=...]
    pallas_call x0 -> x3, Pallas kernels: none -> 23 us  [the longest x1 15.8 us: attend(): pl.pallas_call(functools.partial(attend_kernel, shape), in_specs=[whole()...]
    all_to_all x1 -> x0, blocking collectives: 20.5 us -> none  [body(): lax.all_to_all(pieces, 'seq', split_axis=0, concat_axis=0, tiled=True)]
    rev x2 -> x0, local copies, waits for them, and re-layouts: 19.8 us -> none  [the longest x1 17.4 us: body(): mirrored = jnp.flip(partner[0], 0)]
    reduce_sum x1 -> x0, other arithmetic: 15.3 us -> none  [body(): total = total * decay + jnp.sum(weights, axis=1)]
    all_to_all x1 -> x0, waiting for transfers between devices: 10.7 us -> none  [body(): lax.all_to_all(jnp.flip(pieces, 0), 'seq', split_axis=0, concat_axis=0, t...]
    all_gather x1 -> x0, blocking collectives: 9.62 us -> none  [body(): lax.all_gather(keys, 'seq', axis=0, tiled=True)]
    ppermute x1 -> x5, waiting for transfers between devices: 26.2 us -> 34.2 us  [the longest x1 20.2 us: body(): lax.ppermute(local, ('ws', 'seq'), opposite)]
  transfers between devices with their start and end apart: 3 -> 5, of which waited for: 2 -> 4; matrix products, arithmetic and copies ran while one was open for 20% -> 0% of each run, Pallas kernels for 0% -> 4%
where the time goes in v1:
time: 73.5 us; the launch traced here: 73.2 us
  waiting for transfers between devices  34.2 us (47%)
  Pallas kernels  23 us (31%)
  starting transfers between devices  8.21 us (11%)
  local copies, waits for them, and re-layouts  7.68 us (10%)
    ppermute x1, waiting for transfers between devices, body(): lax.ppermute(local, ('ws', 'seq'), opposite)  20.2 us
    pallas_call x1, Pallas kernels, attend(): pl.pallas_call(functools.partial(attend_kernel, shape), in_specs=[whole()...  15.8 us
    ppermute x3, waiting for transfers between devices, gathered(): lax.ppermute(pair, 'seq', [(s, s ^ k) for s in range(count)])  11.4 us
    unnamed x19, local copies, waits for them, and re-layouts  7.65 us
    pallas_call x1, Pallas kernels, project(): pl.pallas_call(functools.partial(project_kernel, first), in_specs=[whole(...  4.41 us
    ppermute x1, starting transfers between devices, body(): lax.ppermute(local, ('ws', 'seq'), opposite)  4.35 us
    ppermute x3, starting transfers between devices, gathered(): lax.ppermute(pair, 'seq', [(s, s ^ k) for s in range(count)])  3.8 us
    pallas_call x1, Pallas kernels, same_product(): pl.pallas_call(same_kernel, grid=(features // tile,), in_specs=[pl.BlockS...  2.79 us
  transfers between devices with their start and end apart: 5, of which 4 were waited for; matrix products, arithmetic and copies ran while one was open for 0% of the time, Pallas kernels for 4%

profile of v1, /device:TPU:0, one launch (start us, length us, event | category | flops | bytes accessed | tf_op | source)
XLA Modules:
  0.0 73.2 jit_solution(11963049083965177090)
XLA Ops:
  0.0 4.3 %collective-permute-start = (bf16[384,1536]{1,0:T(8,128)(2,1)}, bf16[384,1536]{1,0:T(8,128)(2,1)S(1)}, u32[]{:S(2)}, u32[]{:S(2)}) collective-permute-start(bf16[384,1536]{1,0:T(8,128)(2,1)} %bitcast.3), channel_id=1, source_target_pairs={{0,15},{1,14},{2,13},{3,12},{4,11},{5,10},{6,9},{7,8},{8,7},{9,6},... | collective-permute-start | bytes 3538952 | tf_op jit(solution)/shard_map/ppermute | solution.py:260
  4.3 0.0 copy-start
  4.3 2.3 %copy-done = bf16[1536,1536]{1,0:T(8,128)(2,1)S(1)} copy-done((bf16[1536,1536]{1,0:T(8,128)(2,1)S(1)}, bf16[1536,1536]{1,0:T(8,128)(2,1)}, u32[]{:S(2)}) %copy-start) | copy-done | bytes 4718616
  6.7 0.0 copy-start.1
  6.7 1.3 %copy-done.1 = bf16[1,384,1536]{2,1,0:T(8,128)(2,1)S(1)} copy-done((bf16[1,384,1536]{2,1,0:T(8,128)(2,1)S(1)}, bf16[1,384,1536]{2,1,0:T(8,128)(2,1)}, u32[]{:S(2)}) %copy-start.1) | copy-done | bytes 1179672
  8.0 0.0 copy-start.2
  8.0 2.8 %same_product.1.same = f32[384,1536]{1,0:T(8,128)S(1)} custom-call(bf16[384,1536]{1,0:T(8,128)(2,1)S(1)} %bitcast.4, bf16[1536,1536]{1,0:T(8,128)(2,1)S(1)} %copy-done), custom_call_target="tpu_custom_call" | custom-call | flops 1811939328 | bytes 8257536 | tf_op jit(solution)/shard_map/same_product/pallas_call | solution.py:30
  10.8 20.2 %collective-permute-done.arrived = bf16[384,1536]{1,0:T(8,128)(2,1)S(1)} collective-permute-done((bf16[384,1536]{1,0:T(8,128)(2,1)}, bf16[384,1536]{1,0:T(8,128)(2,1)S(1)}, u32[]{:S(2)}, u32[]{:S(2)}) %collective-permute-start) | collective-permute-done | bytes 1179680 | tf_op jit(solution)/shard_map/ppermute | solution.py:260
  31.0 0.0 copy-done.2
  31.0 1.9 %copy-done.3 = bf16[1536,1024]{1,0:T(8,128)(2,1)S(1)} copy-done((bf16[1536,1024]{1,0:T(8,128)(2,1)S(1)}, bf16[1536,1024]{1,0:T(8,128)(2,1)}, u32[]{:S(2)}) %copy-start.3) | copy-done | bytes 3145752
  32.9 1.1 %copy-done.4 = bf16[1536,192]{0,1:T(8,128)(2,1)S(1)} copy-done((bf16[1536,192]{0,1:T(8,128)(2,1)S(1)}, bf16[1536,192]{0,1:T(8,128)(2,1)}, u32[]{:S(2)}) %copy-start.4) | copy-done | bytes 589848
  34.0 1.0 %copy-done.5 = bf16[1536,128]{1,0:T(8,128)(2,1)S(1)} copy-done((bf16[1536,128]{1,0:T(8,128)(2,1)S(1)}, bf16[1536,128]{1,0:T(8,128)(2,1)}, u32[]{:S(2)}) %copy-start.5) | copy-done | bytes 393240
  35.0 4.4 %project.1 = (bf16[384,1024]{1,0:T(8,128)(2,1)S(1)}, bf16[960,128]{1,0:T(8,128)(2,1)S(1)}) custom-call(bf16[384,1536]{1,0:T(8,128)(2,1)S(1)} %collective-permute-done.arrived, f32[384,1536]{1,0:T(8,128)S(1)} %same_product.1.same, bf16[1536,1536]{1,0:T(8,128)(2,1)S(1)} %copy-done.2, bf16[1536,1024]{1,0:T(8,128)(2,1)S(1)} %copy-done.3, ...), custom_call_target="tpu_custom_call" | custom-call | flops 3397386240 | bytes 8847360 | tf_op jit(solution)/shard_map/project/pallas_call | solution.py:107
  39.4 2.3 %collective-permute-start.1 = (bf16[960,128]{1,0:T(8,128)(2,1)S(1)}, bf16[960,128]{1,0:T(8,128)(2,1)S(1)}, u32[]{:S(2)}, u32[]{:S(2)}) collective-permute-start(bf16[960,128]{1,0:T(8,128)(2,1)S(1)} %get-tuple-element.8), channel_id=1, source_target_pairs={{0,2},{1,3},{2,0},{3,1},{4,6},{5,7},{6,4},{7,5},{8,10},{9,11},{10,... | collective-permute-start | bytes 737288 | tf_op jit(solution)/shard_map/ppermute | solution.py:241
  41.6 1.5 %collective-permute-start.2 = (bf16[960,128]{1,0:T(8,128)(2,1)S(1)}, bf16[960,128]{1,0:T(8,128)(2,1)S(1)}, u32[]{:S(2)}, u32[]{:S(2)}) collective-permute-start(bf16[960,128]{1,0:T(8,128)(2,1)S(1)} %get-tuple-element.8), channel_id=1, source_target_pairs={{0,4},{1,5},{2,6},{3,7},{4,0},{5,1},{6,2},{7,3},{8,12},{9,13},{10,... | collective-permute-start | bytes 737288 | tf_op jit(solution)/shard_map/ppermute | solution.py:241
  43.2 0.0 collective-permute-start.3
  43.2 5.2 %collective-permute-done.1 = bf16[960,128]{1,0:T(8,128)(2,1)S(1)} collective-permute-done((bf16[960,128]{1,0:T(8,128)(2,1)S(1)}, bf16[960,128]{1,0:T(8,128)(2,1)S(1)}, u32[]{:S(2)}, u32[]{:S(2)}) %collective-permute-start.1) | collective-permute-done | bytes 245792 | tf_op jit(solution)/shard_map/ppermute | solution.py:241
  48.4 6.2 %collective-permute-done.2 = bf16[960,128]{1,0:T(8,128)(2,1)S(1)} collective-permute-done((bf16[960,128]{1,0:T(8,128)(2,1)S(1)}, bf16[960,128]{1,0:T(8,128)(2,1)S(1)}, u32[]{:S(2)}, u32[]{:S(2)}) %collective-permute-start.2) | collective-permute-done | bytes 245792 | tf_op jit(solution)/shard_map/ppermute | solution.py:241
  54.6 0.0 collective-permute-done.3
  54.7 0.1 collective-permute-start.4
  54.8 2.6 %collective-permute-done.4.refs_2_ = bf16[3840,128]{1,0:T(8,128)(2,1)S(1)} collective-permute-done((bf16[3840,128]{1,0:T(8,128)(2,1)S(1)}, bf16[3840,128]{1,0:T(8,128)(2,1)S(1)}, u32[]{:S(2)}, u32[]{:S(2)}) %collective-permute-start.4) | collective-permute-done | bytes 983072 | tf_op jit(solution)/shard_map/ppermute | solution.py:244
  57.3 0.0 slice-done
  57.3 0.0 slice-done.1
  57.3 15.8 %attend.1 = bf16[384,1536]{1,0:T(8,128)(2,1)} custom-call(bf16[384,1024]{1,0:T(8,128)(2,1)S(1)} %get-tuple-element.7.refs_0_, bf16[3840,128]{1,0:T(8,128)(2,1)S(1)} %constant_dynamic-update-slice_fusion.refs_1_, bf16[3840,128]{1,0:T(8,128)(2,1)S(1)} %collective-permute-done.4.refs_2_, bf16[1536,1536]{1,0:T(8,128)(2,1)S(1)} %bitcast.6), custom_call_target="tpu_custom_call" | custom-call | flops 7851737088 | bytes 1966080 | tf_op jit(solution)/shard_map/attend/pallas_call | solution.py:224
  (10 shorter events, 0.1 us)
Async XLA Ops:
  0.0 31.0 %collective-permute-start = (bf16[384,1536]{1,0:T(8,128)(2,1)}, bf16[384,1536]{1,0:T(8,128)(2,1)S(1)}, u32[]{:S(2)}, u32[]{:S(2)}) collective-permute-start(bf16[384,1536]{1,0:T(8,128)(2,1)} %bitcast.3), channel_id=1, source_target_pairs={{0,15},{1,14},{2,13},{3,12},{4,11},{5,10},{6,9},{7,8},{8,7},{9,6},... | collective-permute-start | bytes 3538952 | tf_op jit(solution)/shard_map/ppermute | solution.py:260
  4.3 2.3 %copy-start = (bf16[1536,1536]{1,0:T(8,128)(2,1)S(1)}, bf16[1536,1536]{1,0:T(8,128)(2,1)}, u32[]{:S(2)}) copy-start(bf16[1536,1536]{1,0:T(8,128)(2,1)} %w_same.1) | copy-start | bytes 14155780
  6.7 1.3 %copy-start.1 = (bf16[1,384,1536]{2,1,0:T(8,128)(2,1)S(1)}, bf16[1,384,1536]{2,1,0:T(8,128)(2,1)}, u32[]{:S(2)}) copy-start(bf16[1,384,1536]{2,1,0:T(8,128)(2,1)} %param.7) | copy-start | bytes 3538948
  8.0 23.1 %copy-start.2 = (bf16[1536,1536]{1,0:T(8,128)(2,1)S(1)}, bf16[1536,1536]{1,0:T(8,128)(2,1)}, u32[]{:S(2)}) copy-start(bf16[1536,1536]{1,0:T(8,128)(2,1)} %w_partner.1) | copy-start | bytes 14155780
  8.0 49.4 %slice-start = ((s8[4718592]{0:T(1024)(128)(4,1)}), s8[4194304]{0:T(1024)(128)(4,1)S(1)}, s32[]{:S(2)}) async-start(s8[4718592]{0:T(1024)(128)(4,1)} %bitcast.5), calls=%async_computation | async-start | bytes 8388608
  31.0 1.9 %copy-start.3 = (bf16[1536,1024]{1,0:T(8,128)(2,1)S(1)}, bf16[1536,1024]{1,0:T(8,128)(2,1)}, u32[]{:S(2)}) copy-start(bf16[1536,1024]{1,0:T(8,128)(2,1)} %w_query.1) | copy-start | bytes 9437188
  32.9 1.1 %copy-start.4 = (bf16[1536,192]{0,1:T(8,128)(2,1)S(1)}, bf16[1536,192]{0,1:T(8,128)(2,1)}, u32[]{:S(2)}) copy-start(bf16[1536,192]{0,1:T(8,128)(2,1)} %param.12) | copy-start | bytes 1769476
  34.0 1.0 %copy-start.5 = (bf16[1536,128]{1,0:T(8,128)(2,1)S(1)}, bf16[1536,128]{1,0:T(8,128)(2,1)}, u32[]{:S(2)}) copy-start(bf16[1536,128]{1,0:T(8,128)(2,1)} %w_key.1) | copy-start | bytes 1179652
  35.0 22.4 %slice-start.1 = ((s8[4718592]{0:T(1024)(128)(4,1)}), s8[524288]{0:T(1024)(128)(4,1)S(1)}, s32[]{:S(2)}) async-start(s8[4718592]{0:T(1024)(128)(4,1)} %bitcast.5), calls=%async_computation.1 | async-start | bytes 1048576
  39.4 9.0 %collective-permute-start.1 = (bf16[960,128]{1,0:T(8,128)(2,1)S(1)}, bf16[960,128]{1,0:T(8,128)(2,1)S(1)}, u32[]{:S(2)}, u32[]{:S(2)}) collective-permute-start(bf16[960,128]{1,0:T(8,128)(2,1)S(1)} %get-tuple-element.8), channel_id=1, source_target_pairs={{0,2},{1,3},{2,0},{3,1},{4,6},{5,7},{6,4},{7,5},{8,10},{9,11},{10,... | collective-permute-start | bytes 737288 | tf_op jit(solution)/shard_map/ppermute | solution.py:241
  41.6 13.0 %collective-permute-start.2 = (bf16[960,128]{1,0:T(8,128)(2,1)S(1)}, bf16[960,128]{1,0:T(8,128)(2,1)S(1)}, u32[]{:S(2)}, u32[]{:S(2)}) collective-permute-start(bf16[960,128]{1,0:T(8,128)(2,1)S(1)} %get-tuple-element.8), channel_id=1, source_target_pairs={{0,4},{1,5},{2,6},{3,7},{4,0},{5,1},{6,2},{7,3},{8,12},{9,13},{10,... | collective-permute-start | bytes 737288 | tf_op jit(solution)/shard_map/ppermute | solution.py:241
  43.2 11.5 %collective-permute-start.3 = (bf16[960,128]{1,0:T(8,128)(2,1)S(1)}, bf16[960,128]{1,0:T(8,128)(2,1)S(1)}, u32[]{:S(2)}, u32[]{:S(2)}) collective-permute-start(bf16[960,128]{1,0:T(8,128)(2,1)S(1)} %get-tuple-element.8), channel_id=1, source_target_pairs={{0,6},{1,7},{2,4},{3,5},{4,2},{5,3},{6,0},{7,1},{8,14},{9,15},{10,... | collective-permute-start | bytes 737288 | tf_op jit(solution)/shard_map/ppermute | solution.py:241
  54.7 2.6 %collective-permute-start.4 = (bf16[3840,128]{1,0:T(8,128)(2,1)S(1)}, bf16[3840,128]{1,0:T(8,128)(2,1)S(1)}, u32[]{:S(2)}, u32[]{:S(2)}) collective-permute-start(bf16[3840,128]{1,0:T(8,128)(2,1)S(1)} %constant_dynamic-update-slice_fusion.refs_1_), channel_id=1, source_target_pairs={{0,1},{1,0},{2,3},{3,2},{4,5},{5,4},{6,7},{7,6},{8,9},{9,8},{10,11... | collective-permute-start | bytes 2949128 | tf_op jit(solution)/shard_map/ppermute | solution.py:244

commit v2 on v1

v2 whole, which is shorter than its diff:
```python
import functools
import math

import jax
import jax.numpy as jnp
from jax import lax
from jax.experimental import pallas as pl
from jax.experimental.pallas import tpu as pltpu
from jax.sharding import PartitionSpec as P

F32 = jnp.float32
BF16 = jnp.bfloat16
CONTRACT_LAST = (((1,), (1,)), ((), ()))
STACKED = 384


def whole(memory_space=pltpu.VMEM):
    return pl.BlockSpec(memory_space=memory_space)


def reversed_rows(block):
    rows = block.shape[0]
    row = lax.broadcasted_iota(jnp.int32, (rows, rows), 0)
    column = lax.broadcasted_iota(jnp.int32, (rows, rows), 1)
    swap = (row + column == rows - 1).astype(F32).astype(BF16)
    return jnp.dot(swap, block, preferred_element_type=F32).astype(BF16)


def product(left, right):
    return jnp.dot(left, right, preferred_element_type=F32)


def own_kernel(tokens, w_same, w_partner, w_key, w_value, same, partner, w_pair):
    rows, keys = same.shape[0], w_key.shape[1]
    w_pair[:, :keys] = w_key[...]
    w_pair[:, keys : keys + w_value.shape[0]] = w_value[...].T
    w_pair[:, keys + w_value.shape[0] :] = jnp.zeros(
        (w_pair.shape[0], w_pair.shape[1] - keys - w_value.shape[0]), BF16
    )
    block = tokens[:rows, :]
    same[...] = product(block, w_same[...])
    partner[...] = product(reversed_rows(block), w_partner[...])


def own_products(tokens, w_same, w_partner, w_key, w_value, rows):
    width, features = w_same.shape
    both = -(-(w_key.shape[1] + w_value.shape[0]) // 128) * 128
    return pl.pallas_call(
        own_kernel,
        in_specs=[whole()] * 5,
        out_specs=[whole()] * 3,
        out_shape=[jax.ShapeDtypeStruct((rows, features), F32)] * 2
        + [jax.ShapeDtypeStruct((width, both), BF16)],
        compiler_params=pltpu.CompilerParams(vmem_limit_bytes=20 << 20),
        cost_estimate=pl.CostEstimate(
            flops=4 * rows * width * features, bytes_accessed=4 * width * features, transcendentals=0
        ),
        name="own_products",
    )(tokens, w_same, w_partner, w_key, w_value)


def pack(pair, value, rows, lanes):
    width = value.shape[1]
    at = rows
    for lane in range(0, width - width % lanes, lanes):
        pair[at : at + rows, :] = value[:, lane : lane + lanes]
        at += rows
    rest = width % lanes
    if rest:
        share = rows * rest // lanes
        pair[at : at + share, :] = jnp.concatenate(
            [value[i * share : (i + 1) * share, width - rest :] for i in range(lanes // rest)], 1
        )


def unpack(pair, at, rows, lanes, width):
    key = pair[at : at + rows, :]
    at += rows
    parts = []
    for _ in range(width // lanes):
        parts.append(pair[at : at + rows, :])
        at += rows
    rest = width % lanes
    if rest:
        share = rows * rest // lanes
        tail = pair[at : at + share, :]
        parts.append(
            jnp.concatenate([tail[:, i * rest : (i + 1) * rest] for i in range(lanes // rest)], 0)
        )
    return key, jnp.concatenate(parts, 1)


def hidden_kernel(keys, values, arrived, same, partner, w_same, w_partner, w_pair, hidden, own, other):
    rows = arrived.shape[0]
    block = arrived[...]
    upper = (same[...] + product(reversed_rows(block), w_partner[...])).astype(BF16)
    lower = (product(block, w_same[...]) + partner[...]).astype(BF16)
    hidden[:rows, :] = upper
    hidden[rows:, :] = lower
    both = jnp.concatenate([upper, lower], 0)
    result = product(both, w_pair[...]).astype(BF16)
    for pair, at in ((own, 0), (other, rows)):
        pair[:rows, :] = result[at : at + rows, :keys]
        pack(pair, result[at : at + rows, keys : keys + values], rows, keys)


def hidden_and_pairs(arrived, same, partner, w_same, w_partner, w_pair, keys, values):
    rows, width = arrived.shape
    pair = jax.ShapeDtypeStruct((rows * (keys + values) // keys, keys), BF16)
    return pl.pallas_call(
        functools.partial(hidden_kernel, keys, values),
        in_specs=[whole()] * 6,
        out_specs=[whole()] * 3,
        out_shape=[jax.ShapeDtypeStruct((2 * rows, width), BF16), pair, pair],
        compiler_params=pltpu.CompilerParams(vmem_limit_bytes=20 << 20),
        cost_estimate=pl.CostEstimate(
            flops=4 * rows * width * (width + keys + values),
            bytes_accessed=4 * width * width,
            transcendentals=0,
        ),
        name="hidden_and_pairs",
    )(arrived, same, partner, w_same, w_partner, w_pair)


def query_kernel(hidden, w_query, *queries):
    result = product(hidden[...], w_query[...]).astype(BF16)
    at = 0
    for query in queries:
        query[...] = result[at : at + query.shape[0], :]
        at += query.shape[0]


def query_rows(hidden, w_query, sizes):
    width, queries = w_query.shape
    return pl.pallas_call(
        query_kernel,
        in_specs=[whole()] * 2,
        out_specs=[whole()] * len(sizes),
        out_shape=[jax.ShapeDtypeStruct((size, queries), BF16) for size in sizes],
        compiler_params=pltpu.CompilerParams(vmem_limit_bytes=16 << 20),
        cost_estimate=pl.CostEstimate(
            flops=2 * hidden.shape[0] * width * queries,
            bytes_accessed=2 * width * queries,
            transcendentals=0,
        ),
        name="query_rows",
    )(hidden, w_query)


def attend_kernel(shape, *refs):
    n_query, blocks, has_state, last, heads, group, keys, values = shape
    refs = list(refs)
    queries = [refs.pop(0) for _ in range(n_query)]
    pairs = [refs.pop(0) for _ in blocks]
    states = [(refs.pop(0), refs.pop(0)) for _ in range(n_query if has_state else 0)]
    if last:
        w_out, out = refs.pop(0), refs.pop(0)
    else:
        new_sum, new_peak = refs.pop(0), refs.pop(0)
    held, extended, scores = refs.pop(0), refs.pop(0), refs.pop(0)
    if last:
        mixed = refs.pop(0)
    rows = queries[0].shape[0]
    units = [(index, unit) for index in range(n_query) for unit in range(heads // group)]
    padded = extended.shape[1]
    scale = keys**-0.5 * math.log2(math.e)
    seen = 0
    for pair, block in zip(pairs, blocks):
        packed = block * (keys + values) // keys
        for at in range(0, pair.shape[0], packed):
            key, value = unpack(pair, at, block, keys, values)
            held[seen : seen + block, :] = key
            extended[seen : seen + block, :values] = value
            seen += block
    extended[:, values:] = jnp.ones((seen, padded - values), BF16)
    step = 512 if seen % 512 == 0 else 256

    def score(index, unit, slot):
        wide = group * keys
        columns = queries[index][:, unit * wide : (unit + 1) * wide]
        stacked = jnp.concatenate([columns[:, i * keys : (i + 1) * keys] for i in range(group)], 0)
        peak = None
        for at in range(0, seen, step):
            block = lax.dot_general(
                stacked, held[at : at + step, :], CONTRACT_LAST, preferred_element_type=F32
            )
            scores[slot, :, at : at + step] = block
            for lane in range(0, step, 128):
                part = block[:, lane : lane + 128]
                peak = part if peak is None else jnp.maximum(peak, part)
        peak = jnp.max(peak, axis=1, keepdims=True)
        if has_state:
            peak = jnp.maximum(peak, states[index][1][unit][:, :1])
        return peak

    def mix(index, unit, slot, peak):
        total = None
        for at in range(0, seen, step):
            weights = jnp.exp2((scores[slot, :, at : at + step] - peak) * scale).astype(BF16)
            part = jnp.dot(weights, extended[at : at + step, :], preferred_element_type=F32)
            total = part if total is None else total + part
        if has_state:
            old_sum, old_peak = states[index]
            decay = jnp.exp2((old_peak[unit][:, :1] - peak) * scale)
            total = total + old_sum[unit] * decay
        if not last:
            new_sum[unit] = total
            new_peak[unit] = jnp.broadcast_to(peak, new_peak.shape[1:])
            return
        result = (total[:, :values] / total[:, values : values + 1]).astype(BF16)
        wide = group * values
        mixed[index * rows : (index + 1) * rows, unit * wide : (unit + 1) * wide] = jnp.concatenate(
            [result[i * rows : (i + 1) * rows, :] for i in range(group)], 1
        )

    peak = score(*units[0], 0)
    for at, unit in enumerate(units):
        following = score(*units[at + 1], (at + 1) % 2) if at + 1 < len(units) else None
        mix(*unit, at % 2, peak)
        peak = following
    if last:
        out[...] = product(mixed[...], w_out[...]).astype(BF16)


def attend(queries, pairs, block, keys, values, states=None, w_out=None, weight=1.0):
    rows = queries[0].shape[0]
    heads = queries[0].shape[1] // keys
    group = 2
    while group * rows < STACKED and heads % (2 * group) == 0:
        group *= 2
    seen = sum(pair.shape[0] for pair in pairs) * keys // (keys + values)
    padded = (values // 128 + 1) * 128
    last = w_out is not None
    shape = (len(queries), [block] * len(pairs), states is not None, last, heads, group, keys, values)
    arguments = list(queries) + list(pairs) + [part for state in states or () for part in state]
    scratch = [
        pltpu.VMEM((seen, keys), BF16),
        pltpu.VMEM((seen, padded), BF16),
        pltpu.VMEM((2, group * rows, seen), F32),
    ]
    if last:
        arguments.append(w_out)
        out_shape = jax.ShapeDtypeStruct((rows * len(queries), w_out.shape[1]), BF16)
        out_specs = whole()
        scratch.append(pltpu.VMEM((rows * len(queries), heads * values), BF16))
    else:
        out_shape = [
            jax.ShapeDtypeStruct((heads // group, group * rows, padded), F32),
            jax.ShapeDtypeStruct((heads // group, group * rows, 128), F32),
        ]
        out_specs = [whole()] * 2
    flops = int(weight * 2 * len(queries) * rows * heads * seen * (keys + values))
    if last:
        flops += 2 * len(queries) * rows * heads * values * w_out.shape[1]
    return pl.pallas_call(
        functools.partial(attend_kernel, shape),
        in_specs=[whole()] * len(arguments),
        out_specs=out_specs,
        out_shape=out_shape,
        scratch_shapes=scratch,
        compiler_params=pltpu.CompilerParams(vmem_limit_bytes=28 << 20),
        cost_estimate=pl.CostEstimate(
            flops=flops,
            bytes_accessed=2 * seen * (keys + values),
            transcendentals=0,
        ),
        name="attend",
    )(*arguments)


def to_both_cores(parts):
    count = lax.axis_size("seq")
    return parts + [lax.ppermute(part, "seq", [(s, s ^ 1) for s in range(count)]) for part in parts]


def crossed(value, lane_bit, place_bits):
    lanes, count = lax.axis_size("ws"), lax.axis_size("seq")
    pairs = [
        (w * count + s, (w ^ lane_bit) * count + (s ^ place_bits))
        for w in range(lanes)
        for s in range(count)
    ]
    return lax.ppermute(value, ("ws", "seq"), pairs)


def body(tokens, w_same, w_partner, w_query, w_key, w_value, w_out):
    count = lax.axis_size("seq")
    local = tokens[0]
    half = local.shape[0] // 2
    keys, values = w_key.shape[1], w_value.shape[1]
    arrived = crossed(local[half:], 1, count - 1)
    same, partner, w_pair = own_products(local, w_same, w_partner, w_key, w_value.T, half)
    hidden, own, other = hidden_and_pairs(
        arrived, same, partner, w_same, w_partner, w_pair, keys, values
    )
    near = [own] + [crossed(own, 0, k) for k in range(2, count, 2)]
    lifted = crossed(other, 1, 0)
    query, sent = query_rows(hidden, w_query, [half, half])
    near, lifted, query = lax.optimization_barrier((near, lifted, query))
    near = to_both_cores(near)
    brought = crossed(sent, 1, count - 1)
    mine = attend([query], near, half, keys, values, weight=1.7)
    brought, mine = lax.optimization_barrier((brought, mine))
    far = [lifted] + [crossed(lifted, 0, k) for k in range(2, count, 2)]
    theirs = attend([brought], near, half, keys, values, weight=0.1)
    far, theirs = lax.optimization_barrier((far, theirs))
    far = to_both_cores(far)
    result = attend([query, brought], far, half, keys, values, [mine, theirs], w_out)
    return result[None]


def solution(mesh):
    placed = (P("ws", "seq", None), P(), P(), P(), P(), P(), P())
    return jax.shard_map(
        body, mesh=mesh, in_specs=placed, out_specs=P("ws", "seq", None), check_vma=False
    )
```

time: 73.5 us -> 59.4 us (0.81)
  waiting for transfers between devices: 34.2 us -> 12 us
  starting transfers between devices: 8.21 us -> 16.9 us
  Pallas kernels: 23 us -> 22.2 us
    ppermute x5 -> x17, waiting for transfers between devices: 34.2 us -> 12 us  [the longest x9 10.7 us: crossed(): return lax.ppermute(value, ('ws', 'seq'), pairs)]
    ppermute x5 -> x17, starting transfers between devices: 8.21 us -> 16.9 us  [the longest x9 14.8 us: crossed(): return lax.ppermute(value, ('ws', 'seq'), pairs)]
    slice x0 -> x1, local copies, waits for them, and re-layouts: none -> 1.2 us  [body(): arrived = crossed(local[half:], 1, count - 1)]
    unnamed x19 -> x20, local copies, waits for them, and re-layouts: 7.65 us -> 6.75 us
    pallas_call x2 -> x3, Pallas kernels: 7.2 us -> 6.34 us  [the longest x1 2.81 us: hidden_and_pairs(): pl.pallas_call(functools.partial(hidden_kernel, keys, values), in_specs=[...]
    pallas_call x1 -> x3, Pallas kernels: 15.8 us -> 15.9 us  [attend(): pl.pallas_call(functools.partial(attend_kernel, shape), in_specs=[whole()...]
  transfers between devices with their start and end apart: 5 -> 17, of which waited for: 4 -> 12; matrix products, arithmetic and copies ran while one was open for 0% -> 0% of each run, Pallas kernels for 4% -> 16%
where the time goes in v2:
time: 59.4 us; the launch traced here: 59.1 us
  Pallas kernels  22.2 us (37%)
  starting transfers between devices  16.9 us (28%)
  waiting for transfers between devices  12 us (20%)
  local copies, waits for them, and re-layouts  7.95 us (13%)
    pallas_call x3, Pallas kernels, attend(): pl.pallas_call(functools.partial(attend_kernel, shape), in_specs=[whole()...  15.9 us
    ppermute x9, starting transfers between devices, crossed(): return lax.ppermute(value, ('ws', 'seq'), pairs)  14.8 us
    ppermute x9, waiting for transfers between devices, crossed(): return lax.ppermute(value, ('ws', 'seq'), pairs)  10.7 us
    unnamed x20, local copies, waits for them, and re-layouts  6.75 us
    pallas_call x1, Pallas kernels, hidden_and_pairs(): pl.pallas_call(functools.partial(hidden_kernel, keys, values), in_specs=[...  2.81 us
    pallas_call x1, Pallas kernels, own_products(): pl.pallas_call(own_kernel, in_specs=[whole()] * 5, out_specs=[whole()] *...  2.16 us
    ppermute x8, starting transfers between devices, to_both_cores(): lax.ppermute(part, 'seq', [(s, s ^ 1) for s in range(count)])  2.04 us
    pallas_call x1, Pallas kernels, query_rows(): pl.pallas_call(query_kernel, in_specs=[whole()] * 2, out_specs=[whole()]...  1.38 us
  transfers between devices with their start and end apart: 17, of which 12 were waited for; matrix products, arithmetic and copies ran while one was open for 0% of the time, Pallas kernels for 16%

profile of v2, /device:TPU:0, one launch (start us, length us, event | category | flops | bytes accessed | tf_op | source)
XLA Modules:
  0.0 59.1 jit_solution(15132964837100266918)
XLA Ops:
  0.0 1.2 %slice_bitcast_fusion = bf16[192,1536]{1,0:T(8,128)(2,1)S(1)} fusion(bf16[1,384,1536]{2,1,0:T(8,128)(2,1)} %param.7), kind=kLoop, calls=%fused_computation | loop fusion | bytes 1179648 | tf_op jit(solution)/shard_map/slice | solution.py:291
  1.2 4.4 %collective-permute-start = (bf16[192,1536]{1,0:T(8,128)(2,1)S(1)}, bf16[192,1536]{1,0:T(8,128)(2,1)S(1)}, u32[]{:S(2)}, u32[]{:S(2)}) collective-permute-start(bf16[192,1536]{1,0:T(8,128)(2,1)S(1)} %slice_bitcast_fusion), channel_id=1, source_target_pairs={{0,15},{1,14},{2,13},{3,12},{4,11},{5,10},{6,9},{7,8},{8,7},{9,6},... | collective-permute-start | bytes 1769480 | tf_op jit(solution)/shard_map/ppermute | solution.py:283
  5.6 2.3 %copy-done = bf16[1536,1536]{1,0:T(8,128)(2,1)S(1)} copy-done((bf16[1536,1536]{1,0:T(8,128)(2,1)S(1)}, bf16[1536,1536]{1,0:T(8,128)(2,1)}, u32[]{:S(2)}) %copy-start) | copy-done | bytes 4718616
  8.0 2.3 %copy-done.2 = bf16[1536,1536]{1,0:T(8,128)(2,1)S(1)} copy-done((bf16[1536,1536]{1,0:T(8,128)(2,1)S(1)}, bf16[1536,1536]{1,0:T(8,128)(2,1)}, u32[]{:S(2)}) %copy-start.2) | copy-done | bytes 4718616
  10.3 1.1 %copy-done.5 = bf16[1536,192]{0,1:T(8,128)(2,1)S(1)} copy-done((bf16[1536,192]{0,1:T(8,128)(2,1)S(1)}, bf16[1536,192]{0,1:T(8,128)(2,1)}, u32[]{:S(2)}) %copy-start.5) | copy-done | bytes 589848
  11.4 1.0 %copy-done.6 = bf16[1536,128]{1,0:T(8,128)(2,1)S(1)} copy-done((bf16[1536,128]{1,0:T(8,128)(2,1)S(1)}, bf16[1536,128]{1,0:T(8,128)(2,1)}, u32[]{:S(2)}) %copy-start.6) | copy-done | bytes 393240
  12.4 2.2 %own_products.1 = (f32[192,1536]{1,0:T(8,128)S(1)}, f32[192,1536]{1,0:T(8,128)S(1)}, bf16[1536,384]{1,0:T(8,128)(2,1)S(1)}) custom-call(bf16[384,1536]{1,0:T(8,128)(2,1)S(1)} %bitcast.5, bf16[1536,1536]{1,0:T(8,128)(2,1)S(1)} %copy-done, bf16[1536,1536]{1,0:T(8,128)(2,1)S(1)} %copy-done.2, bf16[1536,128]{1,0:T(8,128)(2,1)S(1)} %copy-done.6, ...), custom_call_target="tpu_custom_call" | custom-call | flops 1811939328 | bytes 9437184 | tf_op jit(solution)/shard_map/own_products/pallas_call | solution.py:48
  14.5 4.8 %collective-permute-done.arrived = bf16[192,1536]{1,0:T(8,128)(2,1)S(1)} collective-permute-done((bf16[192,1536]{1,0:T(8,128)(2,1)S(1)}, bf16[192,1536]{1,0:T(8,128)(2,1)S(1)}, u32[]{:S(2)}, u32[]{:S(2)}) %collective-permute-start) | collective-permute-done | bytes 589856 | tf_op jit(solution)/shard_map/ppermute | solution.py:283
  19.3 2.8 %hidden_and_pairs.1 = (bf16[384,1536]{1,0:T(8,128)(2,1)S(1)}, bf16[480,128]{1,0:T(8,128)(2,1)S(1)}, bf16[480,128]{1,0:T(8,128)(2,1)S(1)}) custom-call(bf16[192,1536]{1,0:T(8,128)(2,1)S(1)} %collective-permute-done.arrived, f32[192,1536]{1,0:T(8,128)S(1)} %get-tuple-element.32.same, f32[192,1536]{1,0:T(8,128)S(1)} %get-tuple-element.33.partner, ...), custom_call_target="tpu_custom_call" | custom-call | flops 2189426688 | bytes 9437184 | tf_op jit(solution)/shard_map/hidden_and_pairs/pallas_call | solution.py:110
  22.2 3.3 %collective-permute-start.3 = (bf16[480,128]{1,0:T(8,128)(2,1)S(1)}, bf16[480,128]{1,0:T(8,128)(2,1)S(1)}, u32[]{:S(2)}, u32[]{:S(2)}) collective-permute-start(bf16[480,128]{1,0:T(8,128)(2,1)S(1)} %get-tuple-element.41.refs_1_), channel_id=1, source_target_pairs={{0,6},{1,7},{2,4},{3,5},{4,2},{5,3},{6,0},{7,1},{8,14},{9,15},{10,... | collective-permute-start | bytes 368648 | tf_op jit(solution)/shard_map/ppermute | solution.py:283
  25.5 0.5 collective-permute-start.2
  26.1 2.0 %collective-permute-start.4 = (bf16[480,128]{1,0:T(8,128)(2,1)S(1)}, bf16[480,128]{1,0:T(8,128)(2,1)S(1)}, u32[]{:S(2)}, u32[]{:S(2)}) collective-permute-start(bf16[480,128]{1,0:T(8,128)(2,1)S(1)} %get-tuple-element.36), channel_id=1, source_target_pairs={{0,8},{1,9},{2,10},{3,11},{4,12},{5,13},{6,14},{7,15},{8,0},{9,1},... | collective-permute-start | bytes 368648 | tf_op jit(solution)/shard_map/ppermute | solution.py:283
  28.1 1.4 %query_rows.1 = (bf16[192,1024]{1,0:T(8,128)(2,1)S(1)}, bf16[192,1024]{1,0:T(8,128)(2,1)S(1)}) custom-call(bf16[384,1536]{1,0:T(8,128)(2,1)S(1)} %get-tuple-element.37.hidden, bf16[1536,1024]{1,0:T(8,128)(2,1)S(1)} %copy-done.7), custom_call_target="tpu_custom_call" | custom-call | flops 1207959552 | bytes 3145728 | tf_op jit(solution)/shard_map/query_rows/pallas_call | solution.py:135
  29.5 1.0 %collective-permute-start.5 = (bf16[192,1024]{1,0:T(8,128)(2,1)S(1)}, bf16[192,1024]{1,0:T(8,128)(2,1)S(1)}, u32[]{:S(2)}, u32[]{:S(2)}) collective-permute-start(bf16[192,1024]{1,0:T(8,128)(2,1)S(1)} %get-tuple-element.40), channel_id=1, source_target_pairs={{0,15},{1,14},{2,13},{3,12},{4,11},{5,10},{6,9},{7,8},{8,7},{9,6},... | collective-permute-start | bytes 1179656 | tf_op jit(solution)/shard_map/ppermute | solution.py:283
  30.5 0.5 collective-permute-done.4.refs_2_
  31.0 0.7 %collective-permute-done.2.refs_3_ = bf16[480,128]{1,0:T(8,128)(2,1)S(1)} collective-permute-done((bf16[480,128]{1,0:T(8,128)(2,1)S(1)}, bf16[480,128]{1,0:T(8,128)(2,1)S(1)}, u32[]{:S(2)}, u32[]{:S(2)}) %collective-permute-start.2) | collective-permute-done | bytes 122912 | tf_op jit(solution)/shard_map/ppermute | solution.py:283
  33.3 2.0 %collective-permute-start.12 = (bf16[480,128]{1,0:T(8,128)(2,1)S(1)}, bf16[480,128]{1,0:T(8,128)(2,1)S(1)}, u32[]{:S(2)}, u32[]{:S(2)}) collective-permute-start(bf16[480,128]{1,0:T(8,128)(2,1)S(1)} %collective-permute-done.4.refs_2_), channel_id=1, source_target_pairs={{0,6},{1,7},{2,4},{3,5},{4,2},{5,3},{6,0},{7,1},{8,14},{9,15},{10,... | collective-permute-start | bytes 368648 | tf_op jit(solution)/shard_map/ppermute | solution.py:283
  35.3 1.0 %collective-permute-start.11 = (bf16[480,128]{1,0:T(8,128)(2,1)S(1)}, bf16[480,128]{1,0:T(8,128)(2,1)S(1)}, u32[]{:S(2)}, u32[]{:S(2)}) collective-permute-start(bf16[480,128]{1,0:T(8,128)(2,1)S(1)} %collective-permute-done.4.refs_2_), channel_id=1, source_target_pairs={{0,4},{1,5},{2,6},{3,7},{4,0},{5,1},{6,2},{7,3},{8,12},{9,13},{10,... | collective-permute-start | bytes 368648 | tf_op jit(solution)/shard_map/ppermute | solution.py:283
  36.3 0.5 collective-permute-start.10
  36.8 3.1 %attend.3 = (f32[4,384,256]{2,1,0:T(8,128)S(1)}, f32[4,384,128]{2,1,0:T(8,128)S(1)}) custom-call(bf16[192,1024]{1,0:T(8,128)(2,1)S(1)} %get-tuple-element.39.refs_0_, bf16[480,128]{1,0:T(8,128)(2,1)S(1)} %get-tuple-element.41.refs_1_, bf16[480,128]{1,0:T(8,128)(2,1)S(1)} %collective-permute-done.1.refs_2_, ...), custom_call_target="tpu_custom_call" | custom-call | flops 2566914048 | bytes 983040 | tf_op jit(solution)/shard_map/attend/pallas_call | solution.py:255
  39.9 2.3 %collective-permute-done.5.refs_0_.refs_1_ = bf16[192,1024]{1,0:T(8,128)(2,1)S(1)} collective-permute-done((bf16[192,1024]{1,0:T(8,128)(2,1)S(1)}, bf16[192,1024]{1,0:T(8,128)(2,1)S(1)}, u32[]{:S(2)}, u32[]{:S(2)}) %collective-permute-start.5) | collective-permute-done | bytes 393248 | tf_op jit(solution)/shard_map/ppermute | solution.py:283
  42.1 3.1 %attend.4 = (f32[4,384,256]{2,1,0:T(8,128)S(1)}, f32[4,384,128]{2,1,0:T(8,128)S(1)}) custom-call(bf16[192,1024]{1,0:T(8,128)(2,1)S(1)} %collective-permute-done.5.refs_0_.refs_1_, bf16[480,128]{1,0:T(8,128)(2,1)S(1)} %get-tuple-element.41.refs_1_, bf16[480,128]{1,0:T(8,128)(2,1)S(1)} %collective-permute-done.1.refs_2_, ...), custom_call_target="tpu_custom_call" | custom-call | flops 150994944 | bytes 983040 | tf_op jit(solution)/shard_map/attend/pallas_call | solution.py:255
  45.2 2.0 %collective-permute-done.11.refs_4_ = bf16[480,128]{1,0:T(8,128)(2,1)S(1)} collective-permute-done((bf16[480,128]{1,0:T(8,128)(2,1)S(1)}, bf16[480,128]{1,0:T(8,128)(2,1)S(1)}, u32[]{:S(2)}, u32[]{:S(2)}) %collective-permute-start.11) | collective-permute-done | bytes 122912 | tf_op jit(solution)/shard_map/ppermute | solution.py:283
  49.3 9.7 %attend.5 = bf16[384,1536]{1,0:T(8,128)(2,1)} custom-call(bf16[192,1024]{1,0:T(8,128)(2,1)S(1)} %get-tuple-element.39.refs_0_, bf16[192,1024]{1,0:T(8,128)(2,1)S(1)} %collective-permute-done.5.refs_0_.refs_1_, bf16[480,128]{1,0:T(8,128)(2,1)S(1)} %collective-permute-done.4.refs_2_, bf16[480,128]{1,0:T(8,128)(2,1)S(1)} %collective-permute-done.10.refs_3_, ...), custom_call_target="tpu_custom_call" | custom-call | flops 4831838208 | bytes 983040 | tf_op jit(solution)/shard_map/attend/pallas_call | solution.py:255
  (38 shorter events, 3.9 us)
Async XLA Ops:
  0.0 5.6 %copy-start.4 = (bf16[1,384,1536]{2,1,0:T(8,128)(2,1)S(1)}, bf16[1,384,1536]{2,1,0:T(8,128)(2,1)}, u32[]{:S(2)}) copy-start(bf16[1,384,1536]{2,1,0:T(8,128)(2,1)} %param.7) | copy-start | bytes 3538948
  1.2 18.1 %collective-permute-start = (bf16[192,1536]{1,0:T(8,128)(2,1)S(1)}, bf16[192,1536]{1,0:T(8,128)(2,1)S(1)}, u32[]{:S(2)}, u32[]{:S(2)}) collective-permute-start(bf16[192,1536]{1,0:T(8,128)(2,1)S(1)} %slice_bitcast_fusion), channel_id=1, source_target_pairs={{0,15},{1,14},{2,13},{3,12},{4,11},{5,10},{6,9},{7,8},{8,7},{9,6},... | collective-permute-start | bytes 1769480 | tf_op jit(solution)/shard_map/ppermute | solution.py:283
  5.6 2.3 %copy-start = (bf16[1536,1536]{1,0:T(8,128)(2,1)S(1)}, bf16[1536,1536]{1,0:T(8,128)(2,1)}, u32[]{:S(2)}) copy-start(bf16[1536,1536]{1,0:T(8,128)(2,1)} %w_same.3) | copy-start | bytes 14155780
  12.4 7.0 %copy-start.1 = (bf16[1536,1536]{1,0:T(8,128)(2,1)S(1)}, bf16[1536,1536]{1,0:T(8,128)(2,1)}, u32[]{:S(2)}) copy-start(bf16[1536,1536]{1,0:T(8,128)(2,1)} %w_same.3) | copy-start | bytes 14155780
  12.4 7.0 %copy-start.3 = (bf16[1536,1536]{1,0:T(8,128)(2,1)S(1)}, bf16[1536,1536]{1,0:T(8,128)(2,1)}, u32[]{:S(2)}) copy-start(bf16[1536,1536]{1,0:T(8,128)(2,1)} %w_partner.3) | copy-start | bytes 14155780
  19.3 8.7 %copy-start.7 = (bf16[1536,1024]{1,0:T(8,128)(2,1)S(1)}, bf16[1536,1024]{1,0:T(8,128)(2,1)}, u32[]{:S(2)}) copy-start(bf16[1536,1024]{1,0:T(8,128)(2,1)} %w_query.1) | copy-start | bytes 9437188
  22.2 8.8 %collective-permute-start.3 = (bf16[480,128]{1,0:T(8,128)(2,1)S(1)}, bf16[480,128]{1,0:T(8,128)(2,1)S(1)}, u32[]{:S(2)}, u32[]{:S(2)}) collective-permute-start(bf16[480,128]{1,0:T(8,128)(2,1)S(1)} %get-tuple-element.41.refs_1_), channel_id=1, source_target_pairs={{0,6},{1,7},{2,4},{3,5},{4,2},{5,3},{6,0},{7,1},{8,14},{9,15},{10,... | collective-permute-start | bytes 368648 | tf_op jit(solution)/shard_map/ppermute | solution.py:283
  25.5 6.2 %collective-permute-start.2 = (bf16[480,128]{1,0:T(8,128)(2,1)S(1)}, bf16[480,128]{1,0:T(8,128)(2,1)S(1)}, u32[]{:S(2)}, u32[]{:S(2)}) collective-permute-start(bf16[480,128]{1,0:T(8,128)(2,1)S(1)} %get-tuple-element.41.refs_1_), channel_id=1, source_target_pairs={{0,4},{1,5},{2,6},{3,7},{4,0},{5,1},{6,2},{7,3},{8,12},{9,13},{10,... | collective-permute-start | bytes 368648 | tf_op jit(solution)/shard_map/ppermute | solution.py:283
  26.0 6.0 %collective-permute-start.1 = (bf16[480,128]{1,0:T(8,128)(2,1)S(1)}, bf16[480,128]{1,0:T(8,128)(2,1)S(1)}, u32[]{:S(2)}, u32[]{:S(2)}) collective-permute-start(bf16[480,128]{1,0:T(8,128)(2,1)S(1)} %get-tuple-element.41.refs_1_), channel_id=1, source_target_pairs={{0,2},{1,3},{2,0},{3,1},{4,6},{5,7},{6,4},{7,5},{8,10},{9,11},{10,... | collective-permute-start | bytes 368648 | tf_op jit(solution)/shard_map/ppermute | solution.py:283
  26.1 4.9 %collective-permute-start.4 = (bf16[480,128]{1,0:T(8,128)(2,1)S(1)}, bf16[480,128]{1,0:T(8,128)(2,1)S(1)}, u32[]{:S(2)}, u32[]{:S(2)}) collective-permute-start(bf16[480,128]{1,0:T(8,128)(2,1)S(1)} %get-tuple-element.36), channel_id=1, source_target_pairs={{0,8},{1,9},{2,10},{3,11},{4,12},{5,13},{6,14},{7,15},{8,0},{9,1},... | collective-permute-start | bytes 368648 | tf_op jit(solution)/shard_map/ppermute | solution.py:283
  28.1 21.2 %slice-start = ((s8[4718592]{0:T(1024)(128)(4,1)}), s8[4194304]{0:T(1024)(128)(4,1)S(1)}, s32[]{:S(2)}) async-start(s8[4718592]{0:T(1024)(128)(4,1)} %bitcast.7), calls=%async_computation | async-start | bytes 8388608
  29.5 12.6 %collective-permute-start.5 = (bf16[192,1024]{1,0:T(8,128)(2,1)S(1)}, bf16[192,1024]{1,0:T(8,128)(2,1)S(1)}, u32[]{:S(2)}, u32[]{:S(2)}) collective-permute-start(bf16[192,1024]{1,0:T(8,128)(2,1)S(1)} %get-tuple-element.40), channel_id=1, source_target_pairs={{0,15},{1,14},{2,13},{3,12},{4,11},{5,10},{6,9},{7,8},{8,7},{9,6},... | collective-permute-start | bytes 1179656 | tf_op jit(solution)/shard_map/ppermute | solution.py:283
  31.9 17.4 %slice-start.1 = ((s8[4718592]{0:T(1024)(128)(4,1)}), s8[524288]{0:T(1024)(128)(4,1)S(1)}, s32[]{:S(2)}) async-start(s8[4718592]{0:T(1024)(128)(4,1)} %bitcast.7), calls=%async_computation.1 | async-start | bytes 1048576
  31.9 1.3 %collective-permute-start.6 = (bf16[480,128]{1,0:T(8,128)(2,1)S(1)}, bf16[480,128]{1,0:T(8,128)(2,1)S(1)}, u32[]{:S(2)}, u32[]{:S(2)}) collective-permute-start(bf16[480,128]{1,0:T(8,128)(2,1)S(1)} %get-tuple-element.41.refs_1_), channel_id=1, source_target_pairs={{0,1},{1,0},{2,3},{3,2},{4,5},{5,4},{6,7},{7,6},{8,9},{9,8},{10,11... | collective-permute-start | bytes 368648 | tf_op jit(solution)/shard_map/ppermute | solution.py:273
  32.1 3.2 %collective-permute-start.7 = (bf16[480,128]{1,0:T(8,128)(2,1)S(1)}, bf16[480,128]{1,0:T(8,128)(2,1)S(1)}, u32[]{:S(2)}, u32[]{:S(2)}) collective-permute-start(bf16[480,128]{1,0:T(8,128)(2,1)S(1)} %collective-permute-done.1.refs_2_), channel_id=1, source_target_pairs={{0,1},{1,0},{2,3},{3,2},{4,5},{5,4},{6,7},{7,6},{8,9},{9,8},{10,11... | collective-permute-start | bytes 368648 | tf_op jit(solution)/shard_map/ppermute | solution.py:273
  32.5 3.8 %collective-permute-start.8 = (bf16[480,128]{1,0:T(8,128)(2,1)S(1)}, bf16[480,128]{1,0:T(8,128)(2,1)S(1)}, u32[]{:S(2)}, u32[]{:S(2)}) collective-permute-start(bf16[480,128]{1,0:T(8,128)(2,1)S(1)} %collective-permute-done.2.refs_3_), channel_id=1, source_target_pairs={{0,1},{1,0},{2,3},{3,2},{4,5},{5,4},{6,7},{7,6},{8,9},{9,8},{10,11... | collective-permute-start | bytes 368648 | tf_op jit(solution)/shard_map/ppermute | solution.py:273
  32.6 4.2 %collective-permute-start.9 = (bf16[480,128]{1,0:T(8,128)(2,1)S(1)}, bf16[480,128]{1,0:T(8,128)(2,1)S(1)}, u32[]{:S(2)}, u32[]{:S(2)}) collective-permute-start(bf16[480,128]{1,0:T(8,128)(2,1)S(1)} %collective-permute-done.3.refs_4_), channel_id=1, source_target_pairs={{0,1},{1,0},{2,3},{3,2},{4,5},{5,4},{6,7},{7,6},{8,9},{9,8},{10,11... | collective-permute-start | bytes 368648 | tf_op jit(solution)/shard_map/ppermute | solution.py:273
  33.3 11.9 %collective-permute-start.12 = (bf16[480,128]{1,0:T(8,128)(2,1)S(1)}, bf16[480,128]{1,0:T(8,128)(2,1)S(1)}, u32[]{:S(2)}, u32[]{:S(2)}) collective-permute-start(bf16[480,128]{1,0:T(8,128)(2,1)S(1)} %collective-permute-done.4.refs_2_), channel_id=1, source_target_pairs={{0,6},{1,7},{2,4},{3,5},{4,2},{5,3},{6,0},{7,1},{8,14},{9,15},{10,... | collective-permute-start | bytes 368648 | tf_op jit(solution)/shard_map/ppermute | solution.py:283
  35.3 11.9 %collective-permute-start.11 = (bf16[480,128]{1,0:T(8,128)(2,1)S(1)}, bf16[480,128]{1,0:T(8,128)(2,1)S(1)}, u32[]{:S(2)}, u32[]{:S(2)}) collective-permute-start(bf16[480,128]{1,0:T(8,128)(2,1)S(1)} %collective-permute-done.4.refs_2_), channel_id=1, source_target_pairs={{0,4},{1,5},{2,6},{3,7},{4,0},{5,1},{6,2},{7,3},{8,12},{9,13},{10,... | collective-permute-start | bytes 368648 | tf_op jit(solution)/shard_map/ppermute | solution.py:283
  36.3 11.0 %collective-permute-start.10 = (bf16[480,128]{1,0:T(8,128)(2,1)S(1)}, bf16[480,128]{1,0:T(8,128)(2,1)S(1)}, u32[]{:S(2)}, u32[]{:S(2)}) collective-permute-start(bf16[480,128]{1,0:T(8,128)(2,1)S(1)} %collective-permute-done.4.refs_2_), channel_id=1, source_target_pairs={{0,2},{1,3},{2,0},{3,1},{4,6},{5,7},{6,4},{7,5},{8,10},{9,11},{10,... | collective-permute-start | bytes 368648 | tf_op jit(solution)/shard_map/ppermute | solution.py:283
  47.3 1.3 %collective-permute-start.13 = (bf16[480,128]{1,0:T(8,128)(2,1)S(1)}, bf16[480,128]{1,0:T(8,128)(2,1)S(1)}, u32[]{:S(2)}, u32[]{:S(2)}) collective-permute-start(bf16[480,128]{1,0:T(8,128)(2,1)S(1)} %collective-permute-done.4.refs_2_), channel_id=1, source_target_pairs={{0,1},{1,0},{2,3},{3,2},{4,5},{5,4},{6,7},{7,6},{8,9},{9,8},{10,11... | collective-permute-start | bytes 368648 | tf_op jit(solution)/shard_map/ppermute | solution.py:273
  47.3 1.5 %collective-permute-start.14 = (bf16[480,128]{1,0:T(8,128)(2,1)S(1)}, bf16[480,128]{1,0:T(8,128)(2,1)S(1)}, u32[]{:S(2)}, u32[]{:S(2)}) collective-permute-start(bf16[480,128]{1,0:T(8,128)(2,1)S(1)} %collective-permute-done.10.refs_3_), channel_id=1, source_target_pairs={{0,1},{1,0},{2,3},{3,2},{4,5},{5,4},{6,7},{7,6},{8,9},{9,8},{10,11... | collective-permute-start | bytes 368648 | tf_op jit(solution)/shard_map/ppermute | solution.py:273
  47.8 1.3 %collective-permute-start.15 = (bf16[480,128]{1,0:T(8,128)(2,1)S(1)}, bf16[480,128]{1,0:T(8,128)(2,1)S(1)}, u32[]{:S(2)}, u32[]{:S(2)}) collective-permute-start(bf16[480,128]{1,0:T(8,128)(2,1)S(1)} %collective-permute-done.11.refs_4_), channel_id=1, source_target_pairs={{0,1},{1,0},{2,3},{3,2},{4,5},{5,4},{6,7},{7,6},{8,9},{9,8},{10,11... | collective-permute-start | bytes 368648 | tf_op jit(solution)/shard_map/ppermute | solution.py:273
  47.8 1.5 %collective-permute-start.16 = (bf16[480,128]{1,0:T(8,128)(2,1)S(1)}, bf16[480,128]{1,0:T(8,128)(2,1)S(1)}, u32[]{:S(2)}, u32[]{:S(2)}) collective-permute-start(bf16[480,128]{1,0:T(8,128)(2,1)S(1)} %collective-permute-done.12.refs_5_), channel_id=1, source_target_pairs={{0,1},{1,0},{2,3},{3,2},{4,5},{5,4},{6,7},{7,6},{8,9},{9,8},{10,11... | collective-permute-start | bytes 368648 | tf_op jit(solution)/shard_map/ppermute | solution.py:273
  (3 other events, 4.4 us)

commit v3 on v2

--- a/solution.py
+++ b/solution.py
@@ -12,6 +12,7 @@
 BF16 = jnp.bfloat16
 CONTRACT_LAST = (((1,), (1,)), ((), ()))
 STACKED = 384
+COLUMNS = (2, 1)
 
 
 def whole(memory_space=pltpu.VMEM):
@@ -90,32 +91,57 @@
     return key, jnp.concatenate(parts, 1)
 
 
-def hidden_kernel(keys, values, arrived, same, partner, w_same, w_partner, w_pair, hidden, own, other):
+def add_kernel(at, arrived, same, partner, w_same, w_partner, upper, lower):
+    block = arrived[...]
+    depth = pl.ds(at, block.shape[1])
+    upper[...] = same[...] + product(reversed_rows(block), w_partner[depth, :])
+    lower[...] = partner[...] + product(block, w_same[depth, :])
+
+
+def add_products(at, arrived, same, partner, w_same, w_partner):
+    rows, width = arrived.shape
+    features = w_same.shape[1]
+    return pl.pallas_call(
+        functools.partial(add_kernel, at),
+        in_specs=[whole()] * 5,
+        out_specs=[whole()] * 2,
+        out_shape=[jax.ShapeDtypeStruct((rows, features), F32)] * 2,
+        compiler_params=pltpu.CompilerParams(vmem_limit_bytes=20 << 20),
+        cost_estimate=pl.CostEstimate(
+            flops=4 * rows * width * features, bytes_accessed=4 * width * features, transcendentals=0
+        ),
+        name="add_products",
+    )(arrived, same, partner, w_same, w_partner)
+
+
+def hidden_kernel(keys, values, at, arrived, same, partner, w_same, w_partner, w_pair, hidden, own, other):
     rows = arrived.shape[0]
     block = arrived[...]
-    upper = (same[...] + product(reversed_rows(block), w_partner[...])).astype(BF16)
-    lower = (product(block, w_same[...]) + partner[...]).astype(BF16)
+    depth = pl.ds(at, block.shape[1])
+    upper = (same[...] + product(reversed_rows(block), w_partner[depth, :])).astype(BF16)
+    lower = (partner[...] + product(block, w_same[depth, :])).astype(BF16)
     hidden[:rows, :] = upper
     hidden[rows:, :] = lower
     both = jnp.concatenate([upper, lower], 0)
     result = product(both, w_pair[...]).astype(BF16)
-    for pair, at in ((own, 0), (other, rows)):
-        pair[:rows, :] = result[at : at + rows, :keys]
-        pack(pair, result[at : at + rows, keys : keys + values], rows, keys)
-
-
-def hidden_and_pairs(arrived, same, partner, w_same, w_partner, w_pair, keys, values):
+    for pair, first in ((own, 0), (other, rows)):
+        pair[:rows, :] = result[first : first + rows, :keys]
+        pack(pair, result[first : first + rows, keys : keys + values], rows, keys)
+
+
+def hidden_and_pairs(at, arrived, same, partner, w_same, w_partner, w_pair, keys, values):
     rows, width = arrived.shape
+    features = w_same.shape[1]
     pair = jax.ShapeDtypeStruct((rows * (keys + values) // keys, keys), BF16)
     return pl.pallas_call(
-        functools.partial(hidden_kernel, keys, values),
+        functools.partial(hidden_kernel, keys, values, at),
         in_specs=[whole()] * 6,
         out_specs=[whole()] * 3,
-        out_shape=[jax.ShapeDtypeStruct((2 * rows, width), BF16), pair, pair],
+        out_shape=[jax.ShapeDtypeStruct((2 * rows, features), BF16), pair, pair],
         compiler_params=pltpu.CompilerParams(vmem_limit_bytes=20 << 20),
         cost_estimate=pl.CostEstimate(
-            flops=4 * rows * width * (width + keys + values),
-            bytes_accessed=4 * width * width,
+            flops=4 * rows * (width * features + features * (keys + values)),
+            bytes_accessed=4 * width * features,
             transcendentals=0,
         ),
         name="hidden_and_pairs",
@@ -148,13 +174,16 @@
 
 
 def attend_kernel(shape, *refs):
-    n_query, blocks, has_state, last, heads, group, keys, values = shape
+    n_query, blocks, has_state, last, carried, heads, group, keys, values = shape
     refs = list(refs)
     queries = [refs.pop(0) for _ in range(n_query)]
     pairs = [refs.pop(0) for _ in blocks]
     states = [(refs.pop(0), refs.pop(0)) for _ in range(n_query if has_state else 0)]
     if last:
-        w_out, out = refs.pop(0), refs.pop(0)
+        w_out = refs.pop(0)
+        if carried:
+            refs.pop(0)
+        out = refs.pop(0)
     else:
         new_sum, new_peak = refs.pop(0), refs.pop(0)
     held, extended, scores = refs.pop(0), refs.pop(0), refs.pop(0)
@@ -173,14 +202,14 @@
             extended[seen : seen + block, :values] = value
             seen += block
     extended[:, values:] = jnp.ones((seen, padded - values), BF16)
-    step = 512 if seen % 512 == 0 else 256
+    steps = [(at, min(512, seen - at)) for at in range(0, seen, 512)]
 
     def score(index, unit, slot):
         wide = group * keys
         columns = queries[index][:, unit * wide : (unit + 1) * wide]
         stacked = jnp.concatenate([columns[:, i * keys : (i + 1) * keys] for i in range(group)], 0)
         peak = None
-        for at in range(0, seen, step):
+        for at, step in steps:
             block = lax.dot_general(
                 stacked, held[at : at + step, :], CONTRACT_LAST, preferred_element_type=F32
             )
@@ -195,7 +224,7 @@
 
     def mix(index, unit, slot, peak):
         total = None
-        for at in range(0, seen, step):
+        for at, step in steps:
             weights = jnp.exp2((scores[slot, :, at : at + step] - peak) * scale).astype(BF16)
             part = jnp.dot(weights, extended[at : at + step, :], preferred_element_type=F32)
             total = part if total is None else total + part
@@ -222,7 +251,7 @@
         out[...] = product(mixed[...], w_out[...]).astype(BF16)
 
 
-def attend(queries, pairs, block, keys, values, states=None, w_out=None, weight=1.0):
+def attend(queries, pairs, block, keys, values, states=None, w_out=None, place=None, carried=None, weight=1.0):
     rows = queries[0].shape[0]
     heads = queries[0].shape[1] // keys
     group = 2
@@ -231,17 +260,25 @@
     seen = sum(pair.shape[0] for pair in pairs) * keys // (keys + values)
     padded = (values // 128 + 1) * 128
     last = w_out is not None
-    shape = (len(queries), [block] * len(pairs), states is not None, last, heads, group, keys, values)
+    shape = (len(queries), [block] * len(pairs), states is not None, last, carried is not None, heads, group, keys, values)
     arguments = list(queries) + list(pairs) + [part for state in states or () for part in state]
     scratch = [
         pltpu.VMEM((seen, keys), BF16),
         pltpu.VMEM((seen, padded), BF16),
         pltpu.VMEM((2, group * rows, seen), F32),
     ]
-    if last:
+    in_specs = [whole()] * len(arguments)
+    aliases = {}
+    if last:
+        index, count = place
         arguments.append(w_out)
-        out_shape = jax.ShapeDtypeStruct((rows * len(queries), w_out.shape[1]), BF16)
-        out_specs = whole()
+        in_specs.append(whole())
+        if carried is not None:
+            aliases = {len(arguments): 0}
+            arguments.append(carried)
+            in_specs.append(whole(pl.ANY))
+        out_shape = jax.ShapeDtypeStruct((rows * len(queries) * count, w_out.shape[1]), BF16)
+        out_specs = pl.BlockSpec((rows * len(queries), w_out.shape[1]), lambda i: (index, 0))
         scratch.append(pltpu.VMEM((rows * len(queries), heads * values), BF16))
     else:
         out_shape = [
@@ -254,10 +291,12 @@
         flops += 2 * len(queries) * rows * heads * values * w_out.shape[1]
     return pl.pallas_call(
         functools.partial(attend_kernel, shape),
-        in_specs=[whole()] * len(arguments),
+        grid=(1,),
+        in_specs=in_specs,
         out_specs=out_specs,
         out_shape=out_shape,
         scratch_shapes=scratch,
+        input_output_aliases=aliases,
         compiler_params=pltpu.CompilerParams(vmem_limit_bytes=28 << 20),
         cost_estimate=pl.CostEstimate(
             flops=flops,
@@ -268,19 +307,33 @@
     )(*arguments)
 
 
-def to_both_cores(parts):
+def other_core(value):
     count = lax.axis_size("seq")
-    return parts + [lax.ppermute(part, "seq", [(s, s ^ 1) for s in range(count)]) for part in parts]
+    return lax.ppermute(value, "seq", [(s, s ^ 1) for s in range(count)])
+
+
+def after(value, *others):
+    return lax.optimization_barrier((value, *others))[0]
 
 
 def crossed(value, lane_bit, place_bits):
     lanes, count = lax.axis_size("ws"), lax.axis_size("seq")
+    bits = place_bits if isinstance(place_bits, tuple) else (place_bits, place_bits)
     pairs = [
-        (w * count + s, (w ^ lane_bit) * count + (s ^ place_bits))
+        (w * count + s, (w ^ lane_bit) * count + (s ^ bits[s % 2]))
         for w in range(lanes)
         for s in range(count)
     ]
     return lax.ppermute(value, ("ws", "seq"), pairs)
+
+
+def spread(block, twin):
+    places = list(range(2, lax.axis_size("seq"), 2))
+    whole_chip = jnp.concatenate([block, twin], 0)
+    single = crossed(block, 0, places[-1])
+    return [single] + [
+        crossed(whole_chip, 0, (places[i], places[i + 1])) for i in range(0, len(places) - 1, 2)
+    ]
 
 
 def body(tokens, w_same, w_partner, w_query, w_key, w_value, w_out):
@@ -288,24 +341,31 @@
     local = tokens[0]
     half = local.shape[0] // 2
     keys, values = w_key.shape[1], w_value.shape[1]
-    arrived = crossed(local[half:], 1, count - 1)
+    width = local.shape[1]
+    sizes = [width * part // sum(COLUMNS) for part in COLUMNS]
+    spans = [(sum(sizes[:i]), size) for i, size in enumerate(sizes)]
+    arrived = [crossed(piece, 1, count - 1) for piece in [local[half:, at : at + size] for at, size in spans]]
     same, partner, w_pair = own_products(local, w_same, w_partner, w_key, w_value.T, half)
+    for (at, _), piece in zip(spans[:-1], arrived[:-1]):
+        same, partner = add_products(at, piece, same, partner, w_same, w_partner)
     hidden, own, other = hidden_and_pairs(
-        arrived, same, partner, w_same, w_partner, w_pair, keys, values
+        spans[-1][0], arrived[-1], same, partner, w_same, w_partner, w_pair, keys, values
     )
-    near = [own] + [crossed(own, 0, k) for k in range(2, count, 2)]
+    places = range(2, count, 2)
+    near = [own] + [crossed(own, 0, k) for k in places]
     lifted = crossed(other, 1, 0)
     query, sent = query_rows(hidden, w_query, [half, half])
     near, lifted, query = lax.optimization_barrier((near, lifted, query))
-    near = to_both_cores(near)
+    high = other_core(lifted)
+    early = near + [other_core(part) for part in near] + [lifted, high]
     brought = crossed(sent, 1, count - 1)
-    mine = attend([query], near, half, keys, values, weight=1.7)
-    brought, mine = lax.optimization_barrier((brought, mine))
-    far = [lifted] + [crossed(lifted, 0, k) for k in range(2, count, 2)]
-    theirs = attend([brought], near, half, keys, values, weight=0.1)
-    far, theirs = lax.optimization_barrier((far, theirs))
-    far = to_both_cores(far)
-    result = attend([query, brought], far, half, keys, values, [mine, theirs], w_out)
+    mine = attend([query], early, half, keys, values, weight=0.7)
+    brought = after(brought, mine)
+    far = spread(lifted, high)
+    theirs = attend([brought], early, half, keys, values, weight=1.0)
+    far = after(far, theirs)
+    late = far + [other_core(part) for part in far]
+    result = attend([query, brought], late, half, keys, values, [mine, theirs], w_out, (0, 1))
     return result[None]
 
 

time: 59.4 us -> 56.9 us (0.958)
  waiting for transfers between devices: 12 us -> 6.13 us
  local copies, waits for them, and re-layouts: 7.95 us -> 10.4 us
  Pallas kernels: 22.2 us -> 23.8 us
  starting transfers between devices: 16.9 us -> 16.1 us
    ppermute x9, waiting for transfers between devices: 10.7 us -> 4.63 us  [crossed(): return lax.ppermute(value, ('ws', 'seq'), pairs)]
    unnamed x20, local copies, waits for them, and re-layouts: 6.75 us -> 8.35 us
    pallas_call x4 -> x5, Pallas kernels: 18.7 us -> 20.2 us  [the longest x3 17.2 us: attend(): pl.pallas_call(functools.partial(attend_kernel, shape), grid=(1,), in_spe...]
    slice x1 -> x2, local copies, waits for them, and re-layouts: 1.2 us -> 2.06 us  [body(): local[half:, at:at + size]]
    ppermute x8 -> x7, starting transfers between devices: 2.04 us -> 1.68 us  [other_core(): return lax.ppermute(value, 'seq', [(s, s ^ 1) for s in range(count)])]
    ppermute x8 -> x7, waiting for transfers between devices: 1.32 us -> 1.5 us  [other_core(): return lax.ppermute(value, 'seq', [(s, s ^ 1) for s in range(count)])]
  transfers between devices with their start and end apart: 17 -> 16, of which waited for: 12 -> 8; matrix products, arithmetic and copies ran while one was open for 0% -> 2% of each run, Pallas kernels for 16% -> 24%
where the time goes in v3:
time: 56.9 us; the launch traced here: 56.5 us
  Pallas kernels  23.8 us (42%)
  starting transfers between devices  16.1 us (28%)
  local copies, waits for them, and re-layouts  10.4 us (18%)
  waiting for transfers between devices  6.13 us (11%)
    pallas_call x3, Pallas kernels, attend(): pl.pallas_call(functools.partial(attend_kernel, shape), grid=(1,), in_spe...  17.2 us
    ppermute x9, starting transfers between devices, crossed(): return lax.ppermute(value, ('ws', 'seq'), pairs)  14.4 us
    unnamed x20, local copies, waits for them, and re-layouts  8.35 us
    ppermute x9, waiting for transfers between devices, crossed(): return lax.ppermute(value, ('ws', 'seq'), pairs)  4.63 us
    pallas_call x1, Pallas kernels, own_products(): pl.pallas_call(own_kernel, in_specs=[whole()] * 5, out_specs=[whole()] *...  2.15 us
    slice x2, local copies, waits for them, and re-layouts, body(): local[half:, at:at + size]  2.06 us
    ppermute x7, starting transfers between devices, other_core(): return lax.ppermute(value, 'seq', [(s, s ^ 1) for s in range(count)])  1.68 us
    pallas_call x1, Pallas kernels, hidden_and_pairs(): pl.pallas_call(functools.partial(hidden_kernel, keys, values, at), in_spe...  1.58 us
  transfers between devices with their start and end apart: 16, of which 8 were waited for; matrix products, arithmetic and copies ran while one was open for 2% of the time, Pallas kernels for 24%

profile of v3, /device:TPU:0, one launch (start us, length us, event | category | flops | bytes accessed | tf_op | source)
XLA Modules:
  0.0 56.5 jit_solution(3159910023498873332)
XLA Ops:
  0.0 1.1 %slice.9 = bf16[192,1024]{1,0:T(8,128)(2,1)S(1)} slice(bf16[384,1536]{1,0:T(8,128)(2,1)} %bitcast.3), slice={[192:384], [0:1024]} | slice | bytes 786432 | tf_op jit(solution)/shard_map/slice | solution.py:347
  1.1 4.4 %collective-permute-start.1 = (bf16[192,1024]{1,0:T(8,128)(2,1)S(1)}, bf16[192,1024]{1,0:T(8,128)(2,1)S(1)}, u32[]{:S(2)}, u32[]{:S(2)}) collective-permute-start(bf16[192,1024]{1,0:T(8,128)(2,1)S(1)} %slice.9), channel_id=1, source_target_pairs={{0,15},{1,14},{2,13},{3,12},{4,11},{5,10},{6,9},{7,8},{8,7},{9,6},... | collective-permute-start | bytes 1179656 | tf_op jit(solution)/shard_map/ppermute | solution.py:327
  5.5 0.9 %slice.8 = bf16[192,512]{1,0:T(8,128)(2,1)S(1)} slice(bf16[384,1536]{1,0:T(8,128)(2,1)} %bitcast.4), slice={[192:384], [1024:1536]} | slice | bytes 393216 | tf_op jit(solution)/shard_map/slice | solution.py:347
  6.6 2.3 %copy-done = bf16[1536,1536]{1,0:T(8,128)(2,1)S(1)} copy-done((bf16[1536,1536]{1,0:T(8,128)(2,1)S(1)}, bf16[1536,1536]{1,0:T(8,128)(2,1)}, u32[]{:S(2)}) %copy-start) | copy-done | bytes 4718616
  8.9 2.3 %copy-done.2 = bf16[1536,1536]{1,0:T(8,128)(2,1)S(1)} copy-done((bf16[1536,1536]{1,0:T(8,128)(2,1)S(1)}, bf16[1536,1536]{1,0:T(8,128)(2,1)}, u32[]{:S(2)}) %copy-start.2) | copy-done | bytes 4718616
  11.2 1.1 %copy-done.5 = bf16[1536,192]{0,1:T(8,128)(2,1)S(1)} copy-done((bf16[1536,192]{0,1:T(8,128)(2,1)S(1)}, bf16[1536,192]{0,1:T(8,128)(2,1)}, u32[]{:S(2)}) %copy-start.5) | copy-done | bytes 589848
  12.3 1.0 %copy-done.6 = bf16[1536,128]{1,0:T(8,128)(2,1)S(1)} copy-done((bf16[1536,128]{1,0:T(8,128)(2,1)S(1)}, bf16[1536,128]{1,0:T(8,128)(2,1)}, u32[]{:S(2)}) %copy-start.6) | copy-done | bytes 393240
  13.3 2.2 %own_products.1 = (f32[192,1536]{1,0:T(8,128)S(1)}, f32[192,1536]{1,0:T(8,128)S(1)}, bf16[1536,384]{1,0:T(8,128)(2,1)S(1)}) custom-call(bf16[384,1536]{1,0:T(8,128)(2,1)S(1)} %bitcast.5, bf16[1536,1536]{1,0:T(8,128)(2,1)S(1)} %copy-done, bf16[1536,1536]{1,0:T(8,128)(2,1)S(1)} %copy-done.2, bf16[1536,128]{1,0:T(8,128)(2,1)S(1)} %copy-done.6, ...), custom_call_target="tpu_custom_call" | custom-call | flops 1811939328 | bytes 9437184 | tf_op jit(solution)/shard_map/own_products/pallas_call | solution.py:49
  15.6 1.4 %copy-done.3 = bf16[1536,1536]{1,0:T(8,128)(2,1)S(1)} copy-done((bf16[1536,1536]{1,0:T(8,128)(2,1)S(1)}, bf16[1536,1536]{1,0:T(8,128)(2,1)}, u32[]{:S(2)}) %copy-start.3) | copy-done | bytes 4718616
  17.1 1.5 %add_products.1 = (f32[192,1536]{1,0:T(8,128)S(1)}, f32[192,1536]{1,0:T(8,128)S(1)}) custom-call(bf16[192,1024]{1,0:T(8,128)(2,1)S(1)} %collective-permute-done.1.arrived, f32[192,1536]{1,0:T(8,128)S(1)} %get-tuple-element.28.same, f32[192,1536]{1,0:T(8,128)S(1)} %get-tuple-element.29.partner, bf16[1536,1536]{1,0:T(8,128)(2,1)S(1)} %copy-done.1, ...), custom_call_target="tpu_custom_call" | custom-call | flops 1207959552 | bytes 6291456 | tf_op jit(solution)/shard_map/add_products/pallas_call | solution.py:104
  19.3 1.6 %hidden_and_pairs.1 = (bf16[384,1536]{1,0:T(8,128)(2,1)S(1)}, bf16[480,128]{1,0:T(8,128)(2,1)S(1)}, bf16[480,128]{1,0:T(8,128)(2,1)S(1)}) custom-call(bf16[192,512]{1,0:T(8,128)(2,1)S(1)} %collective-permute-done.arrived, f32[192,1536]{1,0:T(8,128)S(1)} %get-tuple-element.30.same, f32[192,1536]{1,0:T(8,128)S(1)} %get-tuple-element.31.partner, ...), custom_call_target="tpu_custom_call" | custom-call | flops 981467136 | bytes 3145728 | tf_op jit(solution)/shard_map/hidden_and_pairs/pallas_call | solution.py:136
  20.8 3.3 %collective-permute-start.4 = (bf16[480,128]{1,0:T(8,128)(2,1)S(1)}, bf16[480,128]{1,0:T(8,128)(2,1)S(1)}, u32[]{:S(2)}, u32[]{:S(2)}) collective-permute-start(bf16[480,128]{1,0:T(8,128)(2,1)S(1)} %get-tuple-element.39.refs_1_), channel_id=1, source_target_pairs={{0,6},{1,7},{2,4},{3,5},{4,2},{5,3},{6,0},{7,1},{8,14},{9,15},{10,... | collective-permute-start | bytes 368648 | tf_op jit(solution)/shard_map/ppermute | solution.py:327
  24.8 2.0 %collective-permute-start.5 = (bf16[480,128]{1,0:T(8,128)(2,1)S(1)}, bf16[480,128]{1,0:T(8,128)(2,1)S(1)}, u32[]{:S(2)}, u32[]{:S(2)}) collective-permute-start(bf16[480,128]{1,0:T(8,128)(2,1)S(1)} %get-tuple-element.34), channel_id=1, source_target_pairs={{0,8},{1,9},{2,10},{3,11},{4,12},{5,13},{6,14},{7,15},{8,0},{9,1},... | collective-permute-start | bytes 368648 | tf_op jit(solution)/shard_map/ppermute | solution.py:327
  26.8 1.4 %query_rows.1 = (bf16[192,1024]{1,0:T(8,128)(2,1)S(1)}, bf16[192,1024]{1,0:T(8,128)(2,1)S(1)}) custom-call(bf16[384,1536]{1,0:T(8,128)(2,1)S(1)} %get-tuple-element.35.hidden, bf16[1536,1024]{1,0:T(8,128)(2,1)S(1)} %copy-done.7), custom_call_target="tpu_custom_call" | custom-call | flops 1207959552 | bytes 3145728 | tf_op jit(solution)/shard_map/query_rows/pallas_call | solution.py:161
  28.2 1.0 %collective-permute-start.6 = (bf16[192,1024]{1,0:T(8,128)(2,1)S(1)}, bf16[192,1024]{1,0:T(8,128)(2,1)S(1)}, u32[]{:S(2)}, u32[]{:S(2)}) collective-permute-start(bf16[192,1024]{1,0:T(8,128)(2,1)S(1)} %get-tuple-element.38), channel_id=1, source_target_pairs={{0,15},{1,14},{2,13},{3,12},{4,11},{5,10},{6,9},{7,8},{8,7},{9,6},... | collective-permute-start | bytes 1179656 | tf_op jit(solution)/shard_map/ppermute | solution.py:327
  29.7 0.7 %collective-permute-done.3.refs_3_ = bf16[480,128]{1,0:T(8,128)(2,1)S(1)} collective-permute-done((bf16[480,128]{1,0:T(8,128)(2,1)S(1)}, bf16[480,128]{1,0:T(8,128)(2,1)S(1)}, u32[]{:S(2)}, u32[]{:S(2)}) %collective-permute-start.3) | collective-permute-done | bytes 122912 | tf_op jit(solution)/shard_map/ppermute | solution.py:327
  32.2 2.0 %collective-permute-start.12 = (bf16[480,128]{1,0:T(8,128)(2,1)S(1)}, bf16[480,128]{1,0:T(8,128)(2,1)S(1)}, u32[]{:S(2)}, u32[]{:S(2)}) collective-permute-start(bf16[480,128]{1,0:T(8,128)(2,1)S(1)} %collective-permute-done.5.refs_9_), channel_id=1, source_target_pairs={{0,6},{1,7},{2,4},{3,5},{4,2},{5,3},{6,0},{7,1},{8,14},{9,15},{10,... | collective-permute-start | bytes 368648 | tf_op jit(solution)/shard_map/ppermute | solution.py:327
  34.2 1.0 %collective-permute-start.13 = (bf16[960,128]{1,0:T(8,128)(2,1)S(1)}, bf16[960,128]{1,0:T(8,128)(2,1)S(1)}, u32[]{:S(2)}, u32[]{:S(2)}) collective-permute-start(bf16[960,128]{1,0:T(8,128)(2,1)S(1)} %pad_maximum_fusion), channel_id=1, source_target_pairs={{0,2},{1,5},{2,0},{3,7},{4,6},{5,1},{6,4},{7,3},{8,10},{9,13},{10,... | collective-permute-start | bytes 737288 | tf_op jit(solution)/shard_map/ppermute | solution.py:327
  35.2 4.1 %attend.3 = (f32[4,384,256]{2,1,0:T(8,128)S(1)}, f32[4,384,128]{2,1,0:T(8,128)S(1)}) custom-call(bf16[192,1024]{1,0:T(8,128)(2,1)S(1)} %get-tuple-element.37.refs_0_, bf16[480,128]{1,0:T(8,128)(2,1)S(1)} %get-tuple-element.39.refs_1_, bf16[480,128]{1,0:T(8,128)(2,1)S(1)} %collective-permute-done.2.refs_2_, ...), custom_call_target="tpu_custom_call" | custom-call | flops 1321205760 | bytes 1228800 | tf_op jit(solution)/shard_map/attend/pallas_call | solution.py:292
  39.3 1.5 %collective-permute-done.6.refs_0_.refs_1_ = bf16[192,1024]{1,0:T(8,128)(2,1)S(1)} collective-permute-done((bf16[192,1024]{1,0:T(8,128)(2,1)S(1)}, bf16[192,1024]{1,0:T(8,128)(2,1)S(1)}, u32[]{:S(2)}, u32[]{:S(2)}) %collective-permute-start.6) | collective-permute-done | bytes 393248 | tf_op jit(solution)/shard_map/ppermute | solution.py:327
  40.8 4.1 %attend.4 = (f32[4,384,256]{2,1,0:T(8,128)S(1)}, f32[4,384,128]{2,1,0:T(8,128)S(1)}) custom-call(bf16[192,1024]{1,0:T(8,128)(2,1)S(1)} %collective-permute-done.6.refs_0_.refs_1_, bf16[480,128]{1,0:T(8,128)(2,1)S(1)} %get-tuple-element.39.refs_1_, bf16[480,128]{1,0:T(8,128)(2,1)S(1)} %collective-permute-done.2.refs_2_, ...), custom_call_target="tpu_custom_call" | custom-call | flops 1887436800 | bytes 1228800 | tf_op jit(solution)/shard_map/attend/pallas_call | solution.py:292
  45.0 1.0 %collective-permute-done.13.refs_3_ = bf16[960,128]{1,0:T(8,128)(2,1)S(1)} collective-permute-done((bf16[960,128]{1,0:T(8,128)(2,1)S(1)}, bf16[960,128]{1,0:T(8,128)(2,1)S(1)}, u32[]{:S(2)}, u32[]{:S(2)}) %collective-permute-start.13) | collective-permute-done | bytes 245792 | tf_op jit(solution)/shard_map/ppermute | solution.py:327
  46.5 1.2 %collective-permute-done.14.refs_4_ = bf16[480,128]{1,0:T(8,128)(2,1)S(1)} collective-permute-done((bf16[480,128]{1,0:T(8,128)(2,1)S(1)}, bf16[480,128]{1,0:T(8,128)(2,1)S(1)}, u32[]{:S(2)}, u32[]{:S(2)}) %collective-permute-start.14) | collective-permute-done | bytes 122912 | tf_op jit(solution)/shard_map/ppermute | solution.py:312
  47.7 8.9 %attend.5 = bf16[384,1536]{1,0:T(8,128)(2,1)} custom-call(bf16[192,1024]{1,0:T(8,128)(2,1)S(1)} %get-tuple-element.37.refs_0_, bf16[192,1024]{1,0:T(8,128)(2,1)S(1)} %collective-permute-done.6.refs_0_.refs_1_, bf16[480,128]{1,0:T(8,128)(2,1)S(1)} %collective-permute-done.12.refs_2_, bf16[960,128]{1,0:T(8,128)(2,1)S(1)} %collective-permute-done.13.refs_3_, ...), custom_call_target="tpu_custom_call" | custom-call | flops 4076863488 | bytes 737280 | tf_op jit(solution)/shard_map/attend/pallas_call | solution.py:292
  (39 shorter events, 4.4 us)
Async XLA Ops:
  0.0 6.6 %copy-start.4 = (bf16[1,384,1536]{2,1,0:T(8,128)(2,1)S(1)}, bf16[1,384,1536]{2,1,0:T(8,128)(2,1)}, u32[]{:S(2)}) copy-start(bf16[1,384,1536]{2,1,0:T(8,128)(2,1)} %param.7) | copy-start | bytes 3538948
  1.1 14.3 %collective-permute-start.1 = (bf16[192,1024]{1,0:T(8,128)(2,1)S(1)}, bf16[192,1024]{1,0:T(8,128)(2,1)S(1)}, u32[]{:S(2)}, u32[]{:S(2)}) collective-permute-start(bf16[192,1024]{1,0:T(8,128)(2,1)S(1)} %slice.9), channel_id=1, source_target_pairs={{0,15},{1,14},{2,13},{3,12},{4,11},{5,10},{6,9},{7,8},{8,7},{9,6},... | collective-permute-start | bytes 1179656 | tf_op jit(solution)/shard_map/ppermute | solution.py:327
  6.5 12.8 %collective-permute-start = (bf16[192,512]{1,0:T(8,128)(2,1)S(1)}, bf16[192,512]{1,0:T(8,128)(2,1)S(1)}, u32[]{:S(2)}, u32[]{:S(2)}) collective-permute-start(bf16[192,512]{1,0:T(8,128)(2,1)S(1)} %slice.8), channel_id=1, source_target_pairs={{0,15},{1,14},{2,13},{3,12},{4,11},{5,10},{6,9},{7,8},{8,7},{9,6},... | collective-permute-start | bytes 589832 | tf_op jit(solution)/shard_map/ppermute | solution.py:327
  6.6 2.3 %copy-start = (bf16[1536,1536]{1,0:T(8,128)(2,1)S(1)}, bf16[1536,1536]{1,0:T(8,128)(2,1)}, u32[]{:S(2)}) copy-start(bf16[1536,1536]{1,0:T(8,128)(2,1)} %w_same.5) | copy-start | bytes 14155780
  8.9 2.3 %copy-start.2 = (bf16[1536,1536]{1,0:T(8,128)(2,1)S(1)}, bf16[1536,1536]{1,0:T(8,128)(2,1)}, u32[]{:S(2)}) copy-start(bf16[1536,1536]{1,0:T(8,128)(2,1)} %w_partner.5) | copy-start | bytes 14155780
  13.3 2.3 %copy-start.1 = (bf16[1536,1536]{1,0:T(8,128)(2,1)S(1)}, bf16[1536,1536]{1,0:T(8,128)(2,1)}, u32[]{:S(2)}) copy-start(bf16[1536,1536]{1,0:T(8,128)(2,1)} %w_same.5) | copy-start | bytes 14155780
  13.3 3.8 %copy-start.3 = (bf16[1536,1536]{1,0:T(8,128)(2,1)S(1)}, bf16[1536,1536]{1,0:T(8,128)(2,1)}, u32[]{:S(2)}) copy-start(bf16[1536,1536]{1,0:T(8,128)(2,1)} %w_partner.5) | copy-start | bytes 14155780
  19.3 7.5 %copy-start.7 = (bf16[1536,1024]{1,0:T(8,128)(2,1)S(1)}, bf16[1536,1024]{1,0:T(8,128)(2,1)}, u32[]{:S(2)}) copy-start(bf16[1536,1024]{1,0:T(8,128)(2,1)} %w_query.1) | copy-start | bytes 9437188
  20.8 8.8 %collective-permute-start.4 = (bf16[480,128]{1,0:T(8,128)(2,1)S(1)}, bf16[480,128]{1,0:T(8,128)(2,1)S(1)}, u32[]{:S(2)}, u32[]{:S(2)}) collective-permute-start(bf16[480,128]{1,0:T(8,128)(2,1)S(1)} %get-tuple-element.39.refs_1_), channel_id=1, source_target_pairs={{0,6},{1,7},{2,4},{3,5},{4,2},{5,3},{6,0},{7,1},{8,14},{9,15},{10,... | collective-permute-start | bytes 368648 | tf_op jit(solution)/shard_map/ppermute | solution.py:327
  24.1 6.2 %collective-permute-start.3 = (bf16[480,128]{1,0:T(8,128)(2,1)S(1)}, bf16[480,128]{1,0:T(8,128)(2,1)S(1)}, u32[]{:S(2)}, u32[]{:S(2)}) collective-permute-start(bf16[480,128]{1,0:T(8,128)(2,1)S(1)} %get-tuple-element.39.refs_1_), channel_id=1, source_target_pairs={{0,4},{1,5},{2,6},{3,7},{4,0},{5,1},{6,2},{7,3},{8,12},{9,13},{10,... | collective-permute-start | bytes 368648 | tf_op jit(solution)/shard_map/ppermute | solution.py:327
  24.6 6.0 %collective-permute-start.2 = (bf16[480,128]{1,0:T(8,128)(2,1)S(1)}, bf16[480,128]{1,0:T(8,128)(2,1)S(1)}, u32[]{:S(2)}, u32[]{:S(2)}) collective-permute-start(bf16[480,128]{1,0:T(8,128)(2,1)S(1)} %get-tuple-element.39.refs_1_), channel_id=1, source_target_pairs={{0,2},{1,3},{2,0},{3,1},{4,6},{5,7},{6,4},{7,5},{8,10},{9,11},{10,... | collective-permute-start | bytes 368648 | tf_op jit(solution)/shard_map/ppermute | solution.py:327
  24.8 4.9 %collective-permute-start.5 = (bf16[480,128]{1,0:T(8,128)(2,1)S(1)}, bf16[480,128]{1,0:T(8,128)(2,1)S(1)}, u32[]{:S(2)}, u32[]{:S(2)}) collective-permute-start(bf16[480,128]{1,0:T(8,128)(2,1)S(1)} %get-tuple-element.34), channel_id=1, source_target_pairs={{0,8},{1,9},{2,10},{3,11},{4,12},{5,13},{6,14},{7,15},{8,0},{9,1},... | collective-permute-start | bytes 368648 | tf_op jit(solution)/shard_map/ppermute | solution.py:327
  26.8 20.9 %slice-start = ((s8[4718592]{0:T(1024)(128)(4,1)}), s8[4194304]{0:T(1024)(128)(4,1)S(1)}, s32[]{:S(2)}) async-start(s8[4718592]{0:T(1024)(128)(4,1)} %bitcast.7), calls=%async_computation | async-start | bytes 8388608
  28.2 12.7 %collective-permute-start.6 = (bf16[192,1024]{1,0:T(8,128)(2,1)S(1)}, bf16[192,1024]{1,0:T(8,128)(2,1)S(1)}, u32[]{:S(2)}, u32[]{:S(2)}) collective-permute-start(bf16[192,1024]{1,0:T(8,128)(2,1)S(1)} %get-tuple-element.38), channel_id=1, source_target_pairs={{0,15},{1,14},{2,13},{3,12},{4,11},{5,10},{6,9},{7,8},{8,7},{9,6},... | collective-permute-start | bytes 1179656 | tf_op jit(solution)/shard_map/ppermute | solution.py:327
  30.6 1.3 %collective-permute-start.11 = (bf16[480,128]{1,0:T(8,128)(2,1)S(1)}, bf16[480,128]{1,0:T(8,128)(2,1)S(1)}, u32[]{:S(2)}, u32[]{:S(2)}) collective-permute-start(bf16[480,128]{1,0:T(8,128)(2,1)S(1)} %collective-permute-done.5.refs_9_), channel_id=1, source_target_pairs={{0,1},{1,0},{2,3},{3,2},{4,5},{5,4},{6,7},{7,6},{8,9},{9,8},{10,11... | collective-permute-start | bytes 368648 | tf_op jit(solution)/shard_map/ppermute | solution.py:312
  30.8 1.4 %collective-permute-start.7 = (bf16[480,128]{1,0:T(8,128)(2,1)S(1)}, bf16[480,128]{1,0:T(8,128)(2,1)S(1)}, u32[]{:S(2)}, u32[]{:S(2)}) collective-permute-start(bf16[480,128]{1,0:T(8,128)(2,1)S(1)} %get-tuple-element.39.refs_1_), channel_id=1, source_target_pairs={{0,1},{1,0},{2,3},{3,2},{4,5},{5,4},{6,7},{7,6},{8,9},{9,8},{10,11... | collective-permute-start | bytes 368648 | tf_op jit(solution)/shard_map/ppermute | solution.py:312
  31.1 3.1 %collective-permute-start.8 = (bf16[480,128]{1,0:T(8,128)(2,1)S(1)}, bf16[480,128]{1,0:T(8,128)(2,1)S(1)}, u32[]{:S(2)}, u32[]{:S(2)}) collective-permute-start(bf16[480,128]{1,0:T(8,128)(2,1)S(1)} %collective-permute-done.2.refs_2_), channel_id=1, source_target_pairs={{0,1},{1,0},{2,3},{3,2},{4,5},{5,4},{6,7},{7,6},{8,9},{9,8},{10,11... | collective-permute-start | bytes 368648 | tf_op jit(solution)/shard_map/ppermute | solution.py:312
  31.3 3.9 %collective-permute-start.9 = (bf16[480,128]{1,0:T(8,128)(2,1)S(1)}, bf16[480,128]{1,0:T(8,128)(2,1)S(1)}, u32[]{:S(2)}, u32[]{:S(2)}) collective-permute-start(bf16[480,128]{1,0:T(8,128)(2,1)S(1)} %collective-permute-done.3.refs_3_), channel_id=1, source_target_pairs={{0,1},{1,0},{2,3},{3,2},{4,5},{5,4},{6,7},{7,6},{8,9},{9,8},{10,11... | collective-permute-start | bytes 368648 | tf_op jit(solution)/shard_map/ppermute | solution.py:312
  32.0 3.2 %collective-permute-start.10 = (bf16[480,128]{1,0:T(8,128)(2,1)S(1)}, bf16[480,128]{1,0:T(8,128)(2,1)S(1)}, u32[]{:S(2)}, u32[]{:S(2)}) collective-permute-start(bf16[480,128]{1,0:T(8,128)(2,1)S(1)} %collective-permute-done.4.refs_4_), channel_id=1, source_target_pairs={{0,1},{1,0},{2,3},{3,2},{4,5},{5,4},{6,7},{7,6},{8,9},{9,8},{10,11... | collective-permute-start | bytes 368648 | tf_op jit(solution)/shard_map/ppermute | solution.py:312
  32.1 15.5 %slice-start.1 = ((s8[4718592]{0:T(1024)(128)(4,1)}), s8[524288]{0:T(1024)(128)(4,1)S(1)}, s32[]{:S(2)}) async-start(s8[4718592]{0:T(1024)(128)(4,1)} %bitcast.7), calls=%async_computation.1 | async-start | bytes 1048576
  32.2 12.8 %collective-permute-start.12 = (bf16[480,128]{1,0:T(8,128)(2,1)S(1)}, bf16[480,128]{1,0:T(8,128)(2,1)S(1)}, u32[]{:S(2)}, u32[]{:S(2)}) collective-permute-start(bf16[480,128]{1,0:T(8,128)(2,1)S(1)} %collective-permute-done.5.refs_9_), channel_id=1, source_target_pairs={{0,6},{1,7},{2,4},{3,5},{4,2},{5,3},{6,0},{7,1},{8,14},{9,15},{10,... | collective-permute-start | bytes 368648 | tf_op jit(solution)/shard_map/ppermute | solution.py:327
  34.2 11.8 %collective-permute-start.13 = (bf16[960,128]{1,0:T(8,128)(2,1)S(1)}, bf16[960,128]{1,0:T(8,128)(2,1)S(1)}, u32[]{:S(2)}, u32[]{:S(2)}) collective-permute-start(bf16[960,128]{1,0:T(8,128)(2,1)S(1)} %pad_maximum_fusion), channel_id=1, source_target_pairs={{0,2},{1,5},{2,0},{3,7},{4,6},{5,1},{6,4},{7,3},{8,10},{9,13},{10,... | collective-permute-start | bytes 737288 | tf_op jit(solution)/shard_map/ppermute | solution.py:327
  46.0 1.7 %collective-permute-start.15 = (bf16[960,128]{1,0:T(8,128)(2,1)S(1)}, bf16[960,128]{1,0:T(8,128)(2,1)S(1)}, u32[]{:S(2)}, u32[]{:S(2)}) collective-permute-start(bf16[960,128]{1,0:T(8,128)(2,1)S(1)} %collective-permute-done.13.refs_3_), channel_id=1, source_target_pairs={{0,1},{1,0},{2,3},{3,2},{4,5},{5,4},{6,7},{7,6},{8,9},{9,8},{10,11... | collective-permute-start | bytes 737288 | tf_op jit(solution)/shard_map/ppermute | solution.py:312
  46.0 1.7 %collective-permute-start.14 = (bf16[480,128]{1,0:T(8,128)(2,1)S(1)}, bf16[480,128]{1,0:T(8,128)(2,1)S(1)}, u32[]{:S(2)}, u32[]{:S(2)}) collective-permute-start(bf16[480,128]{1,0:T(8,128)(2,1)S(1)} %collective-permute-done.12.refs_2_), channel_id=1, source_target_pairs={{0,1},{1,0},{2,3},{3,2},{4,5},{5,4},{6,7},{7,6},{8,9},{9,8},{10,11... | collective-permute-start | bytes 368648 | tf_op jit(solution)/shard_map/ppermute | solution.py:312
  (2 other events, 2.1 us)

commit v4 on v3

--- a/solution.py
+++ b/solution.py
@@ -12,7 +12,7 @@
 BF16 = jnp.bfloat16
 CONTRACT_LAST = (((1,), (1,)), ((), ()))
 STACKED = 384
-COLUMNS = (2, 1)
+COLUMNS = (5, 1)
 
 
 def whole(memory_space=pltpu.VMEM):
@@ -174,7 +174,7 @@
 
 
 def attend_kernel(shape, *refs):
-    n_query, blocks, has_state, last, carried, heads, group, keys, values = shape
+    n_query, blocks, lead, drop, has_state, last, carried, heads, group, keys, values = shape
     refs = list(refs)
     queries = [refs.pop(0) for _ in range(n_query)]
     pairs = [refs.pop(0) for _ in blocks]
@@ -198,10 +198,12 @@
         packed = block * (keys + values) // keys
         for at in range(0, pair.shape[0], packed):
             key, value = unpack(pair, at, block, keys, values)
-            held[seen : seen + block, :] = key
-            extended[seen : seen + block, :values] = value
-            seen += block
+            taken = lead if lead and not seen else block
+            held[seen : seen + taken, :] = key[block - taken :, :]
+            extended[seen : seen + taken, :values] = value[block - taken :, :]
+            seen += taken
     extended[:, values:] = jnp.ones((seen, padded - values), BF16)
+    seen -= drop
     steps = [(at, min(512, seen - at)) for at in range(0, seen, 512)]
 
     def score(index, unit, slot):
@@ -217,26 +219,41 @@
             for lane in range(0, step, 128):
                 part = block[:, lane : lane + 128]
                 peak = part if peak is None else jnp.maximum(peak, part)
-        peak = jnp.max(peak, axis=1, keepdims=True)
+        peak = jnp.broadcast_to(jnp.max(peak, axis=1, keepdims=True), peak.shape)
         if has_state:
-            peak = jnp.maximum(peak, states[index][1][unit][:, :1])
+            peak = jnp.maximum(peak, states[index][1][unit])
         return peak
 
     def mix(index, unit, slot, peak):
         total = None
         for at, step in steps:
-            weights = jnp.exp2((scores[slot, :, at : at + step] - peak) * scale).astype(BF16)
+            weights = jnp.concatenate(
+                [
+                    jnp.exp2((scores[slot, :, lane : lane + 128] - peak) * scale).astype(BF16)
+                    for lane in range(at, at + step, 128)
+                ],
+                1,
+            )
             part = jnp.dot(weights, extended[at : at + step, :], preferred_element_type=F32)
             total = part if total is None else total + part
         if has_state:
             old_sum, old_peak = states[index]
-            decay = jnp.exp2((old_peak[unit][:, :1] - peak) * scale)
-            total = total + old_sum[unit] * decay
+            decay = jnp.exp2((old_peak[unit] - peak) * scale)
+            total = jnp.concatenate(
+                [
+                    total[:, lane : lane + 128] + old_sum[unit, :, lane : lane + 128] * decay
+                    for lane in range(0, padded, 128)
+                ],
+                1,
+            )
         if not last:
             new_sum[unit] = total
-            new_peak[unit] = jnp.broadcast_to(peak, new_peak.shape[1:])
+            new_peak[unit] = peak
             return
-        result = (total[:, :values] / total[:, values : values + 1]).astype(BF16)
+        inverse = jnp.broadcast_to(1.0 / total[:, values : values + 1], peak.shape)
+        result = jnp.concatenate(
+            [(total[:, lane : lane + 128] * inverse).astype(BF16) for lane in range(0, padded, 128)], 1
+        )[:, :values]
         wide = group * values
         mixed[index * rows : (index + 1) * rows, unit * wide : (unit + 1) * wide] = jnp.concatenate(
             [result[i * rows : (i + 1) * rows, :] for i in range(group)], 1
@@ -251,20 +268,21 @@
         out[...] = product(mixed[...], w_out[...]).astype(BF16)
 
 
-def attend(queries, pairs, block, keys, values, states=None, w_out=None, place=None, carried=None, weight=1.0):
+def attend(queries, pairs, block, keys, values, states=None, w_out=None, place=None, carried=None, weight=1.0, lead=0, drop=0):
     rows = queries[0].shape[0]
     heads = queries[0].shape[1] // keys
     group = 2
     while group * rows < STACKED and heads % (2 * group) == 0:
         group *= 2
-    seen = sum(pair.shape[0] for pair in pairs) * keys // (keys + values)
+    room = sum(pair.shape[0] for pair in pairs) * keys // (keys + values) - (block - lead if lead else 0)
+    seen = room - drop
     padded = (values // 128 + 1) * 128
     last = w_out is not None
-    shape = (len(queries), [block] * len(pairs), states is not None, last, carried is not None, heads, group, keys, values)
+    shape = (len(queries), [block] * len(pairs), lead, drop, states is not None, last, carried is not None, heads, group, keys, values)
     arguments = list(queries) + list(pairs) + [part for state in states or () for part in state]
     scratch = [
-        pltpu.VMEM((seen, keys), BF16),
-        pltpu.VMEM((seen, padded), BF16),
+        pltpu.VMEM((room, keys), BF16),
+        pltpu.VMEM((room, padded), BF16),
         pltpu.VMEM((2, group * rows, seen), F32),
     ]
     in_specs = [whole()] * len(arguments)
@@ -359,13 +377,16 @@
     high = other_core(lifted)
     early = near + [other_core(part) for part in near] + [lifted, high]
     brought = crossed(sent, 1, count - 1)
-    mine = attend([query], early, half, keys, values, weight=0.7)
+    spare = len(early) * half % 256 if len(early) * half % 256 <= half else 0
+    mine = attend([query], early, half, keys, values, weight=0.7, drop=spare)
     brought = after(brought, mine)
     far = spread(lifted, high)
-    theirs = attend([brought], early, half, keys, values, weight=1.0)
+    theirs = attend([brought], early, half, keys, values, weight=1.0, drop=spare)
     far = after(far, theirs)
     late = far + [other_core(part) for part in far]
-    result = attend([query, brought], late, half, keys, values, [mine, theirs], w_out, (0, 1))
+    if spare:
+        late = [high] + late
+    result = attend([query, brought], late, half, keys, values, [mine, theirs], w_out, (0, 1), lead=spare)
     return result[None]
 
 

time: 56.9 us -> 55.7 us (0.979)
  waiting for transfers between devices: 6.13 us -> 8.58 us
  Pallas kernels: 23.8 us -> 21.8 us
  local copies, waits for them, and re-layouts: 10.4 us -> 8.81 us
    ppermute x9, waiting for transfers between devices: 4.63 us -> 7.08 us  [crossed(): return lax.ppermute(value, ('ws', 'seq'), pairs)]
    pallas_call x3, Pallas kernels: 17.2 us -> 15.2 us  [attend(): pl.pallas_call(functools.partial(attend_kernel, shape), grid=(1,), in_spe...]
    unnamed x20, local copies, waits for them, and re-layouts: 8.35 us -> 6.75 us
  transfers between devices with their start and end apart: 16 -> 16, of which waited for: 8 -> 9; matrix products, arithmetic and copies ran while one was open for 2% -> 2% of each run, Pallas kernels for 24% -> 23%
where the time goes in v4:
time: 55.7 us; the launch traced here: 55.4 us
  Pallas kernels  21.8 us (39%)
  starting transfers between devices  16 us (29%)
  local copies, waits for them, and re-layouts  8.81 us (16%)
  waiting for transfers between devices  8.58 us (15%)
    pallas_call x3, Pallas kernels, attend(): pl.pallas_call(functools.partial(attend_kernel, shape), grid=(1,), in_spe...  15.2 us
    ppermute x9, starting transfers between devices, crossed(): return lax.ppermute(value, ('ws', 'seq'), pairs)  14.3 us
    ppermute x9, waiting for transfers between devices, crossed(): return lax.ppermute(value, ('ws', 'seq'), pairs)  7.08 us
    unnamed x20, local copies, waits for them, and re-layouts  6.75 us
    pallas_call x1, Pallas kernels, own_products(): pl.pallas_call(own_kernel, in_specs=[whole()] * 5, out_specs=[whole()] *...  2.16 us
    slice x2, local copies, waits for them, and re-layouts, body(): local[half:, at:at + size]  2.06 us
    pallas_call x1, Pallas kernels, add_products(): pl.pallas_call(functools.partial(add_kernel, at), in_specs=[whole()] * 5,...  1.81 us
    ppermute x7, starting transfers between devices, other_core(): return lax.ppermute(value, 'seq', [(s, s ^ 1) for s in range(count)])  1.68 us
  transfers between devices with their start and end apart: 16, of which 9 were waited for; matrix products, arithmetic and copies ran while one was open for 2% of the time, Pallas kernels for 23%

profile of v4, /device:TPU:0, one launch (start us, length us, event | category | flops | bytes accessed | tf_op | source)
XLA Modules:
  0.0 55.4 jit_solution(12052690456455409955)
XLA Ops:
  0.0 1.2 %slice.9 = bf16[192,1280]{1,0:T(8,128)(2,1)S(1)} slice(bf16[384,1536]{1,0:T(8,128)(2,1)} %bitcast.3), slice={[192:384], [0:1280]} | slice | bytes 983040 | tf_op jit(solution)/shard_map/slice | solution.py:365
  1.2 4.4 %collective-permute-start.1 = (bf16[192,1280]{1,0:T(8,128)(2,1)S(1)}, bf16[192,1280]{1,0:T(8,128)(2,1)S(1)}, u32[]{:S(2)}, u32[]{:S(2)}) collective-permute-start(bf16[192,1280]{1,0:T(8,128)(2,1)S(1)} %slice.9), channel_id=1, source_target_pairs={{0,15},{1,14},{2,13},{3,12},{4,11},{5,10},{6,9},{7,8},{8,7},{9,6},... | collective-permute-start | bytes 1474568 | tf_op jit(solution)/shard_map/ppermute | solution.py:345
  5.6 0.9 %slice.8 = bf16[192,256]{1,0:T(8,128)(2,1)S(1)} slice(bf16[384,1536]{1,0:T(8,128)(2,1)} %bitcast.4), slice={[192:384], [1280:1536]} | slice | bytes 196608 | tf_op jit(solution)/shard_map/slice | solution.py:365
  6.5 2.3 %copy-done = bf16[1536,1536]{1,0:T(8,128)(2,1)S(1)} copy-done((bf16[1536,1536]{1,0:T(8,128)(2,1)S(1)}, bf16[1536,1536]{1,0:T(8,128)(2,1)}, u32[]{:S(2)}) %copy-start) | copy-done | bytes 4718616
  8.8 2.3 %copy-done.2 = bf16[1536,1536]{1,0:T(8,128)(2,1)S(1)} copy-done((bf16[1536,1536]{1,0:T(8,128)(2,1)S(1)}, bf16[1536,1536]{1,0:T(8,128)(2,1)}, u32[]{:S(2)}) %copy-start.2) | copy-done | bytes 4718616
  11.2 1.1 %copy-done.5 = bf16[1536,192]{0,1:T(8,128)(2,1)S(1)} copy-done((bf16[1536,192]{0,1:T(8,128)(2,1)S(1)}, bf16[1536,192]{0,1:T(8,128)(2,1)}, u32[]{:S(2)}) %copy-start.5) | copy-done | bytes 589848
  12.2 1.0 %copy-done.6 = bf16[1536,128]{1,0:T(8,128)(2,1)S(1)} copy-done((bf16[1536,128]{1,0:T(8,128)(2,1)S(1)}, bf16[1536,128]{1,0:T(8,128)(2,1)}, u32[]{:S(2)}) %copy-start.6) | copy-done | bytes 393240
  13.2 2.2 %own_products.1 = (f32[192,1536]{1,0:T(8,128)S(1)}, f32[192,1536]{1,0:T(8,128)S(1)}, bf16[1536,384]{1,0:T(8,128)(2,1)S(1)}) custom-call(bf16[384,1536]{1,0:T(8,128)(2,1)S(1)} %bitcast.5, bf16[1536,1536]{1,0:T(8,128)(2,1)S(1)} %copy-done, bf16[1536,1536]{1,0:T(8,128)(2,1)S(1)} %copy-done.2, bf16[1536,128]{1,0:T(8,128)(2,1)S(1)} %copy-done.6, ...), custom_call_target="tpu_custom_call" | custom-call | flops 1811939328 | bytes 9437184 | tf_op jit(solution)/shard_map/own_products/pallas_call | solution.py:49
  15.4 1.8 %collective-permute-done.1.arrived = bf16[192,1280]{1,0:T(8,128)(2,1)S(1)} collective-permute-done((bf16[192,1280]{1,0:T(8,128)(2,1)S(1)}, bf16[192,1280]{1,0:T(8,128)(2,1)S(1)}, u32[]{:S(2)}, u32[]{:S(2)}) %collective-permute-start.1) | collective-permute-done | bytes 491552 | tf_op jit(solution)/shard_map/ppermute | solution.py:345
  17.2 1.8 %add_products.1 = (f32[192,1536]{1,0:T(8,128)S(1)}, f32[192,1536]{1,0:T(8,128)S(1)}) custom-call(bf16[192,1280]{1,0:T(8,128)(2,1)S(1)} %collective-permute-done.1.arrived, f32[192,1536]{1,0:T(8,128)S(1)} %get-tuple-element.28.same, f32[192,1536]{1,0:T(8,128)S(1)} %get-tuple-element.29.partner, bf16[1536,1536]{1,0:T(8,128)(2,1)S(1)} %copy-done.1, ...), custom_call_target="tpu_custom_call" | custom-call | flops 1509949440 | bytes 7864320 | tf_op jit(solution)/shard_map/add_products/pallas_call | solution.py:104
  19.3 1.3 %hidden_and_pairs.1 = (bf16[384,1536]{1,0:T(8,128)(2,1)S(1)}, bf16[480,128]{1,0:T(8,128)(2,1)S(1)}, bf16[480,128]{1,0:T(8,128)(2,1)S(1)}) custom-call(bf16[192,256]{1,0:T(8,128)(2,1)S(1)} %collective-permute-done.arrived, f32[192,1536]{1,0:T(8,128)S(1)} %get-tuple-element.30.same, f32[192,1536]{1,0:T(8,128)S(1)} %get-tuple-element.31.partner, ...), custom_call_target="tpu_custom_call" | custom-call | flops 679477248 | bytes 1572864 | tf_op jit(solution)/shard_map/hidden_and_pairs/pallas_call | solution.py:136
  20.6 3.3 %collective-permute-start.4 = (bf16[480,128]{1,0:T(8,128)(2,1)S(1)}, bf16[480,128]{1,0:T(8,128)(2,1)S(1)}, u32[]{:S(2)}, u32[]{:S(2)}) collective-permute-start(bf16[480,128]{1,0:T(8,128)(2,1)S(1)} %get-tuple-element.39.refs_1_), channel_id=1, source_target_pairs={{0,6},{1,7},{2,4},{3,5},{4,2},{5,3},{6,0},{7,1},{8,14},{9,15},{10,... | collective-permute-start | bytes 368648 | tf_op jit(solution)/shard_map/ppermute | solution.py:345
  24.5 2.0 %collective-permute-start.5 = (bf16[480,128]{1,0:T(8,128)(2,1)S(1)}, bf16[480,128]{1,0:T(8,128)(2,1)S(1)}, u32[]{:S(2)}, u32[]{:S(2)}) collective-permute-start(bf16[480,128]{1,0:T(8,128)(2,1)S(1)} %get-tuple-element.34), channel_id=1, source_target_pairs={{0,8},{1,9},{2,10},{3,11},{4,12},{5,13},{6,14},{7,15},{8,0},{9,1},... | collective-permute-start | bytes 368648 | tf_op jit(solution)/shard_map/ppermute | solution.py:345
  26.5 1.4 %query_rows.1 = (bf16[192,1024]{1,0:T(8,128)(2,1)S(1)}, bf16[192,1024]{1,0:T(8,128)(2,1)S(1)}) custom-call(bf16[384,1536]{1,0:T(8,128)(2,1)S(1)} %get-tuple-element.35.hidden, bf16[1536,1024]{1,0:T(8,128)(2,1)S(1)} %copy-done.7), custom_call_target="tpu_custom_call" | custom-call | flops 1207959552 | bytes 3145728 | tf_op jit(solution)/shard_map/query_rows/pallas_call | solution.py:161
  27.9 1.0 %collective-permute-start.6 = (bf16[192,1024]{1,0:T(8,128)(2,1)S(1)}, bf16[192,1024]{1,0:T(8,128)(2,1)S(1)}, u32[]{:S(2)}, u32[]{:S(2)}) collective-permute-start(bf16[192,1024]{1,0:T(8,128)(2,1)S(1)} %get-tuple-element.38), channel_id=1, source_target_pairs={{0,15},{1,14},{2,13},{3,12},{4,11},{5,10},{6,9},{7,8},{8,7},{9,6},... | collective-permute-start | bytes 1179656 | tf_op jit(solution)/shard_map/ppermute | solution.py:345
  29.4 0.8 %collective-permute-done.3.refs_3_ = bf16[480,128]{1,0:T(8,128)(2,1)S(1)} collective-permute-done((bf16[480,128]{1,0:T(8,128)(2,1)S(1)}, bf16[480,128]{1,0:T(8,128)(2,1)S(1)}, u32[]{:S(2)}, u32[]{:S(2)}) %collective-permute-start.3) | collective-permute-done | bytes 122912 | tf_op jit(solution)/shard_map/ppermute | solution.py:345
  31.9 2.0 %collective-permute-start.12 = (bf16[480,128]{1,0:T(8,128)(2,1)S(1)}, bf16[480,128]{1,0:T(8,128)(2,1)S(1)}, u32[]{:S(2)}, u32[]{:S(2)}) collective-permute-start(bf16[480,128]{1,0:T(8,128)(2,1)S(1)} %collective-permute-done.5.refs_9_), channel_id=1, source_target_pairs={{0,6},{1,7},{2,4},{3,5},{4,2},{5,3},{6,0},{7,1},{8,14},{9,15},{10,... | collective-permute-start | bytes 368648 | tf_op jit(solution)/shard_map/ppermute | solution.py:345
  34.0 1.0 %collective-permute-start.13 = (bf16[960,128]{1,0:T(8,128)(2,1)S(1)}, bf16[960,128]{1,0:T(8,128)(2,1)S(1)}, u32[]{:S(2)}, u32[]{:S(2)}) collective-permute-start(bf16[960,128]{1,0:T(8,128)(2,1)S(1)} %pad_maximum_fusion), channel_id=1, source_target_pairs={{0,2},{1,5},{2,0},{3,7},{4,6},{5,1},{6,4},{7,3},{8,10},{9,13},{10,... | collective-permute-start | bytes 737288 | tf_op jit(solution)/shard_map/ppermute | solution.py:345
  34.9 3.5 %attend.3 = (f32[4,384,256]{2,1,0:T(8,128)S(1)}, f32[4,384,128]{2,1,0:T(8,128)S(1)}) custom-call(bf16[192,1024]{1,0:T(8,128)(2,1)S(1)} %get-tuple-element.37.refs_0_, bf16[480,128]{1,0:T(8,128)(2,1)S(1)} %get-tuple-element.39.refs_1_, bf16[480,128]{1,0:T(8,128)(2,1)S(1)} %collective-permute-done.2.refs_2_, ...), custom_call_target="tpu_custom_call" | custom-call | flops 1233125376 | bytes 1146880 | tf_op jit(solution)/shard_map/attend/pallas_call | solution.py:310
  38.5 2.1 %collective-permute-done.6.refs_0_.refs_1_ = bf16[192,1024]{1,0:T(8,128)(2,1)S(1)} collective-permute-done((bf16[192,1024]{1,0:T(8,128)(2,1)S(1)}, bf16[192,1024]{1,0:T(8,128)(2,1)S(1)}, u32[]{:S(2)}, u32[]{:S(2)}) %collective-permute-start.6) | collective-permute-done | bytes 393248 | tf_op jit(solution)/shard_map/ppermute | solution.py:345
  40.6 3.7 %attend.4 = (f32[4,384,256]{2,1,0:T(8,128)S(1)}, f32[4,384,128]{2,1,0:T(8,128)S(1)}) custom-call(bf16[192,1024]{1,0:T(8,128)(2,1)S(1)} %collective-permute-done.6.refs_0_.refs_1_, bf16[480,128]{1,0:T(8,128)(2,1)S(1)} %get-tuple-element.39.refs_1_, bf16[480,128]{1,0:T(8,128)(2,1)S(1)} %collective-permute-done.2.refs_2_, ...), custom_call_target="tpu_custom_call" | custom-call | flops 1761607680 | bytes 1146880 | tf_op jit(solution)/shard_map/attend/pallas_call | solution.py:310
  44.3 1.4 %collective-permute-done.13.refs_4_ = bf16[960,128]{1,0:T(8,128)(2,1)S(1)} collective-permute-done((bf16[960,128]{1,0:T(8,128)(2,1)S(1)}, bf16[960,128]{1,0:T(8,128)(2,1)S(1)}, u32[]{:S(2)}, u32[]{:S(2)}) %collective-permute-start.13) | collective-permute-done | bytes 245792 | tf_op jit(solution)/shard_map/ppermute | solution.py:345
  46.2 1.2 %collective-permute-done.14.refs_5_ = bf16[480,128]{1,0:T(8,128)(2,1)S(1)} collective-permute-done((bf16[480,128]{1,0:T(8,128)(2,1)S(1)}, bf16[480,128]{1,0:T(8,128)(2,1)S(1)}, u32[]{:S(2)}, u32[]{:S(2)}) %collective-permute-start.14) | collective-permute-done | bytes 122912 | tf_op jit(solution)/shard_map/ppermute | solution.py:330
  47.4 7.9 %attend.5 = bf16[384,1536]{1,0:T(8,128)(2,1)} custom-call(bf16[192,1024]{1,0:T(8,128)(2,1)S(1)} %get-tuple-element.37.refs_0_, bf16[192,1024]{1,0:T(8,128)(2,1)S(1)} %collective-permute-done.6.refs_0_.refs_1_, bf16[480,128]{1,0:T(8,128)(2,1)S(1)} %collective-permute-done.11.refs_10_.refs_2_, bf16[480,128]{1,0:T(8,128)(2,1)S(1)} %collective-permute-done.12.refs_3_, ...), custom_call_target="tpu_custom_call" | custom-call | flops 4328521728 | bytes 819200 | tf_op jit(solution)/shard_map/attend/pallas_call | solution.py:310
  (39 shorter events, 3.7 us)
Async XLA Ops:
  0.0 6.5 %copy-start.4 = (bf16[1,384,1536]{2,1,0:T(8,128)(2,1)S(1)}, bf16[1,384,1536]{2,1,0:T(8,128)(2,1)}, u32[]{:S(2)}) copy-start(bf16[1,384,1536]{2,1,0:T(8,128)(2,1)} %param.7) | copy-start | bytes 3538948
  1.2 16.0 %collective-permute-start.1 = (bf16[192,1280]{1,0:T(8,128)(2,1)S(1)}, bf16[192,1280]{1,0:T(8,128)(2,1)S(1)}, u32[]{:S(2)}, u32[]{:S(2)}) collective-permute-start(bf16[192,1280]{1,0:T(8,128)(2,1)S(1)} %slice.9), channel_id=1, source_target_pairs={{0,15},{1,14},{2,13},{3,12},{4,11},{5,10},{6,9},{7,8},{8,7},{9,6},... | collective-permute-start | bytes 1474568 | tf_op jit(solution)/shard_map/ppermute | solution.py:345
  6.5 12.8 %collective-permute-start = (bf16[192,256]{1,0:T(8,128)(2,1)S(1)}, bf16[192,256]{1,0:T(8,128)(2,1)S(1)}, u32[]{:S(2)}, u32[]{:S(2)}) collective-permute-start(bf16[192,256]{1,0:T(8,128)(2,1)S(1)} %slice.8), channel_id=1, source_target_pairs={{0,15},{1,14},{2,13},{3,12},{4,11},{5,10},{6,9},{7,8},{8,7},{9,6},... | collective-permute-start | bytes 294920 | tf_op jit(solution)/shard_map/ppermute | solution.py:345
  6.5 2.3 %copy-start = (bf16[1536,1536]{1,0:T(8,128)(2,1)S(1)}, bf16[1536,1536]{1,0:T(8,128)(2,1)}, u32[]{:S(2)}) copy-start(bf16[1536,1536]{1,0:T(8,128)(2,1)} %w_same.5) | copy-start | bytes 14155780
  8.8 2.3 %copy-start.2 = (bf16[1536,1536]{1,0:T(8,128)(2,1)S(1)}, bf16[1536,1536]{1,0:T(8,128)(2,1)}, u32[]{:S(2)}) copy-start(bf16[1536,1536]{1,0:T(8,128)(2,1)} %w_partner.5) | copy-start | bytes 14155780
  13.2 4.0 %copy-start.1 = (bf16[1536,1536]{1,0:T(8,128)(2,1)S(1)}, bf16[1536,1536]{1,0:T(8,128)(2,1)}, u32[]{:S(2)}) copy-start(bf16[1536,1536]{1,0:T(8,128)(2,1)} %w_same.5) | copy-start | bytes 14155780
  13.2 4.0 %copy-start.3 = (bf16[1536,1536]{1,0:T(8,128)(2,1)S(1)}, bf16[1536,1536]{1,0:T(8,128)(2,1)}, u32[]{:S(2)}) copy-start(bf16[1536,1536]{1,0:T(8,128)(2,1)} %w_partner.5) | copy-start | bytes 14155780
  19.3 7.2 %copy-start.7 = (bf16[1536,1024]{1,0:T(8,128)(2,1)S(1)}, bf16[1536,1024]{1,0:T(8,128)(2,1)}, u32[]{:S(2)}) copy-start(bf16[1536,1024]{1,0:T(8,128)(2,1)} %w_query.1) | copy-start | bytes 9437188
  20.6 8.8 %collective-permute-start.4 = (bf16[480,128]{1,0:T(8,128)(2,1)S(1)}, bf16[480,128]{1,0:T(8,128)(2,1)S(1)}, u32[]{:S(2)}, u32[]{:S(2)}) collective-permute-start(bf16[480,128]{1,0:T(8,128)(2,1)S(1)} %get-tuple-element.39.refs_1_), channel_id=1, source_target_pairs={{0,6},{1,7},{2,4},{3,5},{4,2},{5,3},{6,0},{7,1},{8,14},{9,15},{10,... | collective-permute-start | bytes 368648 | tf_op jit(solution)/shard_map/ppermute | solution.py:345
  23.9 6.4 %collective-permute-start.3 = (bf16[480,128]{1,0:T(8,128)(2,1)S(1)}, bf16[480,128]{1,0:T(8,128)(2,1)S(1)}, u32[]{:S(2)}, u32[]{:S(2)}) collective-permute-start(bf16[480,128]{1,0:T(8,128)(2,1)S(1)} %get-tuple-element.39.refs_1_), channel_id=1, source_target_pairs={{0,4},{1,5},{2,6},{3,7},{4,0},{5,1},{6,2},{7,3},{8,12},{9,13},{10,... | collective-permute-start | bytes 368648 | tf_op jit(solution)/shard_map/ppermute | solution.py:345
  24.4 6.0 %collective-permute-start.2 = (bf16[480,128]{1,0:T(8,128)(2,1)S(1)}, bf16[480,128]{1,0:T(8,128)(2,1)S(1)}, u32[]{:S(2)}, u32[]{:S(2)}) collective-permute-start(bf16[480,128]{1,0:T(8,128)(2,1)S(1)} %get-tuple-element.39.refs_1_), channel_id=1, source_target_pairs={{0,2},{1,3},{2,0},{3,1},{4,6},{5,7},{6,4},{7,5},{8,10},{9,11},{10,... | collective-permute-start | bytes 368648 | tf_op jit(solution)/shard_map/ppermute | solution.py:345
  24.5 4.9 %collective-permute-start.5 = (bf16[480,128]{1,0:T(8,128)(2,1)S(1)}, bf16[480,128]{1,0:T(8,128)(2,1)S(1)}, u32[]{:S(2)}, u32[]{:S(2)}) collective-permute-start(bf16[480,128]{1,0:T(8,128)(2,1)S(1)} %get-tuple-element.34), channel_id=1, source_target_pairs={{0,8},{1,9},{2,10},{3,11},{4,12},{5,13},{6,14},{7,15},{8,0},{9,1},... | collective-permute-start | bytes 368648 | tf_op jit(solution)/shard_map/ppermute | solution.py:345
  26.5 20.9 %slice-start = ((s8[4718592]{0:T(1024)(128)(4,1)}), s8[4194304]{0:T(1024)(128)(4,1)S(1)}, s32[]{:S(2)}) async-start(s8[4718592]{0:T(1024)(128)(4,1)} %bitcast.7), calls=%async_computation | async-start | bytes 8388608
  27.9 12.6 %collective-permute-start.6 = (bf16[192,1024]{1,0:T(8,128)(2,1)S(1)}, bf16[192,1024]{1,0:T(8,128)(2,1)S(1)}, u32[]{:S(2)}, u32[]{:S(2)}) collective-permute-start(bf16[192,1024]{1,0:T(8,128)(2,1)S(1)} %get-tuple-element.38), channel_id=1, source_target_pairs={{0,15},{1,14},{2,13},{3,12},{4,11},{5,10},{6,9},{7,8},{8,7},{9,6},... | collective-permute-start | bytes 1179656 | tf_op jit(solution)/shard_map/ppermute | solution.py:345
  30.4 1.3 %collective-permute-start.11 = (bf16[480,128]{1,0:T(8,128)(2,1)S(1)}, bf16[480,128]{1,0:T(8,128)(2,1)S(1)}, u32[]{:S(2)}, u32[]{:S(2)}) collective-permute-start(bf16[480,128]{1,0:T(8,128)(2,1)S(1)} %collective-permute-done.5.refs_9_), channel_id=1, source_target_pairs={{0,1},{1,0},{2,3},{3,2},{4,5},{5,4},{6,7},{7,6},{8,9},{9,8},{10,11... | collective-permute-start | bytes 368648 | tf_op jit(solution)/shard_map/ppermute | solution.py:330
  30.5 1.4 %collective-permute-start.7 = (bf16[480,128]{1,0:T(8,128)(2,1)S(1)}, bf16[480,128]{1,0:T(8,128)(2,1)S(1)}, u32[]{:S(2)}, u32[]{:S(2)}) collective-permute-start(bf16[480,128]{1,0:T(8,128)(2,1)S(1)} %get-tuple-element.39.refs_1_), channel_id=1, source_target_pairs={{0,1},{1,0},{2,3},{3,2},{4,5},{5,4},{6,7},{7,6},{8,9},{9,8},{10,11... | collective-permute-start | bytes 368648 | tf_op jit(solution)/shard_map/ppermute | solution.py:330
  30.9 3.1 %collective-permute-start.8 = (bf16[480,128]{1,0:T(8,128)(2,1)S(1)}, bf16[480,128]{1,0:T(8,128)(2,1)S(1)}, u32[]{:S(2)}, u32[]{:S(2)}) collective-permute-start(bf16[480,128]{1,0:T(8,128)(2,1)S(1)} %collective-permute-done.2.refs_2_), channel_id=1, source_target_pairs={{0,1},{1,0},{2,3},{3,2},{4,5},{5,4},{6,7},{7,6},{8,9},{9,8},{10,11... | collective-permute-start | bytes 368648 | tf_op jit(solution)/shard_map/ppermute | solution.py:330
  31.0 3.9 %collective-permute-start.9 = (bf16[480,128]{1,0:T(8,128)(2,1)S(1)}, bf16[480,128]{1,0:T(8,128)(2,1)S(1)}, u32[]{:S(2)}, u32[]{:S(2)}) collective-permute-start(bf16[480,128]{1,0:T(8,128)(2,1)S(1)} %collective-permute-done.3.refs_3_), channel_id=1, source_target_pairs={{0,1},{1,0},{2,3},{3,2},{4,5},{5,4},{6,7},{7,6},{8,9},{9,8},{10,11... | collective-permute-start | bytes 368648 | tf_op jit(solution)/shard_map/ppermute | solution.py:330
  31.7 3.2 %collective-permute-start.10 = (bf16[480,128]{1,0:T(8,128)(2,1)S(1)}, bf16[480,128]{1,0:T(8,128)(2,1)S(1)}, u32[]{:S(2)}, u32[]{:S(2)}) collective-permute-start(bf16[480,128]{1,0:T(8,128)(2,1)S(1)} %collective-permute-done.4.refs_4_), channel_id=1, source_target_pairs={{0,1},{1,0},{2,3},{3,2},{4,5},{5,4},{6,7},{7,6},{8,9},{9,8},{10,11... | collective-permute-start | bytes 368648 | tf_op jit(solution)/shard_map/ppermute | solution.py:330
  31.9 15.5 %slice-start.1 = ((s8[4718592]{0:T(1024)(128)(4,1)}), s8[524288]{0:T(1024)(128)(4,1)S(1)}, s32[]{:S(2)}) async-start(s8[4718592]{0:T(1024)(128)(4,1)} %bitcast.7), calls=%async_computation.1 | async-start | bytes 1048576
  31.9 12.4 %collective-permute-start.12 = (bf16[480,128]{1,0:T(8,128)(2,1)S(1)}, bf16[480,128]{1,0:T(8,128)(2,1)S(1)}, u32[]{:S(2)}, u32[]{:S(2)}) collective-permute-start(bf16[480,128]{1,0:T(8,128)(2,1)S(1)} %collective-permute-done.5.refs_9_), channel_id=1, source_target_pairs={{0,6},{1,7},{2,4},{3,5},{4,2},{5,3},{6,0},{7,1},{8,14},{9,15},{10,... | collective-permute-start | bytes 368648 | tf_op jit(solution)/shard_map/ppermute | solution.py:345
  34.0 11.8 %collective-permute-start.13 = (bf16[960,128]{1,0:T(8,128)(2,1)S(1)}, bf16[960,128]{1,0:T(8,128)(2,1)S(1)}, u32[]{:S(2)}, u32[]{:S(2)}) collective-permute-start(bf16[960,128]{1,0:T(8,128)(2,1)S(1)} %pad_maximum_fusion), channel_id=1, source_target_pairs={{0,2},{1,5},{2,0},{3,7},{4,6},{5,1},{6,4},{7,3},{8,10},{9,13},{10,... | collective-permute-start | bytes 737288 | tf_op jit(solution)/shard_map/ppermute | solution.py:345
  45.7 1.7 %collective-permute-start.15 = (bf16[960,128]{1,0:T(8,128)(2,1)S(1)}, bf16[960,128]{1,0:T(8,128)(2,1)S(1)}, u32[]{:S(2)}, u32[]{:S(2)}) collective-permute-start(bf16[960,128]{1,0:T(8,128)(2,1)S(1)} %collective-permute-done.13.refs_4_), channel_id=1, source_target_pairs={{0,1},{1,0},{2,3},{3,2},{4,5},{5,4},{6,7},{7,6},{8,9},{9,8},{10,11... | collective-permute-start | bytes 737288 | tf_op jit(solution)/shard_map/ppermute | solution.py:330
  45.7 1.7 %collective-permute-start.14 = (bf16[480,128]{1,0:T(8,128)(2,1)S(1)}, bf16[480,128]{1,0:T(8,128)(2,1)S(1)}, u32[]{:S(2)}, u32[]{:S(2)}) collective-permute-start(bf16[480,128]{1,0:T(8,128)(2,1)S(1)} %collective-permute-done.12.refs_3_), channel_id=1, source_target_pairs={{0,1},{1,0},{2,3},{3,2},{4,5},{5,4},{6,7},{7,6},{8,9},{9,8},{10,11... | collective-permute-start | bytes 368648 | tf_op jit(solution)/shard_map/ppermute | solution.py:330
  (2 other events, 2.1 us)

commit v5 on v4

--- a/solution.py
+++ b/solution.py
@@ -345,13 +345,9 @@
     return lax.ppermute(value, ("ws", "seq"), pairs)
 
 
-def spread(block, twin):
-    places = list(range(2, lax.axis_size("seq"), 2))
+def spread(block, twin, places):
     whole_chip = jnp.concatenate([block, twin], 0)
-    single = crossed(block, 0, places[-1])
-    return [single] + [
-        crossed(whole_chip, 0, (places[i], places[i + 1])) for i in range(0, len(places) - 1, 2)
-    ]
+    return [crossed(whole_chip, 0, (places[i], places[i + 1])) for i in range(0, len(places), 2)]
 
 
 def body(tokens, w_same, w_partner, w_query, w_key, w_value, w_out):
@@ -372,15 +368,17 @@
     places = range(2, count, 2)
     near = [own] + [crossed(own, 0, k) for k in places]
     lifted = crossed(other, 1, 0)
+    across = crossed(other, 1, count - 1)
     query, sent = query_rows(hidden, w_query, [half, half])
-    near, lifted, query = lax.optimization_barrier((near, lifted, query))
+    near, lifted, across, query = lax.optimization_barrier((near, lifted, across, query))
     high = other_core(lifted)
-    early = near + [other_core(part) for part in near] + [lifted, high]
+    early = near + [across]
+    early = early + [other_core(part) for part in early] + [lifted, high]
     brought = crossed(sent, 1, count - 1)
     spare = len(early) * half % 256 if len(early) * half % 256 <= half else 0
-    mine = attend([query], early, half, keys, values, weight=0.7, drop=spare)
+    mine = attend([query], early, half, keys, values, weight=0.5, drop=spare)
     brought = after(brought, mine)
-    far = spread(lifted, high)
+    far = spread(lifted, high, places[:-1])
     theirs = attend([brought], early, half, keys, values, weight=1.0, drop=spare)
     far = after(far, theirs)
     late = far + [other_core(part) for part in far]

time: 55.7 us -> 55.6 us (level)
  waiting for transfers between devices: 8.58 us -> 6.8 us
  starting transfers between devices: 16 us -> 17.2 us
  Pallas kernels: 21.8 us -> 22.4 us
    ppermute x9, waiting for transfers between devices: 7.08 us -> 4.47 us  [crossed(): return lax.ppermute(value, ('ws', 'seq'), pairs)]
    ppermute x7, starting transfers between devices: 1.68 us -> 2.8 us  [other_core(): return lax.ppermute(value, 'seq', [(s, s ^ 1) for s in range(count)])]
    ppermute x7, waiting for transfers between devices: 1.5 us -> 2.33 us  [other_core(): return lax.ppermute(value, 'seq', [(s, s ^ 1) for s in range(count)])]
  transfers between devices with their start and end apart: 16 -> 16, of which waited for: 9 -> 7; matrix products, arithmetic and copies ran while one was open for 2% -> 2% of each run, Pallas kernels for 23% -> 27%
where the time goes in v5:
time: 55.6 us; the launch traced here: 55.3 us
  Pallas kernels  22.4 us (40%)
  starting transfers between devices  17.2 us (31%)
  local copies, waits for them, and re-layouts  8.81 us (16%)
  waiting for transfers between devices  6.8 us (12%)
    pallas_call x3, Pallas kernels, attend(): pl.pallas_call(functools.partial(attend_kernel, shape), grid=(1,), in_spe...  15.7 us
    ppermute x9, starting transfers between devices, crossed(): return lax.ppermute(value, ('ws', 'seq'), pairs)  14.4 us
    unnamed x20, local copies, waits for them, and re-layouts  6.75 us
    ppermute x9, waiting for transfers between devices, crossed(): return lax.ppermute(value, ('ws', 'seq'), pairs)  4.47 us
    ppermute x7, starting transfers between devices, other_core(): return lax.ppermute(value, 'seq', [(s, s ^ 1) for s in range(count)])  2.8 us
    ppermute x7, waiting for transfers between devices, other_core(): return lax.ppermute(value, 'seq', [(s, s ^ 1) for s in range(count)])  2.33 us
    pallas_call x1, Pallas kernels, own_products(): pl.pallas_call(own_kernel, in_specs=[whole()] * 5, out_specs=[whole()] *...  2.16 us
    slice x2, local copies, waits for them, and re-layouts, body(): local[half:, at:at + size]  2.06 us
  transfers between devices with their start and end apart: 16, of which 7 were waited for; matrix products, arithmetic and copies ran while one was open for 2% of the time, Pallas kernels for 27%

profile of v5, /device:TPU:0, one launch (start us, length us, event | category | flops | bytes accessed | tf_op | source)
XLA Modules:
  0.0 55.3 jit_solution(17470858938222494714)
XLA Ops:
  0.0 1.2 %slice.9 = bf16[192,1280]{1,0:T(8,128)(2,1)S(1)} slice(bf16[384,1536]{1,0:T(8,128)(2,1)} %bitcast.3), slice={[192:384], [0:1280]} | slice | bytes 983040 | tf_op jit(solution)/shard_map/slice | solution.py:361
  1.2 4.4 %collective-permute-start.1 = (bf16[192,1280]{1,0:T(8,128)(2,1)S(1)}, bf16[192,1280]{1,0:T(8,128)(2,1)S(1)}, u32[]{:S(2)}, u32[]{:S(2)}) collective-permute-start(bf16[192,1280]{1,0:T(8,128)(2,1)S(1)} %slice.9), channel_id=1, source_target_pairs={{0,15},{1,14},{2,13},{3,12},{4,11},{5,10},{6,9},{7,8},{8,7},{9,6},... | collective-permute-start | bytes 1474568 | tf_op jit(solution)/shard_map/ppermute | solution.py:345
  5.6 0.9 %slice.8 = bf16[192,256]{1,0:T(8,128)(2,1)S(1)} slice(bf16[384,1536]{1,0:T(8,128)(2,1)} %bitcast.4), slice={[192:384], [1280:1536]} | slice | bytes 196608 | tf_op jit(solution)/shard_map/slice | solution.py:361
  6.5 2.3 %copy-done = bf16[1536,1536]{1,0:T(8,128)(2,1)S(1)} copy-done((bf16[1536,1536]{1,0:T(8,128)(2,1)S(1)}, bf16[1536,1536]{1,0:T(8,128)(2,1)}, u32[]{:S(2)}) %copy-start) | copy-done | bytes 4718616
  8.8 2.3 %copy-done.2 = bf16[1536,1536]{1,0:T(8,128)(2,1)S(1)} copy-done((bf16[1536,1536]{1,0:T(8,128)(2,1)S(1)}, bf16[1536,1536]{1,0:T(8,128)(2,1)}, u32[]{:S(2)}) %copy-start.2) | copy-done | bytes 4718616
  11.2 1.1 %copy-done.5 = bf16[1536,192]{0,1:T(8,128)(2,1)S(1)} copy-done((bf16[1536,192]{0,1:T(8,128)(2,1)S(1)}, bf16[1536,192]{0,1:T(8,128)(2,1)}, u32[]{:S(2)}) %copy-start.5) | copy-done | bytes 589848
  12.2 1.0 %copy-done.6 = bf16[1536,128]{1,0:T(8,128)(2,1)S(1)} copy-done((bf16[1536,128]{1,0:T(8,128)(2,1)S(1)}, bf16[1536,128]{1,0:T(8,128)(2,1)}, u32[]{:S(2)}) %copy-start.6) | copy-done | bytes 393240
  13.2 2.2 %own_products.1 = (f32[192,1536]{1,0:T(8,128)S(1)}, f32[192,1536]{1,0:T(8,128)S(1)}, bf16[1536,384]{1,0:T(8,128)(2,1)S(1)}) custom-call(bf16[384,1536]{1,0:T(8,128)(2,1)S(1)} %bitcast.5, bf16[1536,1536]{1,0:T(8,128)(2,1)S(1)} %copy-done, bf16[1536,1536]{1,0:T(8,128)(2,1)S(1)} %copy-done.2, bf16[1536,128]{1,0:T(8,128)(2,1)S(1)} %copy-done.6, ...), custom_call_target="tpu_custom_call" | custom-call | flops 1811939328 | bytes 9437184 | tf_op jit(solution)/shard_map/own_products/pallas_call | solution.py:49
  15.4 1.8 %collective-permute-done.1.arrived = bf16[192,1280]{1,0:T(8,128)(2,1)S(1)} collective-permute-done((bf16[192,1280]{1,0:T(8,128)(2,1)S(1)}, bf16[192,1280]{1,0:T(8,128)(2,1)S(1)}, u32[]{:S(2)}, u32[]{:S(2)}) %collective-permute-start.1) | collective-permute-done | bytes 491552 | tf_op jit(solution)/shard_map/ppermute | solution.py:345
  17.2 1.8 %add_products.1 = (f32[192,1536]{1,0:T(8,128)S(1)}, f32[192,1536]{1,0:T(8,128)S(1)}) custom-call(bf16[192,1280]{1,0:T(8,128)(2,1)S(1)} %collective-permute-done.1.arrived, f32[192,1536]{1,0:T(8,128)S(1)} %get-tuple-element.28.same, f32[192,1536]{1,0:T(8,128)S(1)} %get-tuple-element.29.partner, bf16[1536,1536]{1,0:T(8,128)(2,1)S(1)} %copy-done.1, ...), custom_call_target="tpu_custom_call" | custom-call | flops 1509949440 | bytes 7864320 | tf_op jit(solution)/shard_map/add_products/pallas_call | solution.py:104
  19.3 1.3 %hidden_and_pairs.1 = (bf16[384,1536]{1,0:T(8,128)(2,1)S(1)}, bf16[480,128]{1,0:T(8,128)(2,1)S(1)}, bf16[480,128]{1,0:T(8,128)(2,1)S(1)}) custom-call(bf16[192,256]{1,0:T(8,128)(2,1)S(1)} %collective-permute-done.arrived, f32[192,1536]{1,0:T(8,128)S(1)} %get-tuple-element.30.same, f32[192,1536]{1,0:T(8,128)S(1)} %get-tuple-element.31.partner, ...), custom_call_target="tpu_custom_call" | custom-call | flops 679477248 | bytes 1572864 | tf_op jit(solution)/shard_map/hidden_and_pairs/pallas_call | solution.py:136
  20.6 2.3 %collective-permute-start.2 = (bf16[480,128]{1,0:T(8,128)(2,1)S(1)}, bf16[480,128]{1,0:T(8,128)(2,1)S(1)}, u32[]{:S(2)}, u32[]{:S(2)}) collective-permute-start(bf16[480,128]{1,0:T(8,128)(2,1)S(1)} %get-tuple-element.39.refs_1_), channel_id=1, source_target_pairs={{0,2},{1,3},{2,0},{3,1},{4,6},{5,7},{6,4},{7,5},{8,10},{9,11},{10,... | collective-permute-start | bytes 368648 | tf_op jit(solution)/shard_map/ppermute | solution.py:345
  22.9 1.5 %collective-permute-start.3 = (bf16[480,128]{1,0:T(8,128)(2,1)S(1)}, bf16[480,128]{1,0:T(8,128)(2,1)S(1)}, u32[]{:S(2)}, u32[]{:S(2)}) collective-permute-start(bf16[480,128]{1,0:T(8,128)(2,1)S(1)} %get-tuple-element.39.refs_1_), channel_id=1, source_target_pairs={{0,4},{1,5},{2,6},{3,7},{4,0},{5,1},{6,2},{7,3},{8,12},{9,13},{10,... | collective-permute-start | bytes 368648 | tf_op jit(solution)/shard_map/ppermute | solution.py:345
  24.5 2.0 %collective-permute-start.5 = (bf16[480,128]{1,0:T(8,128)(2,1)S(1)}, bf16[480,128]{1,0:T(8,128)(2,1)S(1)}, u32[]{:S(2)}, u32[]{:S(2)}) collective-permute-start(bf16[480,128]{1,0:T(8,128)(2,1)S(1)} %get-tuple-element.34), channel_id=1, source_target_pairs={{0,8},{1,9},{2,10},{3,11},{4,12},{5,13},{6,14},{7,15},{8,0},{9,1},... | collective-permute-start | bytes 368648 | tf_op jit(solution)/shard_map/ppermute | solution.py:345
  26.5 0.9 %collective-permute-start.6 = (bf16[480,128]{1,0:T(8,128)(2,1)S(1)}, bf16[480,128]{1,0:T(8,128)(2,1)S(1)}, u32[]{:S(2)}, u32[]{:S(2)}) collective-permute-start(bf16[480,128]{1,0:T(8,128)(2,1)S(1)} %get-tuple-element.34), channel_id=1, source_target_pairs={{0,15},{1,14},{2,13},{3,12},{4,11},{5,10},{6,9},{7,8},{8,7},{9,6},... | collective-permute-start | bytes 368648 | tf_op jit(solution)/shard_map/ppermute | solution.py:345
  27.4 1.4 %query_rows.1 = (bf16[192,1024]{1,0:T(8,128)(2,1)S(1)}, bf16[192,1024]{1,0:T(8,128)(2,1)S(1)}) custom-call(bf16[384,1536]{1,0:T(8,128)(2,1)S(1)} %get-tuple-element.35.hidden, bf16[1536,1024]{1,0:T(8,128)(2,1)S(1)} %copy-done.7), custom_call_target="tpu_custom_call" | custom-call | flops 1207959552 | bytes 3145728 | tf_op jit(solution)/shard_map/query_rows/pallas_call | solution.py:161
  28.8 2.7 %collective-permute-start.7 = (bf16[192,1024]{1,0:T(8,128)(2,1)S(1)}, bf16[192,1024]{1,0:T(8,128)(2,1)S(1)}, u32[]{:S(2)}, u32[]{:S(2)}) collective-permute-start(bf16[192,1024]{1,0:T(8,128)(2,1)S(1)} %get-tuple-element.38), channel_id=1, source_target_pairs={{0,15},{1,14},{2,13},{3,12},{4,11},{5,10},{6,9},{7,8},{8,7},{9,6},... | collective-permute-start | bytes 1179656 | tf_op jit(solution)/shard_map/ppermute | solution.py:345
  31.5 2.4 %collective-permute-done.6.refs_5_ = bf16[480,128]{1,0:T(8,128)(2,1)S(1)} collective-permute-done((bf16[480,128]{1,0:T(8,128)(2,1)S(1)}, bf16[480,128]{1,0:T(8,128)(2,1)S(1)}, u32[]{:S(2)}, u32[]{:S(2)}) %collective-permute-start.6) | collective-permute-done | bytes 122912 | tf_op jit(solution)/shard_map/ppermute | solution.py:345
  33.9 1.0 %collective-permute-start.10 = (bf16[480,128]{1,0:T(8,128)(2,1)S(1)}, bf16[480,128]{1,0:T(8,128)(2,1)S(1)}, u32[]{:S(2)}, u32[]{:S(2)}) collective-permute-start(bf16[480,128]{1,0:T(8,128)(2,1)S(1)} %collective-permute-done.3.refs_3_), channel_id=1, source_target_pairs={{0,1},{1,0},{2,3},{3,2},{4,5},{5,4},{6,7},{7,6},{8,9},{9,8},{10,11... | collective-permute-start | bytes 368648 | tf_op jit(solution)/shard_map/ppermute | solution.py:330
  37.5 4.4 %attend.3 = (f32[4,384,256]{2,1,0:T(8,128)S(1)}, f32[4,384,128]{2,1,0:T(8,128)S(1)}) custom-call(bf16[192,1024]{1,0:T(8,128)(2,1)S(1)} %get-tuple-element.37.refs_0_, bf16[480,128]{1,0:T(8,128)(2,1)S(1)} %get-tuple-element.39.refs_1_, bf16[480,128]{1,0:T(8,128)(2,1)S(1)} %collective-permute-done.2.refs_2_, ...), custom_call_target="tpu_custom_call" | custom-call | flops 1132462080 | bytes 1474560 | tf_op jit(solution)/shard_map/attend/pallas_call | solution.py:310
  42.0 4.9 %attend.4 = (f32[4,384,256]{2,1,0:T(8,128)S(1)}, f32[4,384,128]{2,1,0:T(8,128)S(1)}) custom-call(bf16[192,1024]{1,0:T(8,128)(2,1)S(1)} %collective-permute-done.7.refs_0_.refs_1_, bf16[480,128]{1,0:T(8,128)(2,1)S(1)} %get-tuple-element.39.refs_1_, bf16[480,128]{1,0:T(8,128)(2,1)S(1)} %collective-permute-done.2.refs_2_, ...), custom_call_target="tpu_custom_call" | custom-call | flops 2264924160 | bytes 1474560 | tf_op jit(solution)/shard_map/attend/pallas_call | solution.py:310
  46.9 0.8 %collective-permute-start.15 = (bf16[960,128]{1,0:T(8,128)(2,1)S(1)}, bf16[960,128]{1,0:T(8,128)(2,1)S(1)}, u32[]{:S(2)}, u32[]{:S(2)}) collective-permute-start(bf16[960,128]{1,0:T(8,128)(2,1)S(1)} %collective-permute-done.14.refs_2_), channel_id=1, source_target_pairs={{0,1},{1,0},{2,3},{3,2},{4,5},{5,4},{6,7},{7,6},{8,9},{9,8},{10,11... | collective-permute-start | bytes 737288 | tf_op jit(solution)/shard_map/ppermute | solution.py:330
  47.7 1.1 %collective-permute-done.15.refs_3_ = bf16[960,128]{1,0:T(8,128)(2,1)S(1)} collective-permute-done((bf16[960,128]{1,0:T(8,128)(2,1)S(1)}, bf16[960,128]{1,0:T(8,128)(2,1)S(1)}, u32[]{:S(2)}, u32[]{:S(2)}) %collective-permute-start.15) | collective-permute-done | bytes 245792 | tf_op jit(solution)/shard_map/ppermute | solution.py:330
  48.9 6.4 %attend.5 = bf16[384,1536]{1,0:T(8,128)(2,1)} custom-call(bf16[192,1024]{1,0:T(8,128)(2,1)S(1)} %get-tuple-element.37.refs_0_, bf16[192,1024]{1,0:T(8,128)(2,1)S(1)} %collective-permute-done.7.refs_0_.refs_1_, bf16[960,128]{1,0:T(8,128)(2,1)S(1)} %collective-permute-done.14.refs_2_, bf16[960,128]{1,0:T(8,128)(2,1)S(1)} %collective-permute-done.15.refs_3_, ...), custom_call_target="tpu_custom_call" | custom-call | flops 3321888768 | bytes 491520 | tf_op jit(solution)/shard_map/attend/pallas_call | solution.py:310
  (39 shorter events, 3.0 us)
Async XLA Ops:
  0.0 6.5 %copy-start.4 = (bf16[1,384,1536]{2,1,0:T(8,128)(2,1)S(1)}, bf16[1,384,1536]{2,1,0:T(8,128)(2,1)}, u32[]{:S(2)}) copy-start(bf16[1,384,1536]{2,1,0:T(8,128)(2,1)} %param.7) | copy-start | bytes 3538948
  1.2 16.0 %collective-permute-start.1 = (bf16[192,1280]{1,0:T(8,128)(2,1)S(1)}, bf16[192,1280]{1,0:T(8,128)(2,1)S(1)}, u32[]{:S(2)}, u32[]{:S(2)}) collective-permute-start(bf16[192,1280]{1,0:T(8,128)(2,1)S(1)} %slice.9), channel_id=1, source_target_pairs={{0,15},{1,14},{2,13},{3,12},{4,11},{5,10},{6,9},{7,8},{8,7},{9,6},... | collective-permute-start | bytes 1474568 | tf_op jit(solution)/shard_map/ppermute | solution.py:345
  6.5 12.8 %collective-permute-start = (bf16[192,256]{1,0:T(8,128)(2,1)S(1)}, bf16[192,256]{1,0:T(8,128)(2,1)S(1)}, u32[]{:S(2)}, u32[]{:S(2)}) collective-permute-start(bf16[192,256]{1,0:T(8,128)(2,1)S(1)} %slice.8), channel_id=1, source_target_pairs={{0,15},{1,14},{2,13},{3,12},{4,11},{5,10},{6,9},{7,8},{8,7},{9,6},... | collective-permute-start | bytes 294920 | tf_op jit(solution)/shard_map/ppermute | solution.py:345
  6.5 2.3 %copy-start = (bf16[1536,1536]{1,0:T(8,128)(2,1)S(1)}, bf16[1536,1536]{1,0:T(8,128)(2,1)}, u32[]{:S(2)}) copy-start(bf16[1536,1536]{1,0:T(8,128)(2,1)} %w_same.5) | copy-start | bytes 14155780
  8.8 2.3 %copy-start.2 = (bf16[1536,1536]{1,0:T(8,128)(2,1)S(1)}, bf16[1536,1536]{1,0:T(8,128)(2,1)}, u32[]{:S(2)}) copy-start(bf16[1536,1536]{1,0:T(8,128)(2,1)} %w_partner.5) | copy-start | bytes 14155780
  13.2 4.0 %copy-start.1 = (bf16[1536,1536]{1,0:T(8,128)(2,1)S(1)}, bf16[1536,1536]{1,0:T(8,128)(2,1)}, u32[]{:S(2)}) copy-start(bf16[1536,1536]{1,0:T(8,128)(2,1)} %w_same.5) | copy-start | bytes 14155780
  13.2 4.0 %copy-start.3 = (bf16[1536,1536]{1,0:T(8,128)(2,1)S(1)}, bf16[1536,1536]{1,0:T(8,128)(2,1)}, u32[]{:S(2)}) copy-start(bf16[1536,1536]{1,0:T(8,128)(2,1)} %w_partner.5) | copy-start | bytes 14155780
  19.3 8.2 %copy-start.7 = (bf16[1536,1024]{1,0:T(8,128)(2,1)S(1)}, bf16[1536,1024]{1,0:T(8,128)(2,1)}, u32[]{:S(2)}) copy-start(bf16[1536,1024]{1,0:T(8,128)(2,1)} %w_query.1) | copy-start | bytes 9437188
  20.6 8.2 %collective-permute-start.2 = (bf16[480,128]{1,0:T(8,128)(2,1)S(1)}, bf16[480,128]{1,0:T(8,128)(2,1)S(1)}, u32[]{:S(2)}, u32[]{:S(2)}) collective-permute-start(bf16[480,128]{1,0:T(8,128)(2,1)S(1)} %get-tuple-element.39.refs_1_), channel_id=1, source_target_pairs={{0,2},{1,3},{2,0},{3,1},{4,6},{5,7},{6,4},{7,5},{8,10},{9,11},{10,... | collective-permute-start | bytes 368648 | tf_op jit(solution)/shard_map/ppermute | solution.py:345
  22.9 8.6 %collective-permute-start.3 = (bf16[480,128]{1,0:T(8,128)(2,1)S(1)}, bf16[480,128]{1,0:T(8,128)(2,1)S(1)}, u32[]{:S(2)}, u32[]{:S(2)}) collective-permute-start(bf16[480,128]{1,0:T(8,128)(2,1)S(1)} %get-tuple-element.39.refs_1_), channel_id=1, source_target_pairs={{0,4},{1,5},{2,6},{3,7},{4,0},{5,1},{6,2},{7,3},{8,12},{9,13},{10,... | collective-permute-start | bytes 368648 | tf_op jit(solution)/shard_map/ppermute | solution.py:345
  24.5 7.1 %collective-permute-start.4 = (bf16[480,128]{1,0:T(8,128)(2,1)S(1)}, bf16[480,128]{1,0:T(8,128)(2,1)S(1)}, u32[]{:S(2)}, u32[]{:S(2)}) collective-permute-start(bf16[480,128]{1,0:T(8,128)(2,1)S(1)} %get-tuple-element.39.refs_1_), channel_id=1, source_target_pairs={{0,6},{1,7},{2,4},{3,5},{4,2},{5,3},{6,0},{7,1},{8,14},{9,15},{10,... | collective-permute-start | bytes 368648 | tf_op jit(solution)/shard_map/ppermute | solution.py:345
  24.5 7.0 %collective-permute-start.5 = (bf16[480,128]{1,0:T(8,128)(2,1)S(1)}, bf16[480,128]{1,0:T(8,128)(2,1)S(1)}, u32[]{:S(2)}, u32[]{:S(2)}) collective-permute-start(bf16[480,128]{1,0:T(8,128)(2,1)S(1)} %get-tuple-element.34), channel_id=1, source_target_pairs={{0,8},{1,9},{2,10},{3,11},{4,12},{5,13},{6,14},{7,15},{8,0},{9,1},... | collective-permute-start | bytes 368648 | tf_op jit(solution)/shard_map/ppermute | solution.py:345
  26.5 7.4 %collective-permute-start.6 = (bf16[480,128]{1,0:T(8,128)(2,1)S(1)}, bf16[480,128]{1,0:T(8,128)(2,1)S(1)}, u32[]{:S(2)}, u32[]{:S(2)}) collective-permute-start(bf16[480,128]{1,0:T(8,128)(2,1)S(1)} %get-tuple-element.34), channel_id=1, source_target_pairs={{0,15},{1,14},{2,13},{3,12},{4,11},{5,10},{6,9},{7,8},{8,7},{9,6},... | collective-permute-start | bytes 368648 | tf_op jit(solution)/shard_map/ppermute | solution.py:345
  28.8 13.1 %collective-permute-start.7 = (bf16[192,1024]{1,0:T(8,128)(2,1)S(1)}, bf16[192,1024]{1,0:T(8,128)(2,1)S(1)}, u32[]{:S(2)}, u32[]{:S(2)}) collective-permute-start(bf16[192,1024]{1,0:T(8,128)(2,1)S(1)} %get-tuple-element.38), channel_id=1, source_target_pairs={{0,15},{1,14},{2,13},{3,12},{4,11},{5,10},{6,9},{7,8},{8,7},{9,6},... | collective-permute-start | bytes 1179656 | tf_op jit(solution)/shard_map/ppermute | solution.py:345
  33.9 1.9 %collective-permute-start.10 = (bf16[480,128]{1,0:T(8,128)(2,1)S(1)}, bf16[480,128]{1,0:T(8,128)(2,1)S(1)}, u32[]{:S(2)}, u32[]{:S(2)}) collective-permute-start(bf16[480,128]{1,0:T(8,128)(2,1)S(1)} %collective-permute-done.3.refs_3_), channel_id=1, source_target_pairs={{0,1},{1,0},{2,3},{3,2},{4,5},{5,4},{6,7},{7,6},{8,9},{9,8},{10,11... | collective-permute-start | bytes 368648 | tf_op jit(solution)/shard_map/ppermute | solution.py:330
  34.9 1.3 %collective-permute-start.13 = (bf16[480,128]{1,0:T(8,128)(2,1)S(1)}, bf16[480,128]{1,0:T(8,128)(2,1)S(1)}, u32[]{:S(2)}, u32[]{:S(2)}) collective-permute-start(bf16[480,128]{1,0:T(8,128)(2,1)S(1)} %collective-permute-done.5.refs_11_), channel_id=1, source_target_pairs={{0,1},{1,0},{2,3},{3,2},{4,5},{5,4},{6,7},{7,6},{8,9},{9,8},{10,11... | collective-permute-start | bytes 368648 | tf_op jit(solution)/shard_map/ppermute | solution.py:330
  34.9 1.5 %collective-permute-start.11 = (bf16[480,128]{1,0:T(8,128)(2,1)S(1)}, bf16[480,128]{1,0:T(8,128)(2,1)S(1)}, u32[]{:S(2)}, u32[]{:S(2)}) collective-permute-start(bf16[480,128]{1,0:T(8,128)(2,1)S(1)} %collective-permute-done.4.refs_4_), channel_id=1, source_target_pairs={{0,1},{1,0},{2,3},{3,2},{4,5},{5,4},{6,7},{7,6},{8,9},{9,8},{10,11... | collective-permute-start | bytes 368648 | tf_op jit(solution)/shard_map/ppermute | solution.py:330
  35.4 1.4 %collective-permute-start.12 = (bf16[480,128]{1,0:T(8,128)(2,1)S(1)}, bf16[480,128]{1,0:T(8,128)(2,1)S(1)}, u32[]{:S(2)}, u32[]{:S(2)}) collective-permute-start(bf16[480,128]{1,0:T(8,128)(2,1)S(1)} %collective-permute-done.6.refs_5_), channel_id=1, source_target_pairs={{0,1},{1,0},{2,3},{3,2},{4,5},{5,4},{6,7},{7,6},{8,9},{9,8},{10,11... | collective-permute-start | bytes 368648 | tf_op jit(solution)/shard_map/ppermute | solution.py:330
  35.8 1.3 %collective-permute-start.8 = (bf16[480,128]{1,0:T(8,128)(2,1)S(1)}, bf16[480,128]{1,0:T(8,128)(2,1)S(1)}, u32[]{:S(2)}, u32[]{:S(2)}) collective-permute-start(bf16[480,128]{1,0:T(8,128)(2,1)S(1)} %get-tuple-element.39.refs_1_), channel_id=1, source_target_pairs={{0,1},{1,0},{2,3},{3,2},{4,5},{5,4},{6,7},{7,6},{8,9},{9,8},{10,11... | collective-permute-start | bytes 368648 | tf_op jit(solution)/shard_map/ppermute | solution.py:330
  36.2 1.3 %collective-permute-start.9 = (bf16[480,128]{1,0:T(8,128)(2,1)S(1)}, bf16[480,128]{1,0:T(8,128)(2,1)S(1)}, u32[]{:S(2)}, u32[]{:S(2)}) collective-permute-start(bf16[480,128]{1,0:T(8,128)(2,1)S(1)} %collective-permute-done.2.refs_2_), channel_id=1, source_target_pairs={{0,1},{1,0},{2,3},{3,2},{4,5},{5,4},{6,7},{7,6},{8,9},{9,8},{10,11... | collective-permute-start | bytes 368648 | tf_op jit(solution)/shard_map/ppermute | solution.py:330
  36.4 10.5 %collective-permute-start.14 = (bf16[960,128]{1,0:T(8,128)(2,1)S(1)}, bf16[960,128]{1,0:T(8,128)(2,1)S(1)}, u32[]{:S(2)}, u32[]{:S(2)}) collective-permute-start(bf16[960,128]{1,0:T(8,128)(2,1)S(1)} %pad_maximum_fusion), channel_id=1, source_target_pairs={{0,2},{1,5},{2,0},{3,7},{4,6},{5,1},{6,4},{7,3},{8,10},{9,13},{10,... | collective-permute-start | bytes 737288 | tf_op jit(solution)/shard_map/ppermute | solution.py:345
  37.5 11.3 %slice-start = ((s8[4718592]{0:T(1024)(128)(4,1)}), s8[4194304]{0:T(1024)(128)(4,1)S(1)}, s32[]{:S(2)}) async-start(s8[4718592]{0:T(1024)(128)(4,1)} %bitcast.7), calls=%async_computation | async-start | bytes 8388608
  42.0 6.9 %slice-start.1 = ((s8[4718592]{0:T(1024)(128)(4,1)}), s8[524288]{0:T(1024)(128)(4,1)S(1)}, s32[]{:S(2)}) async-start(s8[4718592]{0:T(1024)(128)(4,1)} %bitcast.7), calls=%async_computation.1 | async-start | bytes 1048576
  46.9 1.9 %collective-permute-start.15 = (bf16[960,128]{1,0:T(8,128)(2,1)S(1)}, bf16[960,128]{1,0:T(8,128)(2,1)S(1)}, u32[]{:S(2)}, u32[]{:S(2)}) collective-permute-start(bf16[960,128]{1,0:T(8,128)(2,1)S(1)} %collective-permute-done.14.refs_2_), channel_id=1, source_target_pairs={{0,1},{1,0},{2,3},{3,2},{4,5},{5,4},{6,7},{7,6},{8,9},{9,8},{10,11... | collective-permute-start | bytes 737288 | tf_op jit(solution)/shard_map/ppermute | solution.py:330
  (2 other events, 2.1 us)

commit v6 on v5

--- a/solution.py
+++ b/solution.py
@@ -367,10 +367,11 @@
     )
     places = range(2, count, 2)
     near = [own] + [crossed(own, 0, k) for k in places]
+    across = crossed(other, 1, count - 1)
     lifted = crossed(other, 1, 0)
-    across = crossed(other, 1, count - 1)
     query, sent = query_rows(hidden, w_query, [half, half])
-    near, lifted, across, query = lax.optimization_barrier((near, lifted, across, query))
+    near, lifted, query = lax.optimization_barrier((near, lifted, query))
+    across = after(across, query)
     high = other_core(lifted)
     early = near + [across]
     early = early + [other_core(part) for part in early] + [lifted, high]

time: 55.6 us -> 55.6 us (level)
  no operation moved by 1% of the time
where the time goes in v6:
time: 55.6 us; the launch traced here: 55.3 us
  Pallas kernels  22.4 us (40%)
  starting transfers between devices  17.1 us (31%)
  local copies, waits for them, and re-layouts  8.81 us (16%)
  waiting for transfers between devices  6.8 us (12%)
    pallas_call x3, Pallas kernels, attend(): pl.pallas_call(functools.partial(attend_kernel, shape), grid=(1,), in_spe...  15.7 us
    ppermute x9, starting transfers between devices, crossed(): return lax.ppermute(value, ('ws', 'seq'), pairs)  14.4 us
    unnamed x20, local copies, waits for them, and re-layouts  6.75 us
    ppermute x9, waiting for transfers between devices, crossed(): return lax.ppermute(value, ('ws', 'seq'), pairs)  4.47 us
    ppermute x7, starting transfers between devices, other_core(): return lax.ppermute(value, 'seq', [(s, s ^ 1) for s in range(count)])  2.79 us
    ppermute x7, waiting for transfers between devices, other_core(): return lax.ppermute(value, 'seq', [(s, s ^ 1) for s in range(count)])  2.33 us
    pallas_call x1, Pallas kernels, own_products(): pl.pallas_call(own_kernel, in_specs=[whole()] * 5, out_specs=[whole()] *...  2.16 us
    slice x2, local copies, waits for them, and re-layouts, body(): local[half:, at:at + size]  2.06 us
  transfers between devices with their start and end apart: 16, of which 7 were waited for; matrix products, arithmetic and copies ran while one was open for 2% of the time, Pallas kernels for 27%

profile of v6, /device:TPU:0, one launch (start us, length us, event | category | flops | bytes accessed | tf_op | source)
XLA Modules:
  0.0 55.3 jit_solution(3438909790874389851)
XLA Ops:
  0.0 1.2 %slice.9 = bf16[192,1280]{1,0:T(8,128)(2,1)S(1)} slice(bf16[384,1536]{1,0:T(8,128)(2,1)} %bitcast.3), slice={[192:384], [0:1280]} | slice | bytes 983040 | tf_op jit(solution)/shard_map/slice | solution.py:361
  1.2 4.4 %collective-permute-start.1 = (bf16[192,1280]{1,0:T(8,128)(2,1)S(1)}, bf16[192,1280]{1,0:T(8,128)(2,1)S(1)}, u32[]{:S(2)}, u32[]{:S(2)}) collective-permute-start(bf16[192,1280]{1,0:T(8,128)(2,1)S(1)} %slice.9), channel_id=1, source_target_pairs={{0,15},{1,14},{2,13},{3,12},{4,11},{5,10},{6,9},{7,8},{8,7},{9,6},... | collective-permute-start | bytes 1474568 | tf_op jit(solution)/shard_map/ppermute | solution.py:345
  5.6 0.9 %slice.8 = bf16[192,256]{1,0:T(8,128)(2,1)S(1)} slice(bf16[384,1536]{1,0:T(8,128)(2,1)} %bitcast.4), slice={[192:384], [1280:1536]} | slice | bytes 196608 | tf_op jit(solution)/shard_map/slice | solution.py:361
  6.5 2.3 %copy-done = bf16[1536,1536]{1,0:T(8,128)(2,1)S(1)} copy-done((bf16[1536,1536]{1,0:T(8,128)(2,1)S(1)}, bf16[1536,1536]{1,0:T(8,128)(2,1)}, u32[]{:S(2)}) %copy-start) | copy-done | bytes 4718616
  8.8 2.3 %copy-done.2 = bf16[1536,1536]{1,0:T(8,128)(2,1)S(1)} copy-done((bf16[1536,1536]{1,0:T(8,128)(2,1)S(1)}, bf16[1536,1536]{1,0:T(8,128)(2,1)}, u32[]{:S(2)}) %copy-start.2) | copy-done | bytes 4718616
  11.2 1.1 %copy-done.5 = bf16[1536,192]{0,1:T(8,128)(2,1)S(1)} copy-done((bf16[1536,192]{0,1:T(8,128)(2,1)S(1)}, bf16[1536,192]{0,1:T(8,128)(2,1)}, u32[]{:S(2)}) %copy-start.5) | copy-done | bytes 589848
  12.2 1.0 %copy-done.6 = bf16[1536,128]{1,0:T(8,128)(2,1)S(1)} copy-done((bf16[1536,128]{1,0:T(8,128)(2,1)S(1)}, bf16[1536,128]{1,0:T(8,128)(2,1)}, u32[]{:S(2)}) %copy-start.6) | copy-done | bytes 393240
  13.2 2.2 %own_products.1 = (f32[192,1536]{1,0:T(8,128)S(1)}, f32[192,1536]{1,0:T(8,128)S(1)}, bf16[1536,384]{1,0:T(8,128)(2,1)S(1)}) custom-call(bf16[384,1536]{1,0:T(8,128)(2,1)S(1)} %bitcast.5, bf16[1536,1536]{1,0:T(8,128)(2,1)S(1)} %copy-done, bf16[1536,1536]{1,0:T(8,128)(2,1)S(1)} %copy-done.2, bf16[1536,128]{1,0:T(8,128)(2,1)S(1)} %copy-done.6, ...), custom_call_target="tpu_custom_call" | custom-call | flops 1811939328 | bytes 9437184 | tf_op jit(solution)/shard_map/own_products/pallas_call | solution.py:49
  15.4 1.8 %collective-permute-done.1.arrived = bf16[192,1280]{1,0:T(8,128)(2,1)S(1)} collective-permute-done((bf16[192,1280]{1,0:T(8,128)(2,1)S(1)}, bf16[192,1280]{1,0:T(8,128)(2,1)S(1)}, u32[]{:S(2)}, u32[]{:S(2)}) %collective-permute-start.1) | collective-permute-done | bytes 491552 | tf_op jit(solution)/shard_map/ppermute | solution.py:345
  17.2 1.8 %add_products.1 = (f32[192,1536]{1,0:T(8,128)S(1)}, f32[192,1536]{1,0:T(8,128)S(1)}) custom-call(bf16[192,1280]{1,0:T(8,128)(2,1)S(1)} %collective-permute-done.1.arrived, f32[192,1536]{1,0:T(8,128)S(1)} %get-tuple-element.28.same, f32[192,1536]{1,0:T(8,128)S(1)} %get-tuple-element.29.partner, bf16[1536,1536]{1,0:T(8,128)(2,1)S(1)} %copy-done.1, ...), custom_call_target="tpu_custom_call" | custom-call | flops 1509949440 | bytes 7864320 | tf_op jit(solution)/shard_map/add_products/pallas_call | solution.py:104
  19.3 1.3 %hidden_and_pairs.1 = (bf16[384,1536]{1,0:T(8,128)(2,1)S(1)}, bf16[480,128]{1,0:T(8,128)(2,1)S(1)}, bf16[480,128]{1,0:T(8,128)(2,1)S(1)}) custom-call(bf16[192,256]{1,0:T(8,128)(2,1)S(1)} %collective-permute-done.arrived, f32[192,1536]{1,0:T(8,128)S(1)} %get-tuple-element.30.same, f32[192,1536]{1,0:T(8,128)S(1)} %get-tuple-element.31.partner, ...), custom_call_target="tpu_custom_call" | custom-call | flops 679477248 | bytes 1572864 | tf_op jit(solution)/shard_map/hidden_and_pairs/pallas_call | solution.py:136
  20.6 2.3 %collective-permute-start.2 = (bf16[480,128]{1,0:T(8,128)(2,1)S(1)}, bf16[480,128]{1,0:T(8,128)(2,1)S(1)}, u32[]{:S(2)}, u32[]{:S(2)}) collective-permute-start(bf16[480,128]{1,0:T(8,128)(2,1)S(1)} %get-tuple-element.39.refs_1_), channel_id=1, source_target_pairs={{0,2},{1,3},{2,0},{3,1},{4,6},{5,7},{6,4},{7,5},{8,10},{9,11},{10,... | collective-permute-start | bytes 368648 | tf_op jit(solution)/shard_map/ppermute | solution.py:345
  22.9 1.5 %collective-permute-start.3 = (bf16[480,128]{1,0:T(8,128)(2,1)S(1)}, bf16[480,128]{1,0:T(8,128)(2,1)S(1)}, u32[]{:S(2)}, u32[]{:S(2)}) collective-permute-start(bf16[480,128]{1,0:T(8,128)(2,1)S(1)} %get-tuple-element.39.refs_1_), channel_id=1, source_target_pairs={{0,4},{1,5},{2,6},{3,7},{4,0},{5,1},{6,2},{7,3},{8,12},{9,13},{10,... | collective-permute-start | bytes 368648 | tf_op jit(solution)/shard_map/ppermute | solution.py:345
  24.5 2.0 %collective-permute-start.5 = (bf16[480,128]{1,0:T(8,128)(2,1)S(1)}, bf16[480,128]{1,0:T(8,128)(2,1)S(1)}, u32[]{:S(2)}, u32[]{:S(2)}) collective-permute-start(bf16[480,128]{1,0:T(8,128)(2,1)S(1)} %get-tuple-element.34), channel_id=1, source_target_pairs={{0,8},{1,9},{2,10},{3,11},{4,12},{5,13},{6,14},{7,15},{8,0},{9,1},... | collective-permute-start | bytes 368648 | tf_op jit(solution)/shard_map/ppermute | solution.py:345
  26.5 0.9 %collective-permute-start.7 = (bf16[480,128]{1,0:T(8,128)(2,1)S(1)}, bf16[480,128]{1,0:T(8,128)(2,1)S(1)}, u32[]{:S(2)}, u32[]{:S(2)}) collective-permute-start(bf16[480,128]{1,0:T(8,128)(2,1)S(1)} %get-tuple-element.34), channel_id=1, source_target_pairs={{0,15},{1,14},{2,13},{3,12},{4,11},{5,10},{6,9},{7,8},{8,7},{9,6},... | collective-permute-start | bytes 368648 | tf_op jit(solution)/shard_map/ppermute | solution.py:345
  27.4 1.4 %query_rows.1 = (bf16[192,1024]{1,0:T(8,128)(2,1)S(1)}, bf16[192,1024]{1,0:T(8,128)(2,1)S(1)}) custom-call(bf16[384,1536]{1,0:T(8,128)(2,1)S(1)} %get-tuple-element.35.hidden, bf16[1536,1024]{1,0:T(8,128)(2,1)S(1)} %copy-done.7), custom_call_target="tpu_custom_call" | custom-call | flops 1207959552 | bytes 3145728 | tf_op jit(solution)/shard_map/query_rows/pallas_call | solution.py:161
  28.8 2.7 %collective-permute-start.6 = (bf16[192,1024]{1,0:T(8,128)(2,1)S(1)}, bf16[192,1024]{1,0:T(8,128)(2,1)S(1)}, u32[]{:S(2)}, u32[]{:S(2)}) collective-permute-start(bf16[192,1024]{1,0:T(8,128)(2,1)S(1)} %get-tuple-element.38), channel_id=1, source_target_pairs={{0,15},{1,14},{2,13},{3,12},{4,11},{5,10},{6,9},{7,8},{8,7},{9,6},... | collective-permute-start | bytes 1179656 | tf_op jit(solution)/shard_map/ppermute | solution.py:345
  31.5 2.4 %collective-permute-done.7.refs_5_ = bf16[480,128]{1,0:T(8,128)(2,1)S(1)} collective-permute-done((bf16[480,128]{1,0:T(8,128)(2,1)S(1)}, bf16[480,128]{1,0:T(8,128)(2,1)S(1)}, u32[]{:S(2)}, u32[]{:S(2)}) %collective-permute-start.7) | collective-permute-done | bytes 122912 | tf_op jit(solution)/shard_map/ppermute | solution.py:345
  33.9 1.0 %collective-permute-start.12 = (bf16[480,128]{1,0:T(8,128)(2,1)S(1)}, bf16[480,128]{1,0:T(8,128)(2,1)S(1)}, u32[]{:S(2)}, u32[]{:S(2)}) collective-permute-start(bf16[480,128]{1,0:T(8,128)(2,1)S(1)} %collective-permute-done.7.refs_5_), channel_id=1, source_target_pairs={{0,1},{1,0},{2,3},{3,2},{4,5},{5,4},{6,7},{7,6},{8,9},{9,8},{10,11... | collective-permute-start | bytes 368648 | tf_op jit(solution)/shard_map/ppermute | solution.py:330
  37.5 4.4 %attend.3 = (f32[4,384,256]{2,1,0:T(8,128)S(1)}, f32[4,384,128]{2,1,0:T(8,128)S(1)}) custom-call(bf16[192,1024]{1,0:T(8,128)(2,1)S(1)} %get-tuple-element.37.refs_0_, bf16[480,128]{1,0:T(8,128)(2,1)S(1)} %get-tuple-element.39.refs_1_, bf16[480,128]{1,0:T(8,128)(2,1)S(1)} %collective-permute-done.2.refs_2_, ...), custom_call_target="tpu_custom_call" | custom-call | flops 1132462080 | bytes 1474560 | tf_op jit(solution)/shard_map/attend/pallas_call | solution.py:310
  42.0 4.9 %attend.4 = (f32[4,384,256]{2,1,0:T(8,128)S(1)}, f32[4,384,128]{2,1,0:T(8,128)S(1)}) custom-call(bf16[192,1024]{1,0:T(8,128)(2,1)S(1)} %collective-permute-done.6.refs_0_.refs_1_, bf16[480,128]{1,0:T(8,128)(2,1)S(1)} %get-tuple-element.39.refs_1_, bf16[480,128]{1,0:T(8,128)(2,1)S(1)} %collective-permute-done.2.refs_2_, ...), custom_call_target="tpu_custom_call" | custom-call | flops 2264924160 | bytes 1474560 | tf_op jit(solution)/shard_map/attend/pallas_call | solution.py:310
  46.9 0.8 %collective-permute-start.15 = (bf16[960,128]{1,0:T(8,128)(2,1)S(1)}, bf16[960,128]{1,0:T(8,128)(2,1)S(1)}, u32[]{:S(2)}, u32[]{:S(2)}) collective-permute-start(bf16[960,128]{1,0:T(8,128)(2,1)S(1)} %collective-permute-done.14.refs_2_), channel_id=1, source_target_pairs={{0,1},{1,0},{2,3},{3,2},{4,5},{5,4},{6,7},{7,6},{8,9},{9,8},{10,11... | collective-permute-start | bytes 737288 | tf_op jit(solution)/shard_map/ppermute | solution.py:330
  47.7 1.1 %collective-permute-done.15.refs_3_ = bf16[960,128]{1,0:T(8,128)(2,1)S(1)} collective-permute-done((bf16[960,128]{1,0:T(8,128)(2,1)S(1)}, bf16[960,128]{1,0:T(8,128)(2,1)S(1)}, u32[]{:S(2)}, u32[]{:S(2)}) %collective-permute-start.15) | collective-permute-done | bytes 245792 | tf_op jit(solution)/shard_map/ppermute | solution.py:330
  48.9 6.4 %attend.5 = bf16[384,1536]{1,0:T(8,128)(2,1)} custom-call(bf16[192,1024]{1,0:T(8,128)(2,1)S(1)} %get-tuple-element.37.refs_0_, bf16[192,1024]{1,0:T(8,128)(2,1)S(1)} %collective-permute-done.6.refs_0_.refs_1_, bf16[960,128]{1,0:T(8,128)(2,1)S(1)} %collective-permute-done.14.refs_2_, bf16[960,128]{1,0:T(8,128)(2,1)S(1)} %collective-permute-done.15.refs_3_, ...), custom_call_target="tpu_custom_call" | custom-call | flops 3321888768 | bytes 491520 | tf_op jit(solution)/shard_map/attend/pallas_call | solution.py:310
  (39 shorter events, 3.0 us)
Async XLA Ops:
  0.0 6.5 %copy-start.4 = (bf16[1,384,1536]{2,1,0:T(8,128)(2,1)S(1)}, bf16[1,384,1536]{2,1,0:T(8,128)(2,1)}, u32[]{:S(2)}) copy-start(bf16[1,384,1536]{2,1,0:T(8,128)(2,1)} %param.7) | copy-start | bytes 3538948
  1.2 16.0 %collective-permute-start.1 = (bf16[192,1280]{1,0:T(8,128)(2,1)S(1)}, bf16[192,1280]{1,0:T(8,128)(2,1)S(1)}, u32[]{:S(2)}, u32[]{:S(2)}) collective-permute-start(bf16[192,1280]{1,0:T(8,128)(2,1)S(1)} %slice.9), channel_id=1, source_target_pairs={{0,15},{1,14},{2,13},{3,12},{4,11},{5,10},{6,9},{7,8},{8,7},{9,6},... | collective-permute-start | bytes 1474568 | tf_op jit(solution)/shard_map/ppermute | solution.py:345
  6.5 12.8 %collective-permute-start = (bf16[192,256]{1,0:T(8,128)(2,1)S(1)}, bf16[192,256]{1,0:T(8,128)(2,1)S(1)}, u32[]{:S(2)}, u32[]{:S(2)}) collective-permute-start(bf16[192,256]{1,0:T(8,128)(2,1)S(1)} %slice.8), channel_id=1, source_target_pairs={{0,15},{1,14},{2,13},{3,12},{4,11},{5,10},{6,9},{7,8},{8,7},{9,6},... | collective-permute-start | bytes 294920 | tf_op jit(solution)/shard_map/ppermute | solution.py:345
  6.5 2.3 %copy-start = (bf16[1536,1536]{1,0:T(8,128)(2,1)S(1)}, bf16[1536,1536]{1,0:T(8,128)(2,1)}, u32[]{:S(2)}) copy-start(bf16[1536,1536]{1,0:T(8,128)(2,1)} %w_same.5) | copy-start | bytes 14155780
  8.8 2.3 %copy-start.2 = (bf16[1536,1536]{1,0:T(8,128)(2,1)S(1)}, bf16[1536,1536]{1,0:T(8,128)(2,1)}, u32[]{:S(2)}) copy-start(bf16[1536,1536]{1,0:T(8,128)(2,1)} %w_partner.5) | copy-start | bytes 14155780
  13.2 4.0 %copy-start.1 = (bf16[1536,1536]{1,0:T(8,128)(2,1)S(1)}, bf16[1536,1536]{1,0:T(8,128)(2,1)}, u32[]{:S(2)}) copy-start(bf16[1536,1536]{1,0:T(8,128)(2,1)} %w_same.5) | copy-start | bytes 14155780
  13.2 4.0 %copy-start.3 = (bf16[1536,1536]{1,0:T(8,128)(2,1)S(1)}, bf16[1536,1536]{1,0:T(8,128)(2,1)}, u32[]{:S(2)}) copy-start(bf16[1536,1536]{1,0:T(8,128)(2,1)} %w_partner.5) | copy-start | bytes 14155780
  19.3 8.2 %copy-start.7 = (bf16[1536,1024]{1,0:T(8,128)(2,1)S(1)}, bf16[1536,1024]{1,0:T(8,128)(2,1)}, u32[]{:S(2)}) copy-start(bf16[1536,1024]{1,0:T(8,128)(2,1)} %w_query.1) | copy-start | bytes 9437188
  20.6 8.2 %collective-permute-start.2 = (bf16[480,128]{1,0:T(8,128)(2,1)S(1)}, bf16[480,128]{1,0:T(8,128)(2,1)S(1)}, u32[]{:S(2)}, u32[]{:S(2)}) collective-permute-start(bf16[480,128]{1,0:T(8,128)(2,1)S(1)} %get-tuple-element.39.refs_1_), channel_id=1, source_target_pairs={{0,2},{1,3},{2,0},{3,1},{4,6},{5,7},{6,4},{7,5},{8,10},{9,11},{10,... | collective-permute-start | bytes 368648 | tf_op jit(solution)/shard_map/ppermute | solution.py:345
  22.9 8.6 %collective-permute-start.3 = (bf16[480,128]{1,0:T(8,128)(2,1)S(1)}, bf16[480,128]{1,0:T(8,128)(2,1)S(1)}, u32[]{:S(2)}, u32[]{:S(2)}) collective-permute-start(bf16[480,128]{1,0:T(8,128)(2,1)S(1)} %get-tuple-element.39.refs_1_), channel_id=1, source_target_pairs={{0,4},{1,5},{2,6},{3,7},{4,0},{5,1},{6,2},{7,3},{8,12},{9,13},{10,... | collective-permute-start | bytes 368648 | tf_op jit(solution)/shard_map/ppermute | solution.py:345
  24.5 7.1 %collective-permute-start.4 = (bf16[480,128]{1,0:T(8,128)(2,1)S(1)}, bf16[480,128]{1,0:T(8,128)(2,1)S(1)}, u32[]{:S(2)}, u32[]{:S(2)}) collective-permute-start(bf16[480,128]{1,0:T(8,128)(2,1)S(1)} %get-tuple-element.39.refs_1_), channel_id=1, source_target_pairs={{0,6},{1,7},{2,4},{3,5},{4,2},{5,3},{6,0},{7,1},{8,14},{9,15},{10,... | collective-permute-start | bytes 368648 | tf_op jit(solution)/shard_map/ppermute | solution.py:345
  24.5 7.0 %collective-permute-start.5 = (bf16[480,128]{1,0:T(8,128)(2,1)S(1)}, bf16[480,128]{1,0:T(8,128)(2,1)S(1)}, u32[]{:S(2)}, u32[]{:S(2)}) collective-permute-start(bf16[480,128]{1,0:T(8,128)(2,1)S(1)} %get-tuple-element.34), channel_id=1, source_target_pairs={{0,8},{1,9},{2,10},{3,11},{4,12},{5,13},{6,14},{7,15},{8,0},{9,1},... | collective-permute-start | bytes 368648 | tf_op jit(solution)/shard_map/ppermute | solution.py:345
  26.5 7.4 %collective-permute-start.7 = (bf16[480,128]{1,0:T(8,128)(2,1)S(1)}, bf16[480,128]{1,0:T(8,128)(2,1)S(1)}, u32[]{:S(2)}, u32[]{:S(2)}) collective-permute-start(bf16[480,128]{1,0:T(8,128)(2,1)S(1)} %get-tuple-element.34), channel_id=1, source_target_pairs={{0,15},{1,14},{2,13},{3,12},{4,11},{5,10},{6,9},{7,8},{8,7},{9,6},... | collective-permute-start | bytes 368648 | tf_op jit(solution)/shard_map/ppermute | solution.py:345
  28.8 13.2 %collective-permute-start.6 = (bf16[192,1024]{1,0:T(8,128)(2,1)S(1)}, bf16[192,1024]{1,0:T(8,128)(2,1)S(1)}, u32[]{:S(2)}, u32[]{:S(2)}) collective-permute-start(bf16[192,1024]{1,0:T(8,128)(2,1)S(1)} %get-tuple-element.38), channel_id=1, source_target_pairs={{0,15},{1,14},{2,13},{3,12},{4,11},{5,10},{6,9},{7,8},{8,7},{9,6},... | collective-permute-start | bytes 1179656 | tf_op jit(solution)/shard_map/ppermute | solution.py:345
  33.9 1.9 %collective-permute-start.12 = (bf16[480,128]{1,0:T(8,128)(2,1)S(1)}, bf16[480,128]{1,0:T(8,128)(2,1)S(1)}, u32[]{:S(2)}, u32[]{:S(2)}) collective-permute-start(bf16[480,128]{1,0:T(8,128)(2,1)S(1)} %collective-permute-done.7.refs_5_), channel_id=1, source_target_pairs={{0,1},{1,0},{2,3},{3,2},{4,5},{5,4},{6,7},{7,6},{8,9},{9,8},{10,11... | collective-permute-start | bytes 368648 | tf_op jit(solution)/shard_map/ppermute | solution.py:330
  34.9 1.3 %collective-permute-start.13 = (bf16[480,128]{1,0:T(8,128)(2,1)S(1)}, bf16[480,128]{1,0:T(8,128)(2,1)S(1)}, u32[]{:S(2)}, u32[]{:S(2)}) collective-permute-start(bf16[480,128]{1,0:T(8,128)(2,1)S(1)} %collective-permute-done.5.refs_11_), channel_id=1, source_target_pairs={{0,1},{1,0},{2,3},{3,2},{4,5},{5,4},{6,7},{7,6},{8,9},{9,8},{10,11... | collective-permute-start | bytes 368648 | tf_op jit(solution)/shard_map/ppermute | solution.py:330
  34.9 1.5 %collective-permute-start.10 = (bf16[480,128]{1,0:T(8,128)(2,1)S(1)}, bf16[480,128]{1,0:T(8,128)(2,1)S(1)}, u32[]{:S(2)}, u32[]{:S(2)}) collective-permute-start(bf16[480,128]{1,0:T(8,128)(2,1)S(1)} %collective-permute-done.3.refs_3_), channel_id=1, source_target_pairs={{0,1},{1,0},{2,3},{3,2},{4,5},{5,4},{6,7},{7,6},{8,9},{9,8},{10,11... | collective-permute-start | bytes 368648 | tf_op jit(solution)/shard_map/ppermute | solution.py:330
  35.4 1.4 %collective-permute-start.11 = (bf16[480,128]{1,0:T(8,128)(2,1)S(1)}, bf16[480,128]{1,0:T(8,128)(2,1)S(1)}, u32[]{:S(2)}, u32[]{:S(2)}) collective-permute-start(bf16[480,128]{1,0:T(8,128)(2,1)S(1)} %collective-permute-done.4.refs_4_), channel_id=1, source_target_pairs={{0,1},{1,0},{2,3},{3,2},{4,5},{5,4},{6,7},{7,6},{8,9},{9,8},{10,11... | collective-permute-start | bytes 368648 | tf_op jit(solution)/shard_map/ppermute | solution.py:330
  35.8 1.3 %collective-permute-start.8 = (bf16[480,128]{1,0:T(8,128)(2,1)S(1)}, bf16[480,128]{1,0:T(8,128)(2,1)S(1)}, u32[]{:S(2)}, u32[]{:S(2)}) collective-permute-start(bf16[480,128]{1,0:T(8,128)(2,1)S(1)} %get-tuple-element.39.refs_1_), channel_id=1, source_target_pairs={{0,1},{1,0},{2,3},{3,2},{4,5},{5,4},{6,7},{7,6},{8,9},{9,8},{10,11... | collective-permute-start | bytes 368648 | tf_op jit(solution)/shard_map/ppermute | solution.py:330
  36.2 1.3 %collective-permute-start.9 = (bf16[480,128]{1,0:T(8,128)(2,1)S(1)}, bf16[480,128]{1,0:T(8,128)(2,1)S(1)}, u32[]{:S(2)}, u32[]{:S(2)}) collective-permute-start(bf16[480,128]{1,0:T(8,128)(2,1)S(1)} %collective-permute-done.2.refs_2_), channel_id=1, source_target_pairs={{0,1},{1,0},{2,3},{3,2},{4,5},{5,4},{6,7},{7,6},{8,9},{9,8},{10,11... | collective-permute-start | bytes 368648 | tf_op jit(solution)/shard_map/ppermute | solution.py:330
  36.4 10.5 %collective-permute-start.14 = (bf16[960,128]{1,0:T(8,128)(2,1)S(1)}, bf16[960,128]{1,0:T(8,128)(2,1)S(1)}, u32[]{:S(2)}, u32[]{:S(2)}) collective-permute-start(bf16[960,128]{1,0:T(8,128)(2,1)S(1)} %pad_maximum_fusion), channel_id=1, source_target_pairs={{0,2},{1,5},{2,0},{3,7},{4,6},{5,1},{6,4},{7,3},{8,10},{9,13},{10,... | collective-permute-start | bytes 737288 | tf_op jit(solution)/shard_map/ppermute | solution.py:345
  37.5 11.3 %slice-start = ((s8[4718592]{0:T(1024)(128)(4,1)}), s8[4194304]{0:T(1024)(128)(4,1)S(1)}, s32[]{:S(2)}) async-start(s8[4718592]{0:T(1024)(128)(4,1)} %bitcast.7), calls=%async_computation | async-start | bytes 8388608
  42.0 6.9 %slice-start.1 = ((s8[4718592]{0:T(1024)(128)(4,1)}), s8[524288]{0:T(1024)(128)(4,1)S(1)}, s32[]{:S(2)}) async-start(s8[4718592]{0:T(1024)(128)(4,1)} %bitcast.7), calls=%async_computation.1 | async-start | bytes 1048576
  46.9 1.9 %collective-permute-start.15 = (bf16[960,128]{1,0:T(8,128)(2,1)S(1)}, bf16[960,128]{1,0:T(8,128)(2,1)S(1)}, u32[]{:S(2)}, u32[]{:S(2)}) collective-permute-start(bf16[960,128]{1,0:T(8,128)(2,1)S(1)} %collective-permute-done.14.refs_2_), channel_id=1, source_target_pairs={{0,1},{1,0},{2,3},{3,2},{4,5},{5,4},{6,7},{7,6},{8,9},{9,8},{10,11... | collective-permute-start | bytes 737288 | tf_op jit(solution)/shard_map/ppermute | solution.py:330
  (2 other events, 2.1 us)
